TPU v7x, 1024 devices: a whole 4x4x32 slice. The times are simulated.
1024 devices in a mesh: dp: 64 (over z, core), expert: 16 (over y, x).
Axes of the slice: x: 4, y: 4, z: 32, core: 2. Of those that a mesh axis runs over, the one named last changes fastest.
Arguments:
- tokens: bfloat16 [3072, 4096], P('dp', 'expert'), may hold values from -6 to 6
- picks: int32 [3072, 8], P('dp'), may hold values from 0 to 127, all different within a row; in each aligned block of 48 rows (0 to 47, 48 to 95, ...) at most 6 rows name the same one
- gates: float32 [3072, 8], P('dp'), may hold values from 0.05 to 0.5
- w_gate: bfloat16 [64, 4096, 1536], P('dp', 'expert'), may hold values from -0.09375 to 0.09375
- w_up: bfloat16 [64, 4096, 1536], P('dp', 'expert'), may hold values from -0.09375 to 0.09375
- w_down: bfloat16 [64, 1536, 4096], P('dp', None, 'expert'), may hold values from -0.15625 to 0.15625
- cotangent: bfloat16 [3072, 4096], P('dp', 'expert'), may hold values from -6 to 6
Outputs:
- mixed: bfloat16 [3072, 4096], P('dp', 'expert')
- grad_tokens: bfloat16 [3072, 4096], P('dp', 'expert')
- grad_gates: float32 [3072, 8], P('dp')
Inputs may be any that keep to these rules, and one draw needn't show every extreme that they name: Among the 48 tokens of one index of dp, no expert is named by more than 6 picks, a bound that some block reaches; the 8 picks of a token differ.
All inputs are finite; a program needn't handle non-finite values.
Results may differ from a plain program's by a relative error of at most 0.0064.
Values may be sent and summed in bfloat16 or wider, within the bound.
No kernel may reach another device: no remote copies, remote signals or barrier semaphores. Data moves between devices by JAX's collectives and lax.ppermute only.
A program may use at most 64 MiB of HBM per device.

v0:
```python
import jax
import jax.numpy as jnp
from jax import lax
from jax.sharding import PartitionSpec as P

ROUTED = 128
TOP = 8
CAP = 6


def silu_parts(gate_pre):
    logistic = jax.nn.sigmoid(gate_pre)
    return (gate_pre * logistic, logistic * (1.0 + gate_pre * (1.0 - logistic)))


def shards(tokens, picks, gates, w_gate, w_up, w_down, cotangent):
    tok_rows, feat_cols = tokens.shape
    expert_count = lax.axis_size("dp")
    pair_count = tok_rows * TOP
    slot_total = expert_count * CAP
    flat_picks = picks.reshape(pair_count)
    onehot = (flat_picks[:, None] == jnp.arange(ROUTED, dtype=jnp.int32)[None, :]).astype(jnp.int32)
    slot_rank = jnp.sum((jnp.cumsum(onehot, axis=0) - onehot) * onehot, axis=1)
    target = jnp.where(flat_picks < expert_count, flat_picks * CAP + slot_rank, -1)
    select = (target[None, :] == jnp.arange(slot_total, dtype=jnp.int32)[:, None]).astype(
        jnp.bfloat16
    )
    by_token = jnp.sum(select.reshape(slot_total, tok_rows, TOP), axis=2)
    send_tok = jnp.dot(by_token, tokens, preferred_element_type=jnp.float32).astype(jnp.bfloat16)
    send_tok = send_tok.reshape(expert_count, CAP, feat_cols)
    scaled = (gates[:, :, None] * cotangent[:, None, :].astype(jnp.float32)).astype(jnp.bfloat16)
    send_grad = jnp.dot(
        select, scaled.reshape(pair_count, feat_cols), preferred_element_type=jnp.float32
    ).astype(jnp.bfloat16)
    send_grad = send_grad.reshape(expert_count, CAP, feat_cols)
    recv_tok, recv_grad = (
        lax.all_to_all(send_tok, "dp", split_axis=0, concat_axis=0, tiled=True),
        lax.all_to_all(send_grad, "dp", split_axis=0, concat_axis=0, tiled=True),
    )
    recv_tok = recv_tok.reshape(slot_total, feat_cols)
    recv_grad = recv_grad.reshape(slot_total, feat_cols)
    gate_local = w_gate[0]
    up_local = w_up[0]
    down_local = w_down[0]
    inner = (((0,), (1,)), ((), ()))
    gate_cols = gate_local
    up_cols = up_local
    gate_part = lax.dot_general(gate_cols, recv_tok, inner, preferred_element_type=jnp.float32)
    up_part = lax.dot_general(up_cols, recv_tok, inner, preferred_element_type=jnp.float32)
    gate_part, up_part = (gate_part, up_part)
    down_rows = down_local
    summed = lax.psum_scatter(
        jnp.concatenate(
            [
                gate_part,
                up_part,
                lax.dot_general(
                    down_rows,
                    recv_grad,
                    (((1,), (1,)), ((), ())),
                    preferred_element_type=jnp.float32,
                ),
            ],
            axis=1,
        ),
        "expert",
        scatter_dimension=0,
        tiled=True,
    )
    gate_pre = summed[:, :slot_total]
    up_pre = summed[:, slot_total : 2 * slot_total]
    grad_hidden = summed[:, 2 * slot_total :]
    silu_val, silu_slope = silu_parts(gate_pre)
    hidden_act = (silu_val * up_pre).astype(jnp.bfloat16)
    down_rows = down_local
    expert_out = lax.dot_general(
        lax.all_gather(hidden_act, "expert", axis=0, tiled=True),
        down_rows,
        (((0,), (0,)), ((), ())),
        preferred_element_type=jnp.float32,
    )
    grad_gate = (grad_hidden * up_pre * silu_slope).astype(jnp.bfloat16)
    grad_up = (grad_hidden * silu_val).astype(jnp.bfloat16)
    gate_part = lax.all_gather(grad_gate, "expert", axis=0, tiled=True)
    up_part = lax.all_gather(grad_up, "expert", axis=0, tiled=True)
    gate_cols = gate_local
    up_cols = up_local
    running = lax.dot_general(
        gate_part, gate_cols, (((0,), (1,)), ((), ())), preferred_element_type=jnp.float32
    )
    grad_pick = running + lax.dot_general(
        up_part, up_cols, (((0,), (1,)), ((), ())), preferred_element_type=jnp.float32
    )
    out_slots = expert_out.astype(jnp.bfloat16).reshape(expert_count, CAP, feat_cols)
    grad_slots = grad_pick.astype(jnp.bfloat16).reshape(expert_count, CAP, feat_cols)
    back_out, back_grad = (
        lax.all_to_all(out_slots, "dp", split_axis=0, concat_axis=0, tiled=True),
        lax.all_to_all(grad_slots, "dp", split_axis=0, concat_axis=0, tiled=True),
    )
    back_out = back_out.reshape(slot_total, feat_cols)
    back_grad = back_grad.reshape(slot_total, feat_cols)
    pair_out = lax.dot_general(
        select, back_out, (((0,), (0,)), ((), ())), preferred_element_type=jnp.float32
    )
    pair_dx = lax.dot_general(
        select, back_grad, (((0,), (0,)), ((), ())), preferred_element_type=jnp.float32
    )
    pair_out = pair_out.reshape(tok_rows, TOP, feat_cols)
    pair_dx = pair_dx.reshape(tok_rows, TOP, feat_cols)
    mixed = jnp.sum(gates[:, :, None] * pair_out, axis=1).astype(jnp.bfloat16)
    grad_tokens = jnp.sum(pair_dx, axis=1).astype(jnp.bfloat16)
    local_dots = jnp.sum(cotangent[:, None, :].astype(jnp.float32) * pair_out, axis=2)
    grad_gates = lax.psum(local_dots, "expert")
    return (mixed, grad_tokens, grad_gates)


def solution(mesh):
    placed = (
        P("dp", "expert"),
        P("dp", None),
        P("dp", None),
        P("dp", "expert", None),
        P("dp", "expert", None),
        P("dp", None, "expert"),
        P("dp", "expert"),
    )
    return jax.shard_map(
        shards,
        mesh=mesh,
        in_specs=placed,
        out_specs=(P("dp", "expert"), P("dp", "expert"), P("dp", None)),
        check_vma=False,
    )
```

profile of v0, /device:TPU:32, one launch (start us, length us, event | category | flops | bytes accessed | tf_op | source)
XLA Modules:
  0.0 645.6 jit_solution(2540342506865190936)
XLA Ops:
  7.2 0.8 copy.52
  9.1 0.7 add_select_fusion
  10.1 1.0 convolution_convert_fusion.1
  11.1 0.8 reshape.106
  11.8 29.0 %all-to-all-start = ((bf16[64,6,256]{2,1,0:T(8,128)(2,1)}), bf16[64,6,256]{2,1,0:T(8,128)(2,1)S(1)}, u32[]{:S(2)}, u32[]{:S(2)}) async-start(bf16[64,6,256]{2,1,0:T(8,128)(2,1)} %reshape.106), calls=%async_computation | async-start | bytes 524288 | tf_op jit(solution)/shard_map/all_to_all | solution.py:37
  41.4 0.8 reshape.108
  42.2 40.9 %all-to-all-done = bf16[64,6,256]{2,1,0:T(8,128)(2,1)S(1)} async-done(((bf16[64,6,256]{2,1,0:T(8,128)(2,1)}), bf16[64,6,256]{2,1,0:T(8,128)(2,1)S(1)}, u32[]{:S(2)}, u32[]{:S(2)}) %all-to-all-start) | async-done | bytes 196640 | tf_op jit(solution)/shard_map/all_to_all | solution.py:37
  83.2 6.0 all-to-all-start.1
  89.3 1.6 convolution_bitcast_fusion.1
  90.9 1.9 convolution_bitcast_fusion.2
  92.8 38.7 %all-to-all-done.1 = bf16[64,6,256]{2,1,0:T(8,128)(2,1)} async-done(((bf16[64,6,256]{2,1,0:T(8,128)(2,1)}), bf16[64,6,256]{2,1,0:T(8,128)(2,1)}, u32[]{:S(2)}, u32[]{:S(2)}) %all-to-all-start.1) | async-done | bytes 196640 | tf_op jit(solution)/shard_map/all_to_all | solution.py:38
  131.5 1.0 reshape.109
  132.6 1.8 convolution_bitcast_fusion
  134.5 3.3 pad_maximum_fusion
  137.7 8.1 %copy.64 = f32[1536,1152]{1,0:T(8,128)} copy(f32[1536,1152]{0,1:T(8,128)} %pad_maximum_fusion) | data formatting | bytes 14155776
  145.9 100.6 %reduce-scatter.4.cloned.1.call-done = f32[96,1152]{1,0:T(8,128)} async-done(((f32[1536,1152]{1,0:T(8,128)}), f32[96,1152]{1,0:T(8,128)}) %reduce-scatter.4.cloned.1.call-update) | async-done | bytes 442384 | tf_op jit(solution)/shard_map/reduce_scatter | solution.py:52
  246.5 1.8 multiply_convert_fusion
  248.4 0.7 all-gather.8.cloned.1.call-update
  249.6 80.3 %all-gather.6.cloned.1.call-done = bf16[1536,384]{1,0:T(8,128)(2,1)} async-done(((bf16[96,384]{1,0:T(8,128)(2,1)}), bf16[1536,384]{1,0:T(8,128)(2,1)}) %all-gather.6.cloned.1.call-update) | async-done | bytes 1179664 | tf_op jit(solution)/shard_map/all_gather | solution.py:84
  330.0 1.8 fusion.5
  331.8 81.7 %all-gather.8.cloned.1.call-done = bf16[1536,384]{1,0:T(8,128)(2,1)} async-done(((bf16[96,384]{1,0:T(8,128)(2,1)}), bf16[1536,384]{1,0:T(8,128)(2,1)}) %all-gather.8.cloned.1.call-update) | async-done | bytes 1179664 | tf_op jit(solution)/shard_map/all_gather | solution.py:85
  413.5 1.8 fusion
  415.3 0.8 reshape.112
  416.0 23.6 %all-to-all-start.3 = ((bf16[64,6,256]{2,1,0:T(8,128)(2,1)}), bf16[64,6,256]{2,1,0:T(8,128)(2,1)S(1)}, u32[]{:S(2)}, u32[]{:S(2)}) async-start(bf16[64,6,256]{2,1,0:T(8,128)(2,1)} %reshape.112), calls=%async_computation.3 | async-start | bytes 524288 | tf_op jit(solution)/shard_map/all_to_all | solution.py:98
  439.6 57.2 %all-gather.4.cloned.1.call-done = bf16[1536,384]{1,0:T(8,128)(2,1)} async-done(((bf16[96,384]{1,0:T(8,128)(2,1)}), bf16[1536,384]{1,0:T(8,128)(2,1)}) %all-gather.4.cloned.1.call-update) | async-done | bytes 1179664 | tf_op jit(solution)/shard_map/all_gather | solution.py:77
  496.8 1.8 convolution_convert_fusion
  498.6 0.8 reshape.110
  499.4 23.6 %all-to-all-start.2 = ((bf16[64,6,256]{2,1,0:T(8,128)(2,1)}), bf16[64,6,256]{2,1,0:T(8,128)(2,1)S(1)}, u32[]{:S(2)}, u32[]{:S(2)}) async-start(bf16[64,6,256]{2,1,0:T(8,128)(2,1)} %reshape.110), calls=%async_computation.2 | async-start | bytes 524288 | tf_op jit(solution)/shard_map/all_to_all | solution.py:97
  523.0 0.9 convolution_reduce_fusion
  524.0 41.3 %all-to-all-done.2 = bf16[64,6,256]{2,1,0:T(8,128)(2,1)S(1)} async-done(((bf16[64,6,256]{2,1,0:T(8,128)(2,1)}), bf16[64,6,256]{2,1,0:T(8,128)(2,1)S(1)}, u32[]{:S(2)}, u32[]{:S(2)}) %all-to-all-start.2) | async-done | bytes 196640 | tf_op jit(solution)/shard_map/all_to_all | solution.py:97
  565.3 1.0 multiply_reduce_fusion
  566.3 72.1 %psum.7 = f32[48,8]{1,0:T(8,128)S(1)} all-reduce(f32[48,8]{1,0:T(8,128)S(1)} %get-tuple-element.12), channel_id=1, replica_groups=mesh['dp'=64,'expert'=16] {'expert'}, use_global_device_ids=true, to_apply=%region_8.9 | all-reduce | flops 384 | bytes 3072 | tf_op jit(solution)/shard_map/psum | solution.py:113
  (42 shorter events, 3.6 us)
Async XLA Ops:
  7.2 83.8 %copy-start = (bf16[1,256,1536]{2,1,0:T(8,128)(2,1)S(1)}, bf16[1,256,1536]{2,1,0:T(8,128)(2,1)}, u32[]{:S(2)}) copy-start(bf16[1,256,1536]{2,1,0:T(8,128)(2,1)} %param.10) | copy-start | bytes 2359300
  7.2 33.7 %copy-start.5 = (f32[48,8]{0,1:T(8,128)S(1)}, f32[48,8]{0,1:T(8,128)}, u32[]{:S(2)}) copy-start(f32[48,8]{0,1:T(8,128)} %param.9) | copy-start | bytes 4612
  7.2 33.8 %copy-start.4 = (bf16[48,256]{1,0:T(8,128)(2,1)S(1)}, bf16[48,256]{1,0:T(8,128)(2,1)}, u32[]{:S(2)}) copy-start(bf16[48,256]{1,0:T(8,128)(2,1)} %param.13) | copy-start | bytes 73732
  11.8 71.3 %all-to-all-start = ((bf16[64,6,256]{2,1,0:T(8,128)(2,1)}), bf16[64,6,256]{2,1,0:T(8,128)(2,1)S(1)}, u32[]{:S(2)}, u32[]{:S(2)}) async-start(bf16[64,6,256]{2,1,0:T(8,128)(2,1)} %reshape.106), calls=%async_computation | async-start | bytes 524288 | tf_op jit(solution)/shard_map/all_to_all | solution.py:37
  83.2 48.4 %all-to-all-start.1 = ((bf16[64,6,256]{2,1,0:T(8,128)(2,1)}), bf16[64,6,256]{2,1,0:T(8,128)(2,1)}, u32[]{:S(2)}, u32[]{:S(2)}) async-start(bf16[64,6,256]{2,1,0:T(8,128)(2,1)} %reshape.108), calls=%async_computation.1 | async-start | bytes 524288 | tf_op jit(solution)/shard_map/all_to_all | solution.py:38
  89.2 157.3 %reduce-scatter.4.cloned.1.call-start = ((), (), s32[]{:S(2)}) async-start(), calls=%async_computation.8 | async-start | bytes 7520256 | tf_op jit(solution)/shard_map/reduce_scatter | solution.py:52
  132.6 1.9 copy-start.1
  145.8 267.7 %copy-start.2 = (bf16[1,256,1536]{2,1,0:T(8,128)(2,1)S(1)}, bf16[1,256,1536]{2,1,0:T(8,128)(2,1)}, u32[]{:S(2)}) copy-start(bf16[1,256,1536]{2,1,0:T(8,128)(2,1)} %param.11) | copy-start | bytes 2359300
  145.8 184.1 %all-gather.6.cloned.1.call-start = ((), (), s32[]{:S(2)}) async-start(), calls=%async_computation.6 | async-start | bytes 1253376 | tf_op jit(solution)/shard_map/all_gather | solution.py:84
  248.3 165.2 %all-gather.8.cloned.1.call-start = ((), (), s32[]{:S(2)}) async-start(), calls=%async_computation.7 | async-start | bytes 1253376 | tf_op jit(solution)/shard_map/all_gather | solution.py:85
  249.0 247.8 %all-gather.4.cloned.1.call-start = ((), (), s32[]{:S(2)}) async-start(), calls=%async_computation.5 | async-start | bytes 1253376 | tf_op jit(solution)/shard_map/all_gather | solution.py:77
  249.6 247.2 %copy-start.3 = (bf16[1,1536,256]{2,1,0:T(8,128)(2,1)S(1)}, bf16[1,1536,256]{2,1,0:T(8,128)(2,1)}, u32[]{:S(2)}) copy-start(bf16[1,1536,256]{2,1,0:T(8,128)(2,1)} %param.12) | copy-start | bytes 2359300
  416.0 83.3 %all-to-all-start.3 = ((bf16[64,6,256]{2,1,0:T(8,128)(2,1)}), bf16[64,6,256]{2,1,0:T(8,128)(2,1)S(1)}, u32[]{:S(2)}, u32[]{:S(2)}) async-start(bf16[64,6,256]{2,1,0:T(8,128)(2,1)} %reshape.112), calls=%async_computation.3 | async-start | bytes 524288 | tf_op jit(solution)/shard_map/all_to_all | solution.py:98
  499.4 65.9 %all-to-all-start.2 = ((bf16[64,6,256]{2,1,0:T(8,128)(2,1)}), bf16[64,6,256]{2,1,0:T(8,128)(2,1)S(1)}, u32[]{:S(2)}, u32[]{:S(2)}) async-start(bf16[64,6,256]{2,1,0:T(8,128)(2,1)} %reshape.110), calls=%async_computation.2 | async-start | bytes 524288 | tf_op jit(solution)/shard_map/all_to_all | solution.py:97
Sparse Core Ops, SparseCore 0:
  145.9 100.5 reduce-scatter.3
  251.4 78.5 all-gather.5
  334.9 78.5 all-gather.7
  418.2 78.5 all-gather.3
where the time goes:
time: 646 us
  waiting for transfers between devices  442 us (68%)
  starting transfers between devices  82.3 us (13%)
  blocking collectives  72.1 us (11%)
  local copies, waits for them, and re-layouts  14.7 us (2%)
  between operations  14 us (2%)
  matrix products  13.9 us (2%)
  other arithmetic  6.55 us (1%)
    reduce_scatter x1, waiting for transfers between devices, shards(): lax.psum_scatter(jnp.concatenate([gate_part, up_part, lax.dot_general(dow...  101 us
    all_gather x1, waiting for transfers between devices, shards(): up_part = lax.all_gather(grad_up, 'expert', axis=0, tiled=True)  81.7 us
    all_gather x1, waiting for transfers between devices, shards(): gate_part = lax.all_gather(grad_gate, 'expert', axis=0, tiled=True)  80.3 us
    psum x1, blocking collectives, shards(): grad_gates = lax.psum(local_dots, 'expert')  72.1 us
    all_gather x1, waiting for transfers between devices, shards(): lax.all_gather(hidden_act, 'expert', axis=0, tiled=True)  57.2 us
    all_to_all x1, waiting for transfers between devices, shards(): lax.all_to_all(out_slots, 'dp', split_axis=0, concat_axis=0, tiled=True)  41.3 us
    all_to_all x1, waiting for transfers between devices, shards(): lax.all_to_all(send_tok, 'dp', split_axis=0, concat_axis=0, tiled=True)  40.9 us
    all_to_all x1, waiting for transfers between devices, shards(): lax.all_to_all(send_grad, 'dp', split_axis=0, concat_axis=0, tiled=True)  38.7 us
  transfers between devices with their start and end apart: 8, of which 7 were waited for; matrix products, arithmetic and copies ran while one was open for 2% of the time, Pallas kernels for 0%

commit v1 on v0

v1 whole, which is shorter than its diff:
```python
import jax
import jax.numpy as jnp
from jax import lax
from jax.sharding import PartitionSpec as P

CAP = 6
LANES = 128
F32 = jnp.float32
BF16 = jnp.bfloat16


def split3(v):
    hi = v.astype(BF16).astype(F32)
    mid = (v - hi).astype(BF16).astype(F32)
    return hi, mid, v - hi - mid


def routing(picks, gates, experts):
    ids = jnp.arange(experts, dtype=jnp.int32)
    names = picks[:, :, None] == ids[None, None, :]
    member = jnp.any(names, axis=1)
    gate_te = jnp.sum(jnp.where(names, gates[:, :, None], 0.0), axis=1)
    rows = picks.shape[0]
    before = jnp.arange(rows)[:, None] > jnp.arange(rows)[None, :]
    rank = jnp.dot(before.astype(BF16), member.astype(BF16), preferred_element_type=F32)
    rank = jnp.where(member, rank, -1.0)
    return names, rank, gate_te


def shards(tokens, picks, gates, w_gate, w_up, w_down, cotangent):
    rows, feats = tokens.shape
    experts = lax.axis_size("dp")
    parts = lax.axis_size("expert")
    halves = feats // LANES
    slots = experts * CAP
    pieces = 2 * halves * CAP
    hidden = w_gate.shape[2]
    w_gate, w_up, w_down = w_gate[0], w_up[0], w_down[0]

    names, rank, gate_te = routing(picks, gates, experts)
    rank_t = rank.T
    gate_t = gate_te.T

    j = jnp.arange(pieces, dtype=jnp.int32)
    j_blk, j_slot = j // CAP, (j % CAP).astype(F32)
    c = jnp.arange(2 * halves * rows, dtype=jnp.int32)
    c_blk = c // rows
    rank_c = jnp.tile(rank_t, (1, 2 * halves))
    same = j_blk[:, None] == c_blk[None, :]
    pick_c = (rank_c[:, None, :] == j_slot[None, :, None]) & same[None]
    source = jnp.concatenate(
        [v[:, h * LANES : (h + 1) * LANES] for v in (tokens, cotangent) for h in range(halves)], axis=0
    )
    packed = jnp.dot(
        pick_c.astype(BF16).reshape(experts * pieces, -1), source, preferred_element_type=F32
    )
    hit = rank_t[:, None, :] == j_slot[None, :, None]
    scale = jnp.sum(jnp.where(hit, gate_t[:, None, :], 0.0), axis=2, keepdims=True)
    scale = jnp.where((j_blk >= halves)[None, :, None], scale, 1.0)
    packed = (packed.reshape(experts, pieces, LANES) * scale).astype(BF16)

    recv = lax.all_to_all(packed, "dp", split_axis=0, concat_axis=0, tiled=True)

    recv = recv.reshape(experts, 2, halves, CAP, LANES).transpose(1, 0, 3, 2, 4)
    recv = recv.reshape(2, slots, feats)
    tok, grad = recv[0], recv[1]
    pre = jnp.concatenate(
        [
            jnp.dot(tok, w_gate, preferred_element_type=F32).astype(BF16),
            jnp.dot(tok, w_up, preferred_element_type=F32).astype(BF16),
            lax.dot_general(grad, w_down, (((1,), (1,)), ((), ())), preferred_element_type=F32).astype(BF16),
        ],
        axis=1,
    )
    own = slots // parts
    pre = lax.all_to_all(
        pre.reshape(parts, own, 3 * hidden), "expert", split_axis=0, concat_axis=0, tiled=True
    )
    pre = jnp.sum(pre.astype(F32), axis=0)
    gate_pre, up_pre, grad_hidden = pre[:, :hidden], pre[:, hidden : 2 * hidden], pre[:, 2 * hidden :]
    logistic = jax.nn.sigmoid(gate_pre)
    silu = gate_pre * logistic
    act = (silu * up_pre).astype(BF16)
    grad_gate = (grad_hidden * up_pre * (logistic * (1.0 + gate_pre * (1.0 - logistic)))).astype(BF16)
    grad_up = (grad_hidden * silu).astype(BF16)
    dots = jnp.sum(act.astype(F32) * grad_hidden, axis=1, keepdims=True)
    dots_hi = dots.astype(BF16)
    dots_lo = (dots - dots_hi.astype(F32)).astype(BF16)
    lane = jnp.arange(LANES)[None, :]
    extra = jnp.where(lane == 0, dots_hi, jnp.where(lane == 1, dots_lo, jnp.zeros((), BF16)))
    every = lax.all_gather(
        jnp.concatenate([act, grad_gate, grad_up, extra], axis=1), "expert", axis=0, tiled=True
    )

    dots = every[:, 3 * hidden].astype(F32) + every[:, 3 * hidden + 1].astype(F32)
    dots = jnp.pad(dots.reshape(slots // LANES, LANES), ((0, 48 - slots // LANES), (0, 0)))
    dots = lax.all_gather(dots, "dp", axis=0, tiled=False)[:, : slots // LANES]

    expert_out = jnp.dot(every[:, :hidden], w_down, preferred_element_type=F32)
    grad_pick = lax.dot_general(
        every[:, hidden : 2 * hidden], w_gate, (((1,), (1,)), ((), ())), preferred_element_type=F32
    ) + lax.dot_general(
        every[:, 2 * hidden : 3 * hidden], w_up, (((1,), (1,)), ((), ())), preferred_element_type=F32
    )
    back = jnp.stack([expert_out.astype(BF16), grad_pick.astype(BF16)])
    back = back.reshape(2, experts, CAP, halves, LANES).transpose(1, 0, 3, 2, 4)
    back = lax.all_to_all(
        back.reshape(experts, pieces, LANES), "dp", split_axis=0, concat_axis=0, tiled=True
    )

    kinds = [g for g in split3(gate_t)] + [jnp.ones_like(gate_t)]
    value = jnp.concatenate([g for g in kinds for _ in range(halves)], axis=1)
    m = jnp.arange(4 * halves * rows, dtype=jnp.int32)
    m_kind, m_half = m // (halves * rows), m // rows % halves
    m_array = (m_kind == 3).astype(jnp.int32)
    meets = j_blk[:, None] == (m_array * halves + m_half)[None, :]
    rank_m = jnp.tile(rank_t, (1, 4 * halves))
    mix = jnp.where((rank_m[:, None, :] == j_slot[None, :, None]) & meets[None], value[:, None, :], 0.0)
    out = lax.dot_general(
        mix.astype(BF16).reshape(experts * pieces, -1),
        back.reshape(experts * pieces, LANES),
        (((0,), (0,)), ((), ())),
        preferred_element_type=F32,
    ).reshape(4, halves, rows, LANES)
    mixed = out[0] + out[1] + out[2]
    mixed = jnp.concatenate([mixed[h] for h in range(halves)], axis=1).astype(BF16)
    grad_tokens = jnp.concatenate([out[3, h] for h in range(halves)], axis=1).astype(BF16)

    me = lax.axis_index("dp")
    dots = lax.dynamic_slice_in_dim(dots.reshape(experts, slots), me * CAP, CAP, axis=1)
    dots_te = sum(jnp.where(rank_t == s, dots[:, s : s + 1], 0.0) for s in range(CAP)).T
    grad_gates = jnp.sum(jnp.where(names, dots_te[:, None, :], 0.0), axis=2) / gates
    return mixed, grad_tokens, grad_gates


def solution(mesh):
    placed = (
        P("dp", "expert"),
        P("dp", None),
        P("dp", None),
        P("dp", "expert", None),
        P("dp", "expert", None),
        P("dp", None, "expert"),
        P("dp", "expert"),
    )
    return jax.shard_map(
        shards,
        mesh=mesh,
        in_specs=placed,
        out_specs=(P("dp", "expert"), P("dp", "expert"), P("dp", None)),
        check_vma=False,
    )
```

time: 646 us -> 390 us (0.60)
  the two profiles are of different devices: /device:TPU:32 before, /device:TPU:1 now
where the time goes in v1:
time: 390 us; the launch traced here: 389 us
  waiting for transfers between devices  236 us (61%)
  blocking collectives  83.6 us (21%)
  starting transfers between devices  31 us (8%)
  between operations  14.4 us (4%)
  other arithmetic  8.95 us (2%)
  matrix products  8.11 us (2%)
  local copies, waits for them, and re-layouts  7.49 us (2%)
    all_gather x1, waiting for transfers between devices, shards(): dots = lax.all_gather(dots, 'dp', axis=0, tiled=False)[:, :slots // LANES]  117 us
    all_to_all x1, blocking collectives, shards(): recv = lax.all_to_all(packed, 'dp', split_axis=0, concat_axis=0, tiled=True)  83.6 us
    all_gather x1, waiting for transfers between devices, shards(): lax.all_gather(jnp.concatenate([act, grad_gate, grad_up, extra], axis=1),...  67.3 us
    all_to_all x1, waiting for transfers between devices, shards(): lax.all_to_all(pre.reshape(parts, own, 3 * hidden), 'expert', split_axis=...  51.7 us
    all_to_all x1, starting transfers between devices, shards(): lax.all_to_all(back.reshape(experts, pieces, LANES), 'dp', split_axis=0,...  24.2 us
  transfers between devices with their start and end apart: 4, of which 3 were waited for; matrix products, arithmetic and copies ran while one was open for 2% of the time, Pallas kernels for 0%

profile of v1, /device:TPU:1, one launch (start us, length us, event | category | flops | bytes accessed | tf_op | source)
XLA Modules:
  0.0 389.2 jit_solution(16972426081734369664)
XLA Ops:
  7.2 0.8 copy.66
  8.1 0.8 copy.68
  9.7 0.8 fusion.67
  10.6 0.5 fusion.6
  11.1 83.6 %all_to_all.15 = bf16[64,24,128]{2,1,0:T(8,128)(2,1)S(1)} all-to-all(bf16[64,24,128]{2,1,0:T(8,128)(2,1)S(1)} %fusion.6), channel_id=1, replica_groups=mesh['dp'=64,'expert'=16] {'dp'}, dimensions={0} | all-to-all | bytes 786432 | tf_op jit(solution)/shard_map/all_to_all | solution.py:62
  94.8 0.2 copy.78
  95.0 0.5 convolution_convert_fusion.1
  95.5 0.5 convolution_convert_fusion.2
  96.0 0.2 copy.79
  96.2 0.5 convolution_convert_fusion
  96.7 1.9 pad_maximum_fusion
  98.7 6.8 %all-to-all-start.1 = ((bf16[16,24,4608]{2,1,0:T(8,128)(2,1)}), bf16[16,24,4608]{2,1,0:T(8,128)(2,1)}, u32[]{:S(2)}, u32[]{:S(2)}) async-start(bf16[16,24,4608]{2,1,0:T(8,128)(2,1)} %bitcast.57), calls=%async_computation.1 | async-start | bytes 7077888 | tf_op jit(solution)/shard_map/all_to_all | solution.py:76
  105.6 51.7 %all-to-all-done.1 = bf16[16,24,4608]{2,1,0:T(8,128)(2,1)} async-done(((bf16[16,24,4608]{2,1,0:T(8,128)(2,1)}), bf16[16,24,4608]{2,1,0:T(8,128)(2,1)}, u32[]{:S(2)}, u32[]{:S(2)}) %all-to-all-start.1) | async-done | bytes 3538976 | tf_op jit(solution)/shard_map/all_to_all | solution.py:76
  157.3 2.5 convert_reduce_fusion
  159.8 0.2 multiply_convert_fusion.1
  160.1 0.7 pad_maximum_fusion.2
  160.9 67.3 %all-gather.4.cloned.1.call-done = bf16[384,4736]{1,0:T(8,128)(2,1)} async-done(((bf16[24,4736]{1,0:T(8,128)(2,1)}), bf16[384,4736]{1,0:T(8,128)(2,1)}) %all-gather.4.cloned.1.call-update) | async-done | bytes 3637264 | tf_op jit(solution)/shard_map/all_gather | solution.py:91
  228.2 1.2 add_reduce_fusion
  229.4 0.6 pad.4
  230.1 1.8 fusion.11
  231.8 1.8 fusion.23
  233.7 1.7 fusion.20
  235.6 1.0 copy.82
  236.6 24.2 %all-to-all-start.2 = ((bf16[64,24,128]{2,1,0:T(8,128)(2,1)}), bf16[64,24,128]{2,1,0:T(8,128)(2,1)S(1)}, u32[]{:S(2)}, u32[]{:S(2)}) async-start(bf16[64,24,128]{2,1,0:T(8,128)(2,1)} %copy.82), calls=%async_computation.2 | async-start | bytes 786432 | tf_op jit(solution)/shard_map/all_to_all | solution.py:107
  261.6 116.6 %all-gather.6.cloned.1.call-done = f32[3072,128]{1,0:T(8,128)} async-done(((f32[48,128]{1,0:T(8,128)}), f32[3072,128]{1,0:T(8,128)}) %all-gather.6.cloned.1.call-update) | async-done | bytes 1572880 | tf_op jit(solution)/shard_map/all_gather | solution.py:97
  378.1 1.0 slice.140
  379.1 0.3 dynamic-slice_reduce_fusion.5
  379.5 0.2 select_reduce_fusion.1
  379.7 0.7 copy.85
  380.3 0.8 fusion.70
  381.1 0.6 pad_maximum_fusion.4
  381.8 0.6 pad_maximum_fusion.3
  (52 shorter events, 2.3 us)
Async XLA Ops:
  7.2 88.4 %copy-start = (bf16[1,256,1536]{2,1,0:T(8,128)(2,1)S(1)}, bf16[1,256,1536]{2,1,0:T(8,128)(2,1)}, u32[]{:S(2)}) copy-start(bf16[1,256,1536]{2,1,0:T(8,128)(2,1)} %param.10) | copy-start | bytes 2359300
  9.5 85.5 %copy-start.1 = (bf16[1,256,1536]{2,1,0:T(8,128)(2,1)S(1)}, bf16[1,256,1536]{2,1,0:T(8,128)(2,1)}, u32[]{:S(2)}) copy-start(bf16[1,256,1536]{2,1,0:T(8,128)(2,1)} %param.11) | copy-start | bytes 2359300
  95.0 1.2 copy-start.2
  98.7 58.6 %all-to-all-start.1 = ((bf16[16,24,4608]{2,1,0:T(8,128)(2,1)}), bf16[16,24,4608]{2,1,0:T(8,128)(2,1)}, u32[]{:S(2)}, u32[]{:S(2)}) async-start(bf16[16,24,4608]{2,1,0:T(8,128)(2,1)} %bitcast.57), calls=%async_computation.1 | async-start | bytes 7077888 | tf_op jit(solution)/shard_map/all_to_all | solution.py:76
  105.5 122.7 %all-gather.4.cloned.1.call-start = ((), (), s32[]{:S(2)}) async-start(), calls=%async_computation.3 | async-start | bytes 3864576 | tf_op jit(solution)/shard_map/all_gather | solution.py:91
  160.8 217.3 %all-gather.6.cloned.1.call-start = ((), (), s32[]{:S(2)}) async-start(), calls=%async_computation.4 | async-start | bytes 1597440 | tf_op jit(solution)/shard_map/all_gather | solution.py:97
  236.6 143.7 %all-to-all-start.2 = ((bf16[64,24,128]{2,1,0:T(8,128)(2,1)}), bf16[64,24,128]{2,1,0:T(8,128)(2,1)S(1)}, u32[]{:S(2)}, u32[]{:S(2)}) async-start(bf16[64,24,128]{2,1,0:T(8,128)(2,1)} %copy.82), calls=%async_computation.2 | async-start | bytes 786432 | tf_op jit(solution)/shard_map/all_to_all | solution.py:107
Sparse Core Ops, SparseCore 0:
  161.0 67.2 all-gather.3
  231.5 146.5 all-gather.5

commit v2 on v1

v2 whole, which is shorter than its diff:
```python
import jax
import jax.numpy as jnp
from jax import lax
from jax.sharding import Mesh, PartitionSpec as P

CAP = 6
LANES = 128
SIDE = 4
F32 = jnp.float32
BF16 = jnp.bfloat16


def split3(v):
    hi = v.astype(BF16).astype(F32)
    mid = (v - hi).astype(BF16).astype(F32)
    return hi, mid, v - hi - mid


def exchange(v, axes):
    return lax.all_to_all(v, axes, split_axis=0, concat_axis=0, tiled=True)


def routing(picks, gates, experts):
    ids = jnp.arange(experts, dtype=jnp.int32)
    names = picks[:, :, None] == ids[None, None, :]
    member = jnp.any(names, axis=1)
    gate_te = jnp.sum(jnp.where(names, gates[:, :, None], 0.0), axis=1)
    rows = picks.shape[0]
    before = jnp.arange(rows)[:, None] > jnp.arange(rows)[None, :]
    rank = jnp.dot(before.astype(BF16), member.astype(BF16), preferred_element_type=F32)
    rank = jnp.where(member, rank, -1.0)
    return names, rank, gate_te


def times(a, b):
    return jnp.dot(a, b, preferred_element_type=F32)


def times_t(a, b):
    return lax.dot_general(a, b, (((1,), (1,)), ((), ())), preferred_element_type=F32)


def shards(tokens, picks, gates, w_gate, w_up, w_down, cotangent):
    rows, feats = tokens.shape
    experts = lax.axis_size("dp")
    halves = feats // LANES
    pieces = 2 * halves * CAP
    hidden = w_gate.shape[2]
    quarter = experts // SIDE
    mine = quarter * CAP
    own = mine // SIDE
    all_gate, all_up, all_down = (lax.all_gather(w[0], "x", axis=0, tiled=False) for w in (w_gate, w_up, w_down))

    names, rank, gate_te = routing(picks, gates, experts)
    rank_t = rank.T
    gate_t = gate_te.T

    j = jnp.arange(pieces, dtype=jnp.int32)
    j_blk, j_slot = j // CAP, (j % CAP).astype(F32)
    c = jnp.arange(2 * halves * rows, dtype=jnp.int32)
    c_blk = c // rows
    rank_c = jnp.tile(rank_t, (1, 2 * halves))
    slot_c = rank_c[:, None, :] == j_slot[None, :, None]
    same = (j_blk[:, None] == c_blk[None, :])[None]
    other = (j_blk[:, None] + halves == c_blk[None, :])[None]
    source = jnp.concatenate(
        [v[:, h * LANES : (h + 1) * LANES] for v in (tokens, cotangent) for h in range(halves)], axis=0
    )

    def select(mask):
        mask = (slot_c & mask).astype(BF16).reshape(experts * pieces, -1)
        return times(mask, source).reshape(experts, pieces, LANES)

    hit = rank_t[:, None, :] == j_slot[None, :, None]
    scale = jnp.sum(jnp.where(hit, gate_t[:, None, :], 0.0), axis=2, keepdims=True)
    scale = jnp.where((j_blk >= halves)[None, :, None], scale, 1.0)
    packed = (select(same) * scale).astype(BF16)

    recv = exchange(packed, "dp")
    recv = exchange(recv.reshape(SIDE, quarter * pieces, LANES), "x")

    q = jnp.arange(quarter * pieces, dtype=jnp.int32)
    q_place = (q % pieces) // CAP * mine + q // pieces * CAP + q % CAP
    order = (q_place[None, :] == q[:, None]).astype(BF16)
    recv = lax.dot_general(order, recv, (((1,), (1,)), ((), ())), preferred_element_type=BF16)
    recv = recv.reshape(2, halves, mine, SIDE, LANES).transpose(0, 2, 3, 1, 4)
    recv = recv.reshape(2, mine, SIDE * feats)
    tok, grad = recv[0], recv[1]
    pre = [times(tok, w.reshape(SIDE * feats, hidden)).astype(BF16) for w in (all_gate, all_up)]
    pre.append(sum(times_t(grad[:, i * feats : (i + 1) * feats], all_down[i]) for i in range(SIDE)).astype(BF16))
    pre = jnp.concatenate(pre, axis=1)

    pre = exchange(pre.reshape(SIDE, own, 3 * hidden), "y")
    pre = jnp.sum(pre.astype(F32), axis=0)
    gate_pre, up_pre, grad_hidden = pre[:, :hidden], pre[:, hidden : 2 * hidden], pre[:, 2 * hidden :]
    logistic = jax.nn.sigmoid(gate_pre)
    silu = gate_pre * logistic
    act = (silu * up_pre).astype(BF16)
    grad_gate = (grad_hidden * up_pre * (logistic * (1.0 + gate_pre * (1.0 - logistic)))).astype(BF16)
    grad_up = (grad_hidden * silu).astype(BF16)
    every = lax.all_gather(jnp.concatenate([act, grad_gate, grad_up], axis=1), "y", axis=0, tiled=True)

    act, grad_gate, grad_up = every[:, :hidden], every[:, hidden : 2 * hidden], every[:, 2 * hidden :]
    expert_out = [times(act, all_down[i]).astype(BF16) for i in range(SIDE)]
    grad_pick = [
        (times_t(grad_gate, all_gate[i]) + times_t(grad_up, all_up[i])).astype(BF16) for i in range(SIDE)
    ]
    back = jnp.concatenate(
        [
            v[i][:, h * LANES : (h + 1) * LANES]
            for v in (expert_out, grad_pick)
            for h in range(halves)
            for i in range(SIDE)
        ],
        axis=0,
    ).reshape(2 * halves, SIDE, mine, LANES).transpose(1, 0, 2, 3).reshape(SIDE, quarter * pieces, LANES)
    back = jnp.stack(
        [
            lax.dot_general(order, back[i], (((0,), (0,)), ((), ())), preferred_element_type=BF16)
            for i in range(SIDE)
        ]
    )
    back = exchange(back, "x")
    back = exchange(back.reshape(experts, pieces, LANES), "dp")

    cot_rows = select(other)
    dots = jnp.sum(cot_rows * back.astype(F32), axis=2)
    dots = jnp.sum(dots.reshape(experts, 2 * halves, CAP)[:, :halves], axis=1)
    dots_te = sum(jnp.where(rank_t == s, dots[:, s : s + 1], 0.0) for s in range(CAP)).T
    local = jnp.sum(jnp.where(names, dots_te[:, None, :], 0.0), axis=2)
    parts = SIDE * SIDE
    local = jnp.broadcast_to(local.reshape(1, -1, LANES), (parts, local.size // LANES, LANES))
    grad_gates = jnp.sum(exchange(local, ("y", "x")), axis=0).reshape(gates.shape)

    kinds = [g for g in split3(gate_t)] + [jnp.ones_like(gate_t)]
    value = jnp.concatenate([g for g in kinds for _ in range(halves)], axis=1)
    m = jnp.arange(4 * halves * rows, dtype=jnp.int32)
    m_kind, m_half = m // (halves * rows), m // rows % halves
    m_array = (m_kind == 3).astype(jnp.int32)
    meets = j_blk[:, None] == (m_array * halves + m_half)[None, :]
    rank_m = jnp.tile(rank_t, (1, 4 * halves))
    mix = jnp.where((rank_m[:, None, :] == j_slot[None, :, None]) & meets[None], value[:, None, :], 0.0)
    out = lax.dot_general(
        mix.astype(BF16).reshape(experts * pieces, -1),
        back.reshape(experts * pieces, LANES),
        (((0,), (0,)), ((), ())),
        preferred_element_type=F32,
    ).reshape(4, halves, rows, LANES)
    mixed = out[0] + out[1] + out[2]
    mixed = jnp.concatenate([mixed[h] for h in range(halves)], axis=1).astype(BF16)
    grad_tokens = jnp.concatenate([out[3, h] for h in range(halves)], axis=1).astype(BF16)
    return mixed, grad_tokens, grad_gates


def solution(mesh):
    wide = Mesh(mesh.devices.reshape(mesh.devices.shape[0], SIDE, SIDE), ("dp", "y", "x"))
    split = ("y", "x")
    placed = (
        P("dp", split),
        P("dp", None),
        P("dp", None),
        P("dp", split, None),
        P("dp", split, None),
        P("dp", None, split),
        P("dp", split),
    )
    return jax.shard_map(
        shards,
        mesh=wide,
        in_specs=placed,
        out_specs=(P("dp", split), P("dp", split), P("dp", None)),
        check_vma=False,
    )
```

time: 390 us -> 348 us (0.89)
  waiting for transfers between devices: 236 us -> 149 us
  blocking collectives: 83.6 us -> 121 us
  matrix products: 8.11 us -> 16.9 us
  other arithmetic: 8.95 us -> 2.66 us
  starting transfers between devices: 31 us -> 36.2 us
    all_gather x2 -> x3, waiting for transfers between devices: 184 us -> 83.7 us  [shards(): lax.all_gather(w[0], 'x', axis=0, tiled=False)]
    all_to_all x1 -> x3, blocking collectives: 83.6 us -> 109 us  [exchange(): return lax.all_to_all(v, axes, split_axis=0, concat_axis=0, tiled=True)]
    all_gather x0 -> x1, blocking collectives: none -> 12 us  [shards(): lax.all_gather(jnp.concatenate([act, grad_gate, grad_up], axis=1), 'y', a...]
    all_to_all x2 -> x3, waiting for transfers between devices: 51.7 us -> 63.5 us  [exchange(): return lax.all_to_all(v, axes, split_axis=0, concat_axis=0, tiled=True)]
    dot_general x7 -> x25, matrix products: 7.22 us -> 16 us  [the longest x8 7.31 us: times(): return jnp.dot(a, b, preferred_element_type=F32)]
    all_to_all x2 -> x3, starting transfers between devices: 31 us -> 36.1 us  [exchange(): return lax.all_to_all(v, axes, split_axis=0, concat_axis=0, tiled=True)]
  transfers between devices with their start and end apart: 4 -> 6, of which waited for: 3 -> 5; matrix products, arithmetic and copies ran while one was open for 2% -> 4% of each run, Pallas kernels for 0% -> 0%
where the time goes in v2:
time: 348 us; the launch traced here: 347 us
  waiting for transfers between devices  149 us (43%)
  blocking collectives  121 us (35%)
  starting transfers between devices  36.2 us (10%)
  matrix products  16.9 us (5%)
  between operations  14.2 us (4%)
  local copies, waits for them, and re-layouts  7.01 us (2%)
    all_to_all x3, blocking collectives, exchange(): return lax.all_to_all(v, axes, split_axis=0, concat_axis=0, tiled=True)  109 us
    all_gather x3, waiting for transfers between devices, shards(): lax.all_gather(w[0], 'x', axis=0, tiled=False)  83.7 us
    all_to_all x3, waiting for transfers between devices, exchange(): return lax.all_to_all(v, axes, split_axis=0, concat_axis=0, tiled=True)  63.5 us
    all_to_all x3, starting transfers between devices, exchange(): return lax.all_to_all(v, axes, split_axis=0, concat_axis=0, tiled=True)  36.1 us
    all_gather x1, blocking collectives, shards(): lax.all_gather(jnp.concatenate([act, grad_gate, grad_up], axis=1), 'y', a...  12 us
    dot_general x8, matrix products, times(): return jnp.dot(a, b, preferred_element_type=F32)  7.31 us
  transfers between devices with their start and end apart: 6, of which 5 were waited for; matrix products, arithmetic and copies ran while one was open for 4% of the time, Pallas kernels for 0%

profile of v2, /device:TPU:1, one launch (start us, length us, event | category | flops | bytes accessed | tf_op | source)
XLA Modules:
  0.0 347.4 jit_solution(938420132428864531)
XLA Ops:
  7.2 0.7 all-gather.6.cloned.1.call-update
  7.9 0.7 all-gather.4.cloned.1.call-update
  8.7 0.7 all-gather.8.cloned.1.call-update
  9.4 0.8 copy.58
  10.2 0.8 copy.60
  11.9 0.8 fusion.88
  12.7 0.5 fusion.5
  13.2 83.7 %all_to_all.30 = bf16[64,24,128]{2,1,0:T(8,128)(2,1)} all-to-all(bf16[64,24,128]{2,1,0:T(8,128)(2,1)S(1)} %fusion.5), channel_id=1, replica_groups=mesh['dp'=64,'y'=4,'x'=4] {'dp'}, dimensions={0} | all-to-all | bytes 786432 | tf_op jit(solution)/shard_map/all_to_all | solution.py:20
  96.9 4.0 %all-to-all-start.1 = ((bf16[4,384,128]{2,1,0:T(8,128)(2,1)}), bf16[4,384,128]{2,1,0:T(8,128)(2,1)S(1)}, u32[]{:S(2)}, u32[]{:S(2)}) async-start(bf16[4,384,128]{2,1,0:T(8,128)(2,1)} %bitcast.5), calls=%async_computation.1 | async-start | bytes 786432 | tf_op jit(solution)/shard_map/all_to_all | solution.py:20
  100.9 6.6 %all-to-all-done.1 = bf16[4,384,128]{2,1,0:T(8,128)(2,1)S(1)} async-done(((bf16[4,384,128]{2,1,0:T(8,128)(2,1)}), bf16[4,384,128]{2,1,0:T(8,128)(2,1)S(1)}, u32[]{:S(2)}, u32[]{:S(2)}) %all-to-all-start.1) | async-done | bytes 393248 | tf_op jit(solution)/shard_map/all_to_all | solution.py:20
  108.8 2.6 convolution_convert_fusion
  111.4 25.6 %all-gather.4.cloned.1.call-done = bf16[4,256,1536]{2,1,0:T(8,128)(2,1)} async-done(((bf16[1,256,1536]{2,1,0:T(8,128)(2,1)}), bf16[4,256,1536]{2,1,0:T(8,128)(2,1)}) %all-gather.4.cloned.1.call-update) | async-done | bytes 3145744 | tf_op jit(solution)/shard_map/all_gather | solution.py:52
  137.0 2.5 convolution_convert_fusion.1
  139.6 58.0 %all-gather.8.cloned.1.call-done = bf16[4,1536,256]{2,1,0:T(8,128)(2,1)} async-done(((bf16[1,1536,256]{2,1,0:T(8,128)(2,1)}), bf16[4,1536,256]{2,1,0:T(8,128)(2,1)}) %all-gather.8.cloned.1.call-update) | async-done | bytes 3145744 | tf_op jit(solution)/shard_map/all_gather | solution.py:52
  197.6 1.6 fusion.28
  199.2 1.5 convolution_add_fusion.2
  201.6 16.2 %all_to_all.31 = bf16[4,24,4608]{2,1,0:T(8,128)(2,1)S(1)} all-to-all(bf16[4,24,4608]{2,1,0:T(8,128)(2,1)S(1)} %bitcast.108), channel_id=1, replica_groups=mesh['dp'=64,'y'=4,'x'=4] {'y'}, dimensions={0} | all-to-all | bytes 1769472 | tf_op jit(solution)/shard_map/all_to_all | solution.py:20
  218.1 12.0 %all_gather.15 = bf16[96,4608]{1,0:T(8,128)(2,1)S(1)} all-gather(bf16[24,4608]{1,0:T(8,128)(2,1)S(1)} %pad_maximum_fusion.2), channel_id=1, replica_groups=mesh['dp'=64,'y'=4,'x'=4] {'y'}, dimensions={0}, use_global_device_ids=true | all-gather | bytes 1105920 | tf_op jit(solution)/shard_map/all_gather | solution.py:101
  231.2 0.7 copy-done.1
  232.3 0.7 copy-done
  233.7 0.4 fusion.15
  237.2 9.3 %all_to_all.32 = bf16[4,384,128]{2,1,0:T(8,128)(2,1)} all-to-all(bf16[4,384,128]{2,1,0:T(8,128)(2,1)S(1)} %pad_maximum_fusion.1), channel_id=1, replica_groups=mesh['dp'=64,'y'=4,'x'=4] {'x'}, dimensions={0} | all-to-all | bytes 786432 | tf_op jit(solution)/shard_map/all_to_all | solution.py:20
  246.5 28.6 %all-to-all-start.4 = ((bf16[64,24,128]{2,1,0:T(8,128)(2,1)}), bf16[64,24,128]{2,1,0:T(8,128)(2,1)S(1)}, u32[]{:S(2)}, u32[]{:S(2)}) async-start(bf16[64,24,128]{2,1,0:T(8,128)(2,1)} %bitcast.34), calls=%async_computation.4 | async-start | bytes 786432 | tf_op jit(solution)/shard_map/all_to_all | solution.py:20
  276.0 52.6 %all-to-all-done.4 = bf16[64,24,128]{2,1,0:T(8,128)(2,1)S(1)} async-done(((bf16[64,24,128]{2,1,0:T(8,128)(2,1)}), bf16[64,24,128]{2,1,0:T(8,128)(2,1)S(1)}, u32[]{:S(2)}, u32[]{:S(2)}) %all-to-all-start.4) | async-done | bytes 393248 | tf_op jit(solution)/shard_map/all_to_all | solution.py:20
  328.6 0.6 fusion.6
  329.6 0.6 broadcast_in_dim.169
  330.2 3.5 %all-to-all-start.5 = ((f32[16,3,128]{2,1,0:T(4,128)}), f32[16,3,128]{2,1,0:T(4,128)S(1)}, u32[]{:S(2)}, u32[]{:S(2)}) async-start(f32[16,3,128]{2,1,0:T(4,128)} %broadcast_in_dim.169), calls=%async_computation.5 | async-start | bytes 65536 | tf_op jit(solution)/shard_map/all_to_all | solution.py:20
  333.7 0.8 fusion.90
  334.5 0.6 pad_maximum_fusion.4
  335.1 0.6 pad_maximum_fusion.3
  335.7 4.4 %all-to-all-done.5 = f32[16,3,128]{2,1,0:T(4,128)S(1)} async-done(((f32[16,3,128]{2,1,0:T(4,128)}), f32[16,3,128]{2,1,0:T(4,128)S(1)}, u32[]{:S(2)}, u32[]{:S(2)}) %all-to-all-start.5) | async-done | bytes 24608 | tf_op jit(solution)/shard_map/all_to_all | solution.py:20
  340.2 0.7 copy.73
  (91 shorter events, 10.0 us)
Async XLA Ops:
  7.2 101.6 %all-gather.6.cloned.1.call-start = ((), (), s32[]{:S(2)}) async-start(), calls=%async_computation.7 | async-start | bytes 3932160 | tf_op jit(solution)/shard_map/all_gather | solution.py:52
  7.9 129.1 %all-gather.4.cloned.1.call-start = ((), (), s32[]{:S(2)}) async-start(), calls=%async_computation.6 | async-start | bytes 3932160 | tf_op jit(solution)/shard_map/all_gather | solution.py:52
  8.6 188.9 %all-gather.8.cloned.1.call-start = ((), (), s32[]{:S(2)}) async-start(), calls=%async_computation.8 | async-start | bytes 3932160 | tf_op jit(solution)/shard_map/all_gather | solution.py:52
  96.9 10.6 %all-to-all-start.1 = ((bf16[4,384,128]{2,1,0:T(8,128)(2,1)}), bf16[4,384,128]{2,1,0:T(8,128)(2,1)S(1)}, u32[]{:S(2)}, u32[]{:S(2)}) async-start(bf16[4,384,128]{2,1,0:T(8,128)(2,1)} %bitcast.5), calls=%async_computation.1 | async-start | bytes 786432 | tf_op jit(solution)/shard_map/all_to_all | solution.py:20
  197.6 3.2 copy-start.2
  230.0 1.9 copy-start.1
  230.3 2.6 copy-start
  246.5 82.0 %all-to-all-start.4 = ((bf16[64,24,128]{2,1,0:T(8,128)(2,1)}), bf16[64,24,128]{2,1,0:T(8,128)(2,1)S(1)}, u32[]{:S(2)}, u32[]{:S(2)}) async-start(bf16[64,24,128]{2,1,0:T(8,128)(2,1)} %bitcast.34), calls=%async_computation.4 | async-start | bytes 786432 | tf_op jit(solution)/shard_map/all_to_all | solution.py:20
  330.2 9.9 %all-to-all-start.5 = ((f32[16,3,128]{2,1,0:T(4,128)}), f32[16,3,128]{2,1,0:T(4,128)S(1)}, u32[]{:S(2)}, u32[]{:S(2)}) async-start(f32[16,3,128]{2,1,0:T(4,128)} %broadcast_in_dim.169), calls=%async_computation.5 | async-start | bytes 65536 | tf_op jit(solution)/shard_map/all_to_all | solution.py:20
Sparse Core Ops, SparseCore 0:
  10.7 65.7 all-gather.5
  79.2 57.8 all-gather.3
  139.7 57.8 all-gather.7

commit v3 on v2

--- a/solution.py
+++ b/solution.py
@@ -18,6 +18,10 @@
 
 def exchange(v, axes):
     return lax.all_to_all(v, axes, split_axis=0, concat_axis=0, tiled=True)
+
+
+def take(v, i):
+    return lax.dynamic_index_in_dim(v, i % SIDE, axis=0, keepdims=False)
 
 
 def routing(picks, gates, experts):
@@ -47,9 +51,9 @@
     pieces = 2 * halves * CAP
     hidden = w_gate.shape[2]
     quarter = experts // SIDE
-    mine = quarter * CAP
-    own = mine // SIDE
-    all_gate, all_up, all_down = (lax.all_gather(w[0], "x", axis=0, tiled=False) for w in (w_gate, w_up, w_down))
+    slots = experts * CAP
+    block = quarter * CAP
+    share = hidden // SIDE
 
     names, rank, gate_te = routing(picks, gates, experts)
     rank_t = rank.T
@@ -77,22 +81,38 @@
     packed = (select(same) * scale).astype(BF16)
 
     recv = exchange(packed, "dp")
-    recv = exchange(recv.reshape(SIDE, quarter * pieces, LANES), "x")
+
+    weights = jnp.concatenate([w_gate[0], w_up[0], w_down[0].T], axis=0)
+    weights = jnp.stack([weights[:, i * share : (i + 1) * share] for i in range(SIDE)])
+    me = lax.axis_index("x")
+    weights = jnp.stack(
+        [
+            lax.ppermute(take(weights, me + i), "x", [(d, (d + i) % SIDE) for d in range(SIDE)])
+            if i
+            else take(weights, me)
+            for i in range(SIDE)
+        ]
+    ).reshape(SIDE, 3, feats, share)
 
     q = jnp.arange(quarter * pieces, dtype=jnp.int32)
-    q_place = (q % pieces) // CAP * mine + q // pieces * CAP + q % CAP
+    q_place = (q % pieces) // CAP * block + q // pieces * CAP + q % CAP
     order = (q_place[None, :] == q[:, None]).astype(BF16)
-    recv = lax.dot_general(order, recv, (((1,), (1,)), ((), ())), preferred_element_type=BF16)
-    recv = recv.reshape(2, halves, mine, SIDE, LANES).transpose(0, 2, 3, 1, 4)
-    recv = recv.reshape(2, mine, SIDE * feats)
-    tok, grad = recv[0], recv[1]
-    pre = [times(tok, w.reshape(SIDE * feats, hidden)).astype(BF16) for w in (all_gate, all_up)]
-    pre.append(sum(times_t(grad[:, i * feats : (i + 1) * feats], all_down[i]) for i in range(SIDE)).astype(BF16))
+    recv = recv.reshape(SIDE, quarter * pieces, LANES)
+    recv = jnp.stack([jnp.dot(order, recv[i], preferred_element_type=BF16) for i in range(SIDE)])
+    recv = recv.reshape(SIDE, 2 * halves, block, LANES)
+    recv = jnp.concatenate([recv[:, i].reshape(slots, LANES) for i in range(2 * halves)], axis=1)
+    recv, weights = lax.optimization_barrier((recv, weights))
+    recv = exchange(jnp.broadcast_to(recv[None], (SIDE, slots, 2 * feats)), "x")
+    recv = [take(recv, me + SIDE - i) for i in range(SIDE)]
+    tok = jnp.concatenate([v[:, :feats] for v in recv], axis=1)
+    grad = jnp.concatenate([v[:, feats:] for v in recv], axis=1)
+    held = [weights[:, i].reshape(SIDE * feats, share) for i in range(3)]
+    pre = [times(v, w).astype(BF16) for v, w in zip((tok, tok, grad), held)]
     pre = jnp.concatenate(pre, axis=1)
 
-    pre = exchange(pre.reshape(SIDE, own, 3 * hidden), "y")
+    pre = exchange(pre.reshape(SIDE, slots // SIDE, 3 * share), "y")
     pre = jnp.sum(pre.astype(F32), axis=0)
-    gate_pre, up_pre, grad_hidden = pre[:, :hidden], pre[:, hidden : 2 * hidden], pre[:, 2 * hidden :]
+    gate_pre, up_pre, grad_hidden = pre[:, :share], pre[:, share : 2 * share], pre[:, 2 * share :]
     logistic = jax.nn.sigmoid(gate_pre)
     silu = gate_pre * logistic
     act = (silu * up_pre).astype(BF16)
@@ -100,27 +120,26 @@
     grad_up = (grad_hidden * silu).astype(BF16)
     every = lax.all_gather(jnp.concatenate([act, grad_gate, grad_up], axis=1), "y", axis=0, tiled=True)
 
-    act, grad_gate, grad_up = every[:, :hidden], every[:, hidden : 2 * hidden], every[:, 2 * hidden :]
-    expert_out = [times(act, all_down[i]).astype(BF16) for i in range(SIDE)]
-    grad_pick = [
-        (times_t(grad_gate, all_gate[i]) + times_t(grad_up, all_up[i])).astype(BF16) for i in range(SIDE)
-    ]
-    back = jnp.concatenate(
+    act, grad_gate, grad_up = (every[:, i * share : (i + 1) * share] for i in range(3))
+    expert_out = times_t(act, held[2]).astype(BF16)
+    grad_pick = (times_t(grad_gate, held[0]) + times_t(grad_up, held[1])).astype(BF16)
+    back = jnp.stack(
         [
-            v[i][:, h * LANES : (h + 1) * LANES]
-            for v in (expert_out, grad_pick)
-            for h in range(halves)
+            jnp.concatenate([v[:, i * feats : (i + 1) * feats] for v in (expert_out, grad_pick)], axis=1)
             for i in range(SIDE)
-        ],
-        axis=0,
-    ).reshape(2 * halves, SIDE, mine, LANES).transpose(1, 0, 2, 3).reshape(SIDE, quarter * pieces, LANES)
+        ]
+    )
+    back = jnp.stack([take(back, me + SIDE - i) for i in range(SIDE)])
+    back = jnp.sum(exchange(back, "x").astype(F32), axis=0).astype(BF16)
+    back = jnp.stack(
+        [back[:, i * LANES : (i + 1) * LANES].reshape(SIDE, block, LANES) for i in range(2 * halves)], axis=1
+    ).reshape(SIDE, quarter * pieces, LANES)
     back = jnp.stack(
         [
             lax.dot_general(order, back[i], (((0,), (0,)), ((), ())), preferred_element_type=BF16)
             for i in range(SIDE)
         ]
     )
-    back = exchange(back, "x")
     back = exchange(back.reshape(experts, pieces, LANES), "dp")
 
     cot_rows = select(other)

time: 348 us -> 256 us (0.74)
  blocking collectives: 121 us -> 44.9 us
  waiting for transfers between devices: 149 us -> 118 us
  starting transfers between devices: 36.2 us -> 61.8 us
  between operations: 14.2 us -> 1.58 us
  matrix products: 16.9 us -> 8.98 us
  local copies, waits for them, and re-layouts: 7.01 us -> 13.7 us
    all_gather x3 -> x0, waiting for transfers between devices: 83.7 us -> none  [shards(): lax.all_gather(w[0], 'x', axis=0, tiled=False)]
    all_to_all x3 -> x2, blocking collectives: 109 us -> 33.3 us  [exchange(): return lax.all_to_all(v, axes, split_axis=0, concat_axis=0, tiled=True)]
    all_to_all x3 -> x4, waiting for transfers between devices: 63.5 us -> 91.9 us  [exchange(): return lax.all_to_all(v, axes, split_axis=0, concat_axis=0, tiled=True)]
    ppermute x0 -> x3, waiting for transfers between devices: none -> 26.3 us  [shards(): lax.ppermute(take(weights, me + i), 'x', [(d, (d + i) % SIDE) for d in ra...]
    all_to_all x3 -> x4, starting transfers between devices: 36.1 us -> 52.5 us  [exchange(): return lax.all_to_all(v, axes, split_axis=0, concat_axis=0, tiled=True)]
    ppermute x0 -> x3, starting transfers between devices: none -> 9.33 us  [shards(): lax.ppermute(take(weights, me + i), 'x', [(d, (d + i) % SIDE) for d in ra...]
    dot_general x12 -> x3, matrix products: 6.86 us -> 1.8 us  [times_t(): lax.dot_general(a, b, (((1,), (1,)), ((), ())), preferred_element_type=F32)]
    dot_general x8 -> x5, matrix products: 7.31 us -> 3.71 us  [times(): return jnp.dot(a, b, preferred_element_type=F32)]
  transfers between devices with their start and end apart: 6 -> 7, of which waited for: 5 -> 7; matrix products, arithmetic and copies ran while one was open for 4% -> 2% of each run, Pallas kernels for 0% -> 0%
where the time goes in v3:
time: 256 us; the launch traced here: 255 us
  waiting for transfers between devices  118 us (46%)
  starting transfers between devices  61.8 us (24%)
  blocking collectives  44.9 us (18%)
  local copies, waits for them, and re-layouts  13.7 us (5%)
  matrix products  8.98 us (4%)
  other arithmetic  6.03 us (2%)
    all_to_all x4, waiting for transfers between devices, exchange(): return lax.all_to_all(v, axes, split_axis=0, concat_axis=0, tiled=True)  91.9 us
    all_to_all x4, starting transfers between devices, exchange(): return lax.all_to_all(v, axes, split_axis=0, concat_axis=0, tiled=True)  52.5 us
    all_to_all x2, blocking collectives, exchange(): return lax.all_to_all(v, axes, split_axis=0, concat_axis=0, tiled=True)  33.3 us
    ppermute x3, waiting for transfers between devices, shards(): lax.ppermute(take(weights, me + i), 'x', [(d, (d + i) % SIDE) for d in ra...  26.3 us
    all_gather x1, blocking collectives, shards(): lax.all_gather(jnp.concatenate([act, grad_gate, grad_up], axis=1), 'y', a...  11.7 us
    ppermute x3, starting transfers between devices, shards(): lax.ppermute(take(weights, me + i), 'x', [(d, (d + i) % SIDE) for d in ra...  9.33 us
    unnamed x52, local copies, waits for them, and re-layouts  5.19 us
  transfers between devices with their start and end apart: 7, of which 7 were waited for; matrix products, arithmetic and copies ran while one was open for 2% of the time, Pallas kernels for 0%

profile of v3, /device:TPU:1, one launch (start us, length us, event | category | flops | bytes accessed | tf_op | source)
XLA Modules:
  0.0 255.2 jit_solution(3666729341886299394)
XLA Ops:
  0.7 0.8 copy.64
  1.9 0.8 copy.66
  3.8 0.8 fusion.93
  4.6 0.7 broadcast_compare_fusion.1
  5.3 1.3 fusion.4
  6.5 30.5 %all-to-all-start = ((bf16[64,24,128]{2,1,0:T(8,128)(2,1)}), bf16[64,24,128]{2,1,0:T(8,128)(2,1)S(1)}, u32[]{:S(2)}, u32[]{:S(2)}) async-start(bf16[64,24,128]{2,1,0:T(8,128)(2,1)} %fusion.4), calls=%async_computation | async-start | bytes 786432 | tf_op jit(solution)/shard_map/all_to_all | solution.py:20
  38.6 4.4 %collective-permute-start.2 = (bf16[768,384]{1,0:T(8,128)(2,1)S(1)}, bf16[768,384]{1,0:T(8,128)(2,1)S(1)}, u32[]{:S(2)}, u32[]{:S(2)}) collective-permute-start(bf16[768,384]{1,0:T(8,128)(2,1)S(1)} %get-tuple-element.26), channel_id=1, source_target_pairs={{0,3},{1,0},{2,1},{3,2},{4,7},{5,4},{6,5},{7,6},{8,11},{9,8},{10,9... | collective-permute-start | bytes 1769480 | tf_op jit(solution)/shard_map/ppermute | solution.py:90
  42.9 2.4 collective-permute-start.1
  45.4 2.5 collective-permute-start
  47.9 8.0 %collective-permute-done.2 = bf16[768,384]{1,0:T(8,128)(2,1)S(1)} collective-permute-done((bf16[768,384]{1,0:T(8,128)(2,1)S(1)}, bf16[768,384]{1,0:T(8,128)(2,1)S(1)}, u32[]{:S(2)}, u32[]{:S(2)}) %collective-permute-start.2) | collective-permute-done | bytes 589856 | tf_op jit(solution)/shard_map/ppermute | solution.py:90
  55.9 4.6 %collective-permute-done.1 = bf16[768,384]{1,0:T(8,128)(2,1)S(1)} collective-permute-done((bf16[768,384]{1,0:T(8,128)(2,1)S(1)}, bf16[768,384]{1,0:T(8,128)(2,1)S(1)}, u32[]{:S(2)}, u32[]{:S(2)}) %collective-permute-start.1) | collective-permute-done | bytes 589856 | tf_op jit(solution)/shard_map/ppermute | solution.py:90
  60.5 13.7 %collective-permute-done = bf16[768,384]{1,0:T(8,128)(2,1)S(1)} collective-permute-done((bf16[768,384]{1,0:T(8,128)(2,1)S(1)}, bf16[768,384]{1,0:T(8,128)(2,1)S(1)}, u32[]{:S(2)}, u32[]{:S(2)}) %collective-permute-start) | collective-permute-done | bytes 589856 | tf_op jit(solution)/shard_map/ppermute | solution.py:90
  74.6 15.8 %all-to-all-done = bf16[64,24,128]{2,1,0:T(8,128)(2,1)S(1)} async-done(((bf16[64,24,128]{2,1,0:T(8,128)(2,1)}), bf16[64,24,128]{2,1,0:T(8,128)(2,1)S(1)}, u32[]{:S(2)}, u32[]{:S(2)}) %all-to-all-start) | async-done | bytes 393248 | tf_op jit(solution)/shard_map/all_to_all | solution.py:20
  91.8 1.3 broadcast_in_dim.161
  93.1 4.4 %all-to-all-start.1 = ((bf16[4,384,512]{2,1,0:T(8,128)(2,1)}), bf16[4,384,512]{2,1,0:T(8,128)(2,1)}, u32[]{:S(2)}, u32[]{:S(2)}) async-start(bf16[4,384,512]{2,1,0:T(8,128)(2,1)} %broadcast_in_dim.161), calls=%async_computation.1 | async-start | bytes 3145728 | tf_op jit(solution)/shard_map/all_to_all | solution.py:20
  97.4 1.5 fusion.81
  98.9 18.4 %all-to-all-done.1 = bf16[4,384,512]{2,1,0:T(8,128)(2,1)} async-done(((bf16[4,384,512]{2,1,0:T(8,128)(2,1)}), bf16[4,384,512]{2,1,0:T(8,128)(2,1)}, u32[]{:S(2)}, u32[]{:S(2)}) %all-to-all-start.1) | async-done | bytes 1572896 | tf_op jit(solution)/shard_map/all_to_all | solution.py:20
  117.3 1.5 dynamic-slice_bitcast_fusion.6
  118.9 1.0 copy-done
  119.9 0.6 convolution_convert_fusion.2
  121.7 0.6 convolution_convert_fusion.1
  122.4 0.9 copy.76
  123.3 15.2 %all_to_all.30 = bf16[4,96,1152]{2,1,0:T(8,128)(2,1)S(1)} all-to-all(bf16[4,96,1152]{2,1,0:T(8,128)(2,1)S(1)} %bitcast.130), channel_id=1, replica_groups=mesh['dp'=64,'y'=4,'x'=4] {'y'}, dimensions={0} | all-to-all | bytes 1769472 | tf_op jit(solution)/shard_map/all_to_all | solution.py:20
  138.8 11.7 %all_gather.3 = bf16[384,1152]{1,0:T(8,128)(2,1)S(1)} all-gather(bf16[96,1152]{1,0:T(8,128)(2,1)S(1)} %pad_maximum_fusion.11), channel_id=1, replica_groups=mesh['dp'=64,'y'=4,'x'=4] {'y'}, dimensions={0}, use_global_device_ids=true | all-gather | bytes 1105920 | tf_op jit(solution)/shard_map/all_gather | solution.py:121
  153.6 18.0 %all_to_all.31 = bf16[4,384,512]{2,1,0:T(8,128)(2,1)S(1)} all-to-all(bf16[4,384,512]{2,1,0:T(8,128)(2,1)S(1)} %pad_maximum_fusion.4), channel_id=1, replica_groups=mesh['dp'=64,'y'=4,'x'=4] {'x'}, dimensions={0} | all-to-all | bytes 3145728 | tf_op jit(solution)/shard_map/all_to_all | solution.py:20
  173.7 0.8 pad_maximum_fusion.10
  174.5 14.1 %all-to-all-start.4 = ((bf16[64,24,128]{2,1,0:T(8,128)(2,1)}), bf16[64,24,128]{2,1,0:T(8,128)(2,1)S(1)}, u32[]{:S(2)}, u32[]{:S(2)}) async-start(bf16[64,24,128]{2,1,0:T(8,128)(2,1)} %bitcast.59), calls=%async_computation.4 | async-start | bytes 786432 | tf_op jit(solution)/shard_map/all_to_all | solution.py:20
  189.5 52.5 %all-to-all-done.4 = bf16[64,24,128]{2,1,0:T(8,128)(2,1)S(1)} async-done(((bf16[64,24,128]{2,1,0:T(8,128)(2,1)}), bf16[64,24,128]{2,1,0:T(8,128)(2,1)S(1)}, u32[]{:S(2)}, u32[]{:S(2)}) %all-to-all-start.4) | async-done | bytes 393248 | tf_op jit(solution)/shard_map/all_to_all | solution.py:20
  242.0 0.8 fusion.95
  244.5 3.5 %all-to-all-start.5 = ((f32[16,3,128]{2,1,0:T(4,128)}), f32[16,3,128]{2,1,0:T(4,128)S(1)}, u32[]{:S(2)}, u32[]{:S(2)}) async-start(f32[16,3,128]{2,1,0:T(4,128)} %broadcast_in_dim.176), calls=%async_computation.5 | async-start | bytes 65536 | tf_op jit(solution)/shard_map/all_to_all | solution.py:20
  249.3 5.2 %all-to-all-done.5 = f32[16,3,128]{2,1,0:T(4,128)S(1)} async-done(((f32[16,3,128]{2,1,0:T(4,128)}), f32[16,3,128]{2,1,0:T(4,128)S(1)}, u32[]{:S(2)}, u32[]{:S(2)}) %all-to-all-start.5) | async-done | bytes 24608 | tf_op jit(solution)/shard_map/all_to_all | solution.py:20
  254.6 0.7 copy.80
  (133 shorter events, 14.9 us)
Async XLA Ops:
  0.6 36.5 %copy-start.22 = (f32[24]{0:T(128)}, f32[24]{0:T(128)S(1)}, u32[]{:S(2)}) copy-start(f32[24]{0:T(128)S(1)} %get-tuple-element.95) | copy-start | bytes 292
  1.5 35.6 %copy-start.11 = (s32[48,8]{1,0:T(8,128)}, s32[48,8]{1,0:T(8,128)S(1)}, u32[]{:S(2)}) copy-start(s32[48,8]{1,0:T(8,128)S(1)} %copy.64) | copy-start | bytes 4612
  1.5 35.7 %copy-start.6 = (bf16[1,1536,256]{2,1,0:T(8,128)(2,1)S(1)}, bf16[1,1536,256]{2,1,0:T(8,128)(2,1)}, u32[]{:S(2)}) copy-start(bf16[1,1536,256]{2,1,0:T(8,128)(2,1)} %param.12) | copy-start | bytes 2359300
  1.8 35.4 %copy-start.9 = (f32[48,64]{1,0:T(8,128)}, f32[48,64]{1,0:T(8,128)S(1)}, u32[]{:S(2)}) copy-start(f32[48,64]{1,0:T(8,128)S(1)} %convolution_select_fusion) | copy-start | bytes 36868
  1.9 35.3 %copy-start.13 = (f32[64,192]{1,0:T(8,128)}, f32[64,192]{1,0:T(8,128)S(1)}, u32[]{:S(2)}) copy-start(f32[64,192]{1,0:T(8,128)S(1)} %copy.73) | copy-start | bytes 147460
  2.9 0.6 copy-start.7
  4.6 32.6 %copy-start.15 = (bf16[48,128]{1,0:T(8,128)(2,1)}, bf16[48,128]{1,0:T(8,128)(2,1)S(1)}, u32[]{:S(2)}) copy-start(bf16[48,128]{1,0:T(8,128)(2,1)S(1)} %get-tuple-element.81) | copy-start | bytes 36868
  4.6 32.6 %copy-start.17 = (bf16[48,128]{1,0:T(8,128)(2,1)}, bf16[48,128]{1,0:T(8,128)(2,1)S(1)}, u32[]{:S(2)}) copy-start(bf16[48,128]{1,0:T(8,128)(2,1)S(1)} %get-tuple-element.96) | copy-start | bytes 36868
  4.6 32.6 %copy-start.19 = (bf16[48,128]{1,0:T(8,128)(2,1)}, bf16[48,128]{1,0:T(8,128)(2,1)S(1)}, u32[]{:S(2)}) copy-start(bf16[48,128]{1,0:T(8,128)(2,1)S(1)} %get-tuple-element.97) | copy-start | bytes 36868
  6.5 31.0 %copy-start.4 = (bf16[1,256,1536]{2,1,0:T(8,128)(2,1)S(1)}, bf16[1,256,1536]{2,1,0:T(8,128)(2,1)}, u32[]{:S(2)}) copy-start(bf16[1,256,1536]{2,1,0:T(8,128)(2,1)} %param.11) | copy-start | bytes 2359300
  6.5 31.0 %copy-start.5 = (bf16[1,256,1536]{2,1,0:T(8,128)(2,1)S(1)}, bf16[1,256,1536]{2,1,0:T(8,128)(2,1)}, u32[]{:S(2)}) copy-start(bf16[1,256,1536]{2,1,0:T(8,128)(2,1)} %param.10) | copy-start | bytes 2359300
  6.5 83.9 %all-to-all-start = ((bf16[64,24,128]{2,1,0:T(8,128)(2,1)}), bf16[64,24,128]{2,1,0:T(8,128)(2,1)S(1)}, u32[]{:S(2)}, u32[]{:S(2)}) async-start(bf16[64,24,128]{2,1,0:T(8,128)(2,1)} %fusion.4), calls=%async_computation | async-start | bytes 786432 | tf_op jit(solution)/shard_map/all_to_all | solution.py:20
  38.6 17.4 %collective-permute-start.2 = (bf16[768,384]{1,0:T(8,128)(2,1)S(1)}, bf16[768,384]{1,0:T(8,128)(2,1)S(1)}, u32[]{:S(2)}, u32[]{:S(2)}) collective-permute-start(bf16[768,384]{1,0:T(8,128)(2,1)S(1)} %get-tuple-element.26), channel_id=1, source_target_pairs={{0,3},{1,0},{2,1},{3,2},{4,7},{5,4},{6,5},{7,6},{8,11},{9,8},{10,9... | collective-permute-start | bytes 1769480 | tf_op jit(solution)/shard_map/ppermute | solution.py:90
  42.9 17.6 %collective-permute-start.1 = (bf16[768,384]{1,0:T(8,128)(2,1)S(1)}, bf16[768,384]{1,0:T(8,128)(2,1)S(1)}, u32[]{:S(2)}, u32[]{:S(2)}) collective-permute-start(bf16[768,384]{1,0:T(8,128)(2,1)S(1)} %get-tuple-element.27), channel_id=1, source_target_pairs={{0,2},{1,3},{2,0},{3,1},{4,6},{5,7},{6,4},{7,5},{8,10},{9,11},{10,... | collective-permute-start | bytes 1769480 | tf_op jit(solution)/shard_map/ppermute | solution.py:90
  45.4 28.9 %collective-permute-start = (bf16[768,384]{1,0:T(8,128)(2,1)S(1)}, bf16[768,384]{1,0:T(8,128)(2,1)S(1)}, u32[]{:S(2)}, u32[]{:S(2)}) collective-permute-start(bf16[768,384]{1,0:T(8,128)(2,1)S(1)} %get-tuple-element.28), channel_id=1, source_target_pairs={{0,1},{1,2},{2,3},{3,0},{4,5},{5,6},{6,7},{7,4},{8,9},{9,10},{10,1... | collective-permute-start | bytes 1769480 | tf_op jit(solution)/shard_map/ppermute | solution.py:90
  93.1 24.3 %all-to-all-start.1 = ((bf16[4,384,512]{2,1,0:T(8,128)(2,1)}), bf16[4,384,512]{2,1,0:T(8,128)(2,1)}, u32[]{:S(2)}, u32[]{:S(2)}) async-start(bf16[4,384,512]{2,1,0:T(8,128)(2,1)} %broadcast_in_dim.161), calls=%async_computation.1 | async-start | bytes 3145728 | tf_op jit(solution)/shard_map/all_to_all | solution.py:20
  118.8 1.1 copy-start
  119.9 1.1 copy-start.2
  138.5 11.9 %copy-start.3 = (bf16[4,1,256,384]{3,2,1,0:T(8,128)(2,1)S(1)}, bf16[4,1,256,384]{3,2,1,0:T(8,128)(2,1)}, u32[]{:S(2)}) copy-start(bf16[4,1,256,384]{3,2,1,0:T(8,128)(2,1)} %get-tuple-element.24) | copy-start | bytes 2359300
  151.1 1.1 copy-start.1
  172.2 16.5 %copy-start.10 = (f32[48,64]{1,0:T(8,128)S(1)}, f32[48,64]{1,0:T(8,128)}, u32[]{:S(2)}) copy-start(f32[48,64]{1,0:T(8,128)} %copy-done.9) | copy-start | bytes 36868
  172.2 16.5 %copy-start.8 = (f32[48,64]{1,0:T(8,128)S(1)}, f32[48,64]{1,0:T(8,128)}, u32[]{:S(2)}) copy-start(f32[48,64]{1,0:T(8,128)} %copy-done.7) | copy-start | bytes 36868
  173.0 69.1 %copy-start.23 = (f32[24]{0:T(128)S(1)}, f32[24]{0:T(128)}, u32[]{:S(2)}) copy-start(f32[24]{0:T(128)} %copy-done.22) | copy-start | bytes 292
  174.5 67.5 %all-to-all-start.4 = ((bf16[64,24,128]{2,1,0:T(8,128)(2,1)}), bf16[64,24,128]{2,1,0:T(8,128)(2,1)S(1)}, u32[]{:S(2)}, u32[]{:S(2)}) async-start(bf16[64,24,128]{2,1,0:T(8,128)(2,1)} %bitcast.59), calls=%async_computation.4 | async-start | bytes 786432 | tf_op jit(solution)/shard_map/all_to_all | solution.py:20
  189.5 53.4 %copy-start.14 = (f32[64,192]{1,0:T(8,128)S(1)}, f32[64,192]{1,0:T(8,128)}, u32[]{:S(2)}) copy-start(f32[64,192]{1,0:T(8,128)} %copy-done.13) | copy-start | bytes 147460
  189.5 53.4 %copy-start.16 = (bf16[48,128]{1,0:T(8,128)(2,1)S(1)}, bf16[48,128]{1,0:T(8,128)(2,1)}, u32[]{:S(2)}) copy-start(bf16[48,128]{1,0:T(8,128)(2,1)} %copy-done.15) | copy-start | bytes 36868
  189.5 53.4 %copy-start.18 = (bf16[48,128]{1,0:T(8,128)(2,1)S(1)}, bf16[48,128]{1,0:T(8,128)(2,1)}, u32[]{:S(2)}) copy-start(bf16[48,128]{1,0:T(8,128)(2,1)} %copy-done.17) | copy-start | bytes 36868
  189.5 53.4 %copy-start.20 = (bf16[48,128]{1,0:T(8,128)(2,1)S(1)}, bf16[48,128]{1,0:T(8,128)(2,1)}, u32[]{:S(2)}) copy-start(bf16[48,128]{1,0:T(8,128)(2,1)} %copy-done.19) | copy-start | bytes 36868
  189.5 53.4 %copy-start.21 = (pred[24,192]{1,0:T(8,128)(4,1)S(1)}, pred[24,192]{1,0:T(8,128)(4,1)}, u32[]{:S(2)}) copy-start(pred[24,192]{1,0:T(8,128)(4,1)} %get-tuple-element.90) | copy-start | bytes 13828
  242.8 0.8 copy-start.12
  244.5 9.9 %all-to-all-start.5 = ((f32[16,3,128]{2,1,0:T(4,128)}), f32[16,3,128]{2,1,0:T(4,128)S(1)}, u32[]{:S(2)}, u32[]{:S(2)}) async-start(f32[16,3,128]{2,1,0:T(4,128)} %broadcast_in_dim.176), calls=%async_computation.5 | async-start | bytes 65536 | tf_op jit(solution)/shard_map/all_to_all | solution.py:20

commit v4 on v3

--- a/solution.py
+++ b/solution.py
@@ -92,7 +92,10 @@
             else take(weights, me)
             for i in range(SIDE)
         ]
-    ).reshape(SIDE, 3, feats, share)
+    )
+    weights = [take(weights, me + SIDE - i) for i in range(SIDE)]
+    held = [jnp.concatenate([w[i * feats : (i + 1) * feats] for w in weights], axis=0) for i in range(3)]
+    recv, *held = lax.optimization_barrier((recv, *held))
 
     q = jnp.arange(quarter * pieces, dtype=jnp.int32)
     q_place = (q % pieces) // CAP * block + q // pieces * CAP + q % CAP
@@ -101,12 +104,9 @@
     recv = jnp.stack([jnp.dot(order, recv[i], preferred_element_type=BF16) for i in range(SIDE)])
     recv = recv.reshape(SIDE, 2 * halves, block, LANES)
     recv = jnp.concatenate([recv[:, i].reshape(slots, LANES) for i in range(2 * halves)], axis=1)
-    recv, weights = lax.optimization_barrier((recv, weights))
     recv = exchange(jnp.broadcast_to(recv[None], (SIDE, slots, 2 * feats)), "x")
-    recv = [take(recv, me + SIDE - i) for i in range(SIDE)]
-    tok = jnp.concatenate([v[:, :feats] for v in recv], axis=1)
-    grad = jnp.concatenate([v[:, feats:] for v in recv], axis=1)
-    held = [weights[:, i].reshape(SIDE * feats, share) for i in range(3)]
+    tok = jnp.concatenate([recv[i, :, :feats] for i in range(SIDE)], axis=1)
+    grad = jnp.concatenate([recv[i, :, feats:] for i in range(SIDE)], axis=1)
     pre = [times(v, w).astype(BF16) for v, w in zip((tok, tok, grad), held)]
     pre = jnp.concatenate(pre, axis=1)
 
@@ -129,7 +129,6 @@
             for i in range(SIDE)
         ]
     )
-    back = jnp.stack([take(back, me + SIDE - i) for i in range(SIDE)])
     back = jnp.sum(exchange(back, "x").astype(F32), axis=0).astype(BF16)
     back = jnp.stack(
         [back[:, i * LANES : (i + 1) * LANES].reshape(SIDE, block, LANES) for i in range(2 * halves)], axis=1
@@ -148,6 +147,7 @@
     dots_te = sum(jnp.where(rank_t == s, dots[:, s : s + 1], 0.0) for s in range(CAP)).T
     local = jnp.sum(jnp.where(names, dots_te[:, None, :], 0.0), axis=2)
     parts = SIDE * SIDE
+    back, local = lax.optimization_barrier((back, local))
     local = jnp.broadcast_to(local.reshape(1, -1, LANES), (parts, local.size // LANES, LANES))
     grad_gates = jnp.sum(exchange(local, ("y", "x")), axis=0).reshape(gates.shape)
 

time: 256 us -> 248 us (0.969)
  blocking collectives: 44.9 us -> 67.2 us
  waiting for transfers between devices: 118 us -> 96.6 us
  local copies, waits for them, and re-layouts: 13.7 us -> 9.81 us
  starting transfers between devices: 61.8 us -> 58.2 us
    all_to_all x2 -> x3, blocking collectives: 33.3 us -> 55.7 us  [exchange(): return lax.all_to_all(v, axes, split_axis=0, concat_axis=0, tiled=True)]
    all_to_all x4 -> x3, waiting for transfers between devices: 91.9 us -> 74.5 us  [exchange(): return lax.all_to_all(v, axes, split_axis=0, concat_axis=0, tiled=True)]
    all_to_all x4 -> x3, starting transfers between devices: 52.5 us -> 47.7 us  [exchange(): return lax.all_to_all(v, axes, split_axis=0, concat_axis=0, tiled=True)]
    ppermute x3, waiting for transfers between devices: 26.3 us -> 22.1 us  [shards(): lax.ppermute(take(weights, me + i), 'x', [(d, (d + i) % SIDE) for d in ra...]
    unnamed x52 -> x15, local copies, waits for them, and re-layouts: 5.19 us -> 3.37 us
  transfers between devices with their start and end apart: 7 -> 6, of which waited for: 7 -> 6; matrix products, arithmetic and copies ran while one was open for 2% -> 2% of each run, Pallas kernels for 0% -> 0%
where the time goes in v4:
time: 248 us; the launch traced here: 247 us
  waiting for transfers between devices  96.6 us (39%)
  blocking collectives  67.2 us (27%)
  starting transfers between devices  58.2 us (23%)
  local copies, waits for them, and re-layouts  9.81 us (4%)
  matrix products  8.8 us (4%)
  other arithmetic  5.4 us (2%)
    all_to_all x3, waiting for transfers between devices, exchange(): return lax.all_to_all(v, axes, split_axis=0, concat_axis=0, tiled=True)  74.5 us
    all_to_all x3, blocking collectives, exchange(): return lax.all_to_all(v, axes, split_axis=0, concat_axis=0, tiled=True)  55.7 us
    all_to_all x3, starting transfers between devices, exchange(): return lax.all_to_all(v, axes, split_axis=0, concat_axis=0, tiled=True)  47.7 us
    ppermute x3, waiting for transfers between devices, shards(): lax.ppermute(take(weights, me + i), 'x', [(d, (d + i) % SIDE) for d in ra...  22.1 us
    all_gather x1, blocking collectives, shards(): lax.all_gather(jnp.concatenate([act, grad_gate, grad_up], axis=1), 'y', a...  11.5 us
    ppermute x3, starting transfers between devices, shards(): lax.ppermute(take(weights, me + i), 'x', [(d, (d + i) % SIDE) for d in ra...  10.5 us
  transfers between devices with their start and end apart: 6, of which 6 were waited for; matrix products, arithmetic and copies ran while one was open for 2% of the time, Pallas kernels for 0%

profile of v4, /device:TPU:1, one launch (start us, length us, event | category | flops | bytes accessed | tf_op | source)
XLA Modules:
  0.0 247.3 jit_solution(10522524284244203029)
XLA Ops:
  0.7 0.8 copy.56
  1.5 0.8 copy.58
  3.2 0.8 fusion.88
  4.1 1.3 fusion.4
  5.3 30.7 %all-to-all-start = ((bf16[64,24,128]{2,1,0:T(8,128)(2,1)}), bf16[64,24,128]{2,1,0:T(8,128)(2,1)}, u32[]{:S(2)}, u32[]{:S(2)}) async-start(bf16[64,24,128]{2,1,0:T(8,128)(2,1)} %fusion.4), calls=%async_computation | async-start | bytes 786432 | tf_op jit(solution)/shard_map/all_to_all | solution.py:20
  37.9 1.2 constant_dynamic-slice_fusion
  39.0 3.1 %collective-permute-start = (bf16[768,384]{0,1:T(8,128)(2,1)}, bf16[768,384]{0,1:T(8,128)(2,1)S(1)}, u32[]{:S(2)}, u32[]{:S(2)}) collective-permute-start(bf16[768,384]{0,1:T(8,128)(2,1)} %get-tuple-element.42), channel_id=1, source_target_pairs={{0,1},{1,2},{2,3},{3,0},{4,5},{5,6},{6,7},{7,4},{8,9},{9,10},{10,1... | collective-permute-start | bytes 1769480 | tf_op jit(solution)/shard_map/ppermute | solution.py:90
  42.2 4.4 %collective-permute-start.1 = (bf16[768,384]{0,1:T(8,128)(2,1)}, bf16[768,384]{0,1:T(8,128)(2,1)S(1)}, u32[]{:S(2)}, u32[]{:S(2)}) collective-permute-start(bf16[768,384]{0,1:T(8,128)(2,1)} %get-tuple-element.41), channel_id=1, source_target_pairs={{0,2},{1,3},{2,0},{3,1},{4,6},{5,7},{6,4},{7,5},{8,10},{9,11},{10,... | collective-permute-start | bytes 1769480 | tf_op jit(solution)/shard_map/ppermute | solution.py:90
  46.5 3.1 %collective-permute-start.2 = (bf16[768,384]{0,1:T(8,128)(2,1)S(1)}, bf16[768,384]{0,1:T(8,128)(2,1)S(1)}, u32[]{:S(2)}, u32[]{:S(2)}) collective-permute-start(bf16[768,384]{0,1:T(8,128)(2,1)S(1)} %get-tuple-element.40), channel_id=1, source_target_pairs={{0,3},{1,0},{2,1},{3,2},{4,7},{5,4},{6,5},{7,6},{8,11},{9,8},{10,9... | collective-permute-start | bytes 1769480 | tf_op jit(solution)/shard_map/ppermute | solution.py:90
  49.6 7.2 %collective-permute-done = bf16[768,384]{0,1:T(8,128)(2,1)S(1)} collective-permute-done((bf16[768,384]{0,1:T(8,128)(2,1)}, bf16[768,384]{0,1:T(8,128)(2,1)S(1)}, u32[]{:S(2)}, u32[]{:S(2)}) %collective-permute-start) | collective-permute-done | bytes 589856 | tf_op jit(solution)/shard_map/ppermute | solution.py:90
  56.8 13.6 %collective-permute-done.1 = bf16[768,384]{0,1:T(8,128)(2,1)S(1)} collective-permute-done((bf16[768,384]{0,1:T(8,128)(2,1)}, bf16[768,384]{0,1:T(8,128)(2,1)S(1)}, u32[]{:S(2)}, u32[]{:S(2)}) %collective-permute-start.1) | collective-permute-done | bytes 589856 | tf_op jit(solution)/shard_map/ppermute | solution.py:90
  70.4 1.3 collective-permute-done.2
  72.6 16.8 %all-to-all-done = bf16[64,24,128]{2,1,0:T(8,128)(2,1)} async-done(((bf16[64,24,128]{2,1,0:T(8,128)(2,1)}), bf16[64,24,128]{2,1,0:T(8,128)(2,1)}, u32[]{:S(2)}, u32[]{:S(2)}) %all-to-all-start) | async-done | bytes 393248 | tf_op jit(solution)/shard_map/all_to_all | solution.py:20
  89.3 1.1 fusion.86
  91.9 23.4 %all_to_all.30 = bf16[4,384,512]{2,1,0:T(8,128)(2,1)S(1)} all-to-all(bf16[4,384,512]{2,1,0:T(8,128)(2,1)S(1)} %broadcast_in_dim.161), channel_id=1, replica_groups=mesh['dp'=64,'y'=4,'x'=4] {'x'}, dimensions={0} | all-to-all | bytes 3145728 | tf_op jit(solution)/shard_map/all_to_all | solution.py:20
  115.3 0.6 convolution_convert_fusion.3
  115.9 0.6 convolution_convert_fusion.2
  116.5 0.6 convolution_convert_fusion.1
  117.2 0.9 copy.69
  118.1 15.0 %all_to_all.31 = bf16[4,96,1152]{2,1,0:T(8,128)(2,1)S(1)} all-to-all(bf16[4,96,1152]{2,1,0:T(8,128)(2,1)S(1)} %bitcast.158), channel_id=1, replica_groups=mesh['dp'=64,'y'=4,'x'=4] {'y'}, dimensions={0} | all-to-all | bytes 1769472 | tf_op jit(solution)/shard_map/all_to_all | solution.py:20
  133.3 11.5 %all_gather.3 = bf16[384,1152]{1,0:T(8,128)(2,1)S(1)} all-gather(bf16[96,1152]{1,0:T(8,128)(2,1)S(1)} %pad_maximum_fusion.13), channel_id=1, replica_groups=mesh['dp'=64,'y'=4,'x'=4] {'y'}, dimensions={0}, use_global_device_ids=true | all-gather | bytes 1105920 | tf_op jit(solution)/shard_map/all_gather | solution.py:121
  147.0 17.4 %all_to_all.32 = bf16[4,384,512]{2,1,0:T(8,128)(2,1)S(1)} all-to-all(bf16[4,384,512]{2,1,0:T(8,128)(2,1)S(1)} %pad_maximum_fusion.3), channel_id=1, replica_groups=mesh['dp'=64,'y'=4,'x'=4] {'x'}, dimensions={0} | all-to-all | bytes 3145728 | tf_op jit(solution)/shard_map/all_to_all | solution.py:20
  166.5 0.8 pad_maximum_fusion.12
  167.3 13.5 %all-to-all-start.4 = ((bf16[64,24,128]{2,1,0:T(8,128)(2,1)}), bf16[64,24,128]{2,1,0:T(8,128)(2,1)S(1)}, u32[]{:S(2)}, u32[]{:S(2)}) async-start(bf16[64,24,128]{2,1,0:T(8,128)(2,1)} %bitcast.71), calls=%async_computation.4 | async-start | bytes 786432 | tf_op jit(solution)/shard_map/all_to_all | solution.py:20
  181.6 52.6 %all-to-all-done.4 = bf16[64,24,128]{2,1,0:T(8,128)(2,1)S(1)} async-done(((bf16[64,24,128]{2,1,0:T(8,128)(2,1)}), bf16[64,24,128]{2,1,0:T(8,128)(2,1)S(1)}, u32[]{:S(2)}, u32[]{:S(2)}) %all-to-all-start.4) | async-done | bytes 393248 | tf_op jit(solution)/shard_map/all_to_all | solution.py:20
  235.1 0.8 fusion.90
  236.0 0.6 broadcast_in_dim.176
  236.6 3.5 %all-to-all-start.5 = ((f32[16,3,128]{2,1,0:T(4,128)}), f32[16,3,128]{2,1,0:T(4,128)S(1)}, u32[]{:S(2)}, u32[]{:S(2)}) async-start(f32[16,3,128]{2,1,0:T(4,128)} %broadcast_in_dim.176), calls=%async_computation.5 | async-start | bytes 65536 | tf_op jit(solution)/shard_map/all_to_all | solution.py:20
  240.1 0.6 pad_maximum_fusion.17
  240.7 0.6 pad_maximum_fusion.16
  241.4 5.2 %all-to-all-done.5 = f32[16,3,128]{2,1,0:T(4,128)S(1)} async-done(((f32[16,3,128]{2,1,0:T(4,128)}), f32[16,3,128]{2,1,0:T(4,128)S(1)}, u32[]{:S(2)}, u32[]{:S(2)}) %all-to-all-start.5) | async-done | bytes 24608 | tf_op jit(solution)/shard_map/all_to_all | solution.py:20
  246.6 0.7 copy.73
  (91 shorter events, 11.4 us)
Async XLA Ops:
  1.5 34.6 %copy-start.3 = (bf16[1,256,1536]{2,1,0:T(8,128)(2,1)S(1)}, bf16[1,256,1536]{2,1,0:T(8,128)(2,1)}, u32[]{:S(2)}) copy-start(bf16[1,256,1536]{2,1,0:T(8,128)(2,1)} %param.10) | copy-start | bytes 2359300
  5.3 31.1 %copy-start.4 = (bf16[1,256,1536]{2,1,0:T(8,128)(2,1)S(1)}, bf16[1,256,1536]{2,1,0:T(8,128)(2,1)}, u32[]{:S(2)}) copy-start(bf16[1,256,1536]{2,1,0:T(8,128)(2,1)} %param.11) | copy-start | bytes 2359300
  5.3 84.0 %all-to-all-start = ((bf16[64,24,128]{2,1,0:T(8,128)(2,1)}), bf16[64,24,128]{2,1,0:T(8,128)(2,1)}, u32[]{:S(2)}, u32[]{:S(2)}) async-start(bf16[64,24,128]{2,1,0:T(8,128)(2,1)} %fusion.4), calls=%async_computation | async-start | bytes 786432 | tf_op jit(solution)/shard_map/all_to_all | solution.py:20
  36.1 1.1 copy-start.2
  39.0 17.8 %collective-permute-start = (bf16[768,384]{0,1:T(8,128)(2,1)}, bf16[768,384]{0,1:T(8,128)(2,1)S(1)}, u32[]{:S(2)}, u32[]{:S(2)}) collective-permute-start(bf16[768,384]{0,1:T(8,128)(2,1)} %get-tuple-element.42), channel_id=1, source_target_pairs={{0,1},{1,2},{2,3},{3,0},{4,5},{5,6},{6,7},{7,4},{8,9},{9,10},{10,1... | collective-permute-start | bytes 1769480 | tf_op jit(solution)/shard_map/ppermute | solution.py:90
  42.2 28.3 %collective-permute-start.1 = (bf16[768,384]{0,1:T(8,128)(2,1)}, bf16[768,384]{0,1:T(8,128)(2,1)S(1)}, u32[]{:S(2)}, u32[]{:S(2)}) collective-permute-start(bf16[768,384]{0,1:T(8,128)(2,1)} %get-tuple-element.41), channel_id=1, source_target_pairs={{0,2},{1,3},{2,0},{3,1},{4,6},{5,7},{6,4},{7,5},{8,10},{9,11},{10,... | collective-permute-start | bytes 1769480 | tf_op jit(solution)/shard_map/ppermute | solution.py:90
  46.5 25.2 %collective-permute-start.2 = (bf16[768,384]{0,1:T(8,128)(2,1)S(1)}, bf16[768,384]{0,1:T(8,128)(2,1)S(1)}, u32[]{:S(2)}, u32[]{:S(2)}) collective-permute-start(bf16[768,384]{0,1:T(8,128)(2,1)S(1)} %get-tuple-element.40), channel_id=1, source_target_pairs={{0,3},{1,0},{2,1},{3,2},{4,7},{5,4},{6,5},{7,6},{8,11},{9,8},{10,9... | collective-permute-start | bytes 1769480 | tf_op jit(solution)/shard_map/ppermute | solution.py:90
  72.6 42.8 %copy-start = (bf16[1024,384]{0,1:T(8,128)(2,1)}, bf16[1024,384]{0,1:T(8,128)(2,1)S(1)}, u32[]{:S(2)}) copy-start(bf16[1024,384]{0,1:T(8,128)(2,1)S(1)} %get-tuple-element.10) | copy-start | bytes 2359300
  133.3 12.1 %copy-start.1 = (bf16[1024,384]{0,1:T(8,128)(2,1)S(1)}, bf16[1024,384]{0,1:T(8,128)(2,1)}, u32[]{:S(2)}) copy-start(bf16[1024,384]{0,1:T(8,128)(2,1)} %copy-done) | copy-start | bytes 2359300
  167.3 66.8 %all-to-all-start.4 = ((bf16[64,24,128]{2,1,0:T(8,128)(2,1)}), bf16[64,24,128]{2,1,0:T(8,128)(2,1)S(1)}, u32[]{:S(2)}, u32[]{:S(2)}) async-start(bf16[64,24,128]{2,1,0:T(8,128)(2,1)} %bitcast.71), calls=%async_computation.4 | async-start | bytes 786432 | tf_op jit(solution)/shard_map/all_to_all | solution.py:20
  236.6 9.9 %all-to-all-start.5 = ((f32[16,3,128]{2,1,0:T(4,128)}), f32[16,3,128]{2,1,0:T(4,128)S(1)}, u32[]{:S(2)}, u32[]{:S(2)}) async-start(f32[16,3,128]{2,1,0:T(4,128)} %broadcast_in_dim.176), calls=%async_computation.5 | async-start | bytes 65536 | tf_op jit(solution)/shard_map/all_to_all | solution.py:20

commit v5 on v4

v5 whole, which is shorter than its diff:
```python
import jax
import jax.numpy as jnp
from jax import lax
from jax.sharding import Mesh, PartitionSpec as P

CAP = 6
LANES = 128
SIDE = 4
F32 = jnp.float32
BF16 = jnp.bfloat16


def split3(v):
    hi = v.astype(BF16).astype(F32)
    mid = (v - hi).astype(BF16).astype(F32)
    return hi, mid, v - hi - mid


def exchange(v, axes):
    return lax.all_to_all(v, axes, split_axis=0, concat_axis=0, tiled=True)


def take(v, i):
    return lax.dynamic_index_in_dim(v, i % SIDE, axis=0, keepdims=False)


def routing(picks_t, gates_t, experts):
    ids = jnp.arange(experts, dtype=jnp.int32)
    names = picks_t[:, None, :] == ids[None, :, None]
    member = jnp.any(names, axis=0)
    gate = jnp.sum(jnp.where(names, gates_t[:, None, :], 0.0), axis=0)
    rows = picks_t.shape[1]
    before = jnp.arange(rows)[:, None] < jnp.arange(rows)[None, :]
    rank = jnp.dot(member.astype(BF16), before.astype(BF16), preferred_element_type=F32)
    return names, jnp.where(member, rank, -1000.0), gate


def times(a, b):
    return jnp.dot(a, b, preferred_element_type=F32)


def times_t(a, b):
    return lax.dot_general(a, b, (((1,), (1,)), ((), ())), preferred_element_type=F32)


def shards(tokens, picks, gates, w_gate, w_up, w_down, cotangent):
    rows, feats = tokens.shape
    experts = lax.axis_size("dp")
    halves = feats // LANES
    pieces = 2 * halves * CAP
    hidden = w_gate.shape[2]
    quarter = experts // SIDE
    slots = experts * CAP
    block = quarter * CAP
    share = hidden // SIDE

    names, rank, gate = routing(picks.T, gates.T, experts)

    j = jnp.arange(pieces, dtype=jnp.int32)
    j_row = j.astype(F32)[None, :, None]

    def rows_of(rank, blocks):
        return jnp.concatenate([rank + CAP * i for i in blocks], axis=1)[:, None, :]

    source = jnp.concatenate(
        [v[:, h * LANES : (h + 1) * LANES] for v in (tokens, cotangent) for h in range(halves)], axis=0
    )

    def select(target, rows_from):
        mask = (target == j_row).astype(BF16).reshape(experts * pieces, -1)
        return times(mask, rows_from).reshape(experts, pieces, LANES)

    hit = rank[:, None, :] == (j % CAP).astype(F32)[None, :, None]
    scale = jnp.sum(jnp.where(hit, gate[:, None, :], 0.0), axis=2, keepdims=True)
    scale = jnp.where((j >= halves * CAP)[None, :, None], scale, 1.0)
    packed = (select(rows_of(rank, range(2 * halves)), source) * scale).astype(BF16)

    recv = exchange(packed, "dp")

    weights = jnp.concatenate([w_gate[0], w_up[0], w_down[0].T], axis=0)
    weights = jnp.stack([weights[:, i * share : (i + 1) * share] for i in range(SIDE)])
    me = lax.axis_index("x")
    weights = jnp.stack(
        [
            lax.ppermute(take(weights, me + i), "x", [(d, (d + i) % SIDE) for d in range(SIDE)])
            if i
            else take(weights, me)
            for i in range(SIDE)
        ]
    )
    weights = [take(weights, me + SIDE - i) for i in range(SIDE)]
    held = [jnp.concatenate([w[i * feats : (i + 1) * feats] for w in weights], axis=0) for i in range(3)]
    recv, *held = lax.optimization_barrier((recv, *held))

    q = jnp.arange(quarter * pieces, dtype=jnp.int32)
    q_place = (q % pieces) // CAP * block + q // pieces * CAP + q % CAP
    order = (q_place[None, :] == q[:, None]).astype(BF16)
    recv = recv.reshape(SIDE, quarter * pieces, LANES)
    recv = lax.dot_general(order, recv, (((1,), (1,)), ((), ())), preferred_element_type=BF16)
    recv = recv.reshape(2 * halves, block, SIDE, LANES).transpose(2, 1, 0, 3).reshape(slots, 2 * feats)
    recv = exchange(jnp.broadcast_to(recv[None], (SIDE, slots, 2 * feats)), "x")
    tok = jnp.concatenate([recv[i, :, :feats] for i in range(SIDE)], axis=1)
    grad = jnp.concatenate([recv[i, :, feats:] for i in range(SIDE)], axis=1)
    pre = [times(v, w).astype(BF16) for v, w in zip((tok, tok, grad), held)]
    pre = jnp.concatenate(pre, axis=1)

    pre = exchange(pre.reshape(SIDE, slots // SIDE, 3 * share), "y")
    pre = jnp.sum(pre.astype(F32), axis=0)
    gate_pre, up_pre, grad_hidden = pre[:, :share], pre[:, share : 2 * share], pre[:, 2 * share :]
    logistic = jax.nn.sigmoid(gate_pre)
    silu = gate_pre * logistic
    act = (silu * up_pre).astype(BF16)
    grad_gate = (grad_hidden * up_pre * (logistic * (1.0 + gate_pre * (1.0 - logistic)))).astype(BF16)
    grad_up = (grad_hidden * silu).astype(BF16)
    every = lax.all_gather(jnp.concatenate([act, grad_gate, grad_up], axis=1), "y", axis=0, tiled=True)

    act, grad_gate, grad_up = (every[:, i * share : (i + 1) * share] for i in range(3))
    expert_out = times_t(act, held[2]).astype(BF16)
    grad_pick = (times_t(grad_gate, held[0]) + times_t(grad_up, held[1])).astype(BF16)
    back = jnp.stack(
        [
            jnp.concatenate([v[:, i * feats : (i + 1) * feats] for v in (expert_out, grad_pick)], axis=1)
            for i in range(SIDE)
        ]
    )
    back = jnp.sum(exchange(back, "x").astype(F32), axis=0).astype(BF16)
    back = back.reshape(SIDE, block, 2 * halves, LANES).transpose(2, 1, 0, 3)
    back = back.reshape(quarter * pieces, SIDE, LANES)
    back = lax.dot_general(order, back, (((0,), (0,)), ((), ())), preferred_element_type=BF16)
    back = back.transpose(1, 0, 2)
    back, rank, gate = lax.optimization_barrier((back, rank, gate))
    back = exchange(back.reshape(experts, pieces, LANES), "dp")

    cot_rows = select(rows_of(rank, range(halves)), source[halves * rows :]).astype(BF16)
    kinds = [g for g in split3(gate)] + [jnp.ones_like(gate)]
    value = jnp.concatenate([g for g in kinds for _ in range(halves)], axis=1)[:, None, :]
    mix = rows_of(rank, [i // 3 * halves + h for i in range(4) for h in range(halves)])
    mix = jnp.where(mix == j_row, value, 0.0).astype(BF16).reshape(experts * pieces, -1)
    back, cot_rows, mix = lax.optimization_barrier((back, cot_rows, mix))

    dots = jnp.sum(cot_rows.astype(F32) * back.astype(F32), axis=2)
    dots = sum(dots[:, h * CAP : (h + 1) * CAP] for h in range(halves))
    dots = sum(jnp.where(rank == i, dots[:, i : i + 1], 0.0) for i in range(CAP))
    local = jnp.sum(jnp.where(names, dots[None], 0.0), axis=1)
    back, local = lax.optimization_barrier((back, local))
    grad_gates = jnp.sum(exchange(jnp.broadcast_to(local, (SIDE * SIDE, *local.shape)), ("y", "x")), axis=0).T

    out = lax.dot_general(
        mix, back.reshape(experts * pieces, LANES), (((0,), (0,)), ((), ())), preferred_element_type=F32
    ).reshape(4, halves, rows, LANES)
    mixed = out[0] + out[1] + out[2]
    mixed = jnp.concatenate([mixed[h] for h in range(halves)], axis=1).astype(BF16)
    grad_tokens = jnp.concatenate([out[3, h] for h in range(halves)], axis=1).astype(BF16)
    return mixed, grad_tokens, grad_gates


def solution(mesh):
    wide = Mesh(mesh.devices.reshape(mesh.devices.shape[0], SIDE, SIDE), ("dp", "y", "x"))
    split = ("y", "x")
    placed = (
        P("dp", split),
        P("dp", None),
        P("dp", None),
        P("dp", split, None),
        P("dp", split, None),
        P("dp", None, split),
        P("dp", split),
    )
    return jax.shard_map(
        shards,
        mesh=wide,
        in_specs=placed,
        out_specs=(P("dp", split), P("dp", split), P("dp", None)),
        check_vma=False,
    )
```

time: 248 us -> 247 us (level)
  no operation moved by 1% of the time
where the time goes in v5:
time: 247 us; the launch traced here: 246 us
  waiting for transfers between devices  95.5 us (39%)
  blocking collectives  67.1 us (27%)
  starting transfers between devices  57.9 us (23%)
  matrix products  8.31 us (3%)
  local copies, waits for them, and re-layouts  8.1 us (3%)
  other arithmetic  7.57 us (3%)
    all_to_all x3, waiting for transfers between devices, exchange(): return lax.all_to_all(v, axes, split_axis=0, concat_axis=0, tiled=True)  73.4 us
    all_to_all x3, blocking collectives, exchange(): return lax.all_to_all(v, axes, split_axis=0, concat_axis=0, tiled=True)  55.6 us
    all_to_all x3, starting transfers between devices, exchange(): return lax.all_to_all(v, axes, split_axis=0, concat_axis=0, tiled=True)  47.4 us
    ppermute x3, waiting for transfers between devices, shards(): lax.ppermute(take(weights, me + i), 'x', [(d, (d + i) % SIDE) for d in ra...  22.1 us
    all_gather x1, blocking collectives, shards(): lax.all_gather(jnp.concatenate([act, grad_gate, grad_up], axis=1), 'y', a...  11.5 us
    ppermute x3, starting transfers between devices, shards(): lax.ppermute(take(weights, me + i), 'x', [(d, (d + i) % SIDE) for d in ra...  10.5 us
  transfers between devices with their start and end apart: 6, of which 6 were waited for; matrix products, arithmetic and copies ran while one was open for 2% of the time, Pallas kernels for 0%

profile of v5, /device:TPU:1, one launch (start us, length us, event | category | flops | bytes accessed | tf_op | source)
XLA Modules:
  0.0 245.9 jit_solution(12148188847040994139)
XLA Ops:
  0.7 0.9 fusion.32
  1.9 0.9 select_reduce_fusion.2
  3.1 0.8 fusion.70
  3.8 1.2 fusion.6
  5.1 30.6 %all-to-all-start = ((bf16[64,24,128]{2,1,0:T(8,128)(2,1)}), bf16[64,24,128]{2,1,0:T(8,128)(2,1)}, u32[]{:S(2)}, u32[]{:S(2)}) async-start(bf16[64,24,128]{2,1,0:T(8,128)(2,1)} %fusion.6), calls=%async_computation | async-start | bytes 786432 | tf_op jit(solution)/shard_map/all_to_all | solution.py:20
  37.5 1.2 constant_dynamic-slice_fusion
  38.6 3.1 %collective-permute-start = (bf16[768,384]{0,1:T(8,128)(2,1)}, bf16[768,384]{0,1:T(8,128)(2,1)S(1)}, u32[]{:S(2)}, u32[]{:S(2)}) collective-permute-start(bf16[768,384]{0,1:T(8,128)(2,1)} %get-tuple-element.48), channel_id=1, source_target_pairs={{0,1},{1,2},{2,3},{3,0},{4,5},{5,6},{6,7},{7,4},{8,9},{9,10},{10,1... | collective-permute-start | bytes 1769480 | tf_op jit(solution)/shard_map/ppermute | solution.py:85
  41.8 4.4 %collective-permute-start.1 = (bf16[768,384]{0,1:T(8,128)(2,1)}, bf16[768,384]{0,1:T(8,128)(2,1)S(1)}, u32[]{:S(2)}, u32[]{:S(2)}) collective-permute-start(bf16[768,384]{0,1:T(8,128)(2,1)} %get-tuple-element.47), channel_id=1, source_target_pairs={{0,2},{1,3},{2,0},{3,1},{4,6},{5,7},{6,4},{7,5},{8,10},{9,11},{10,... | collective-permute-start | bytes 1769480 | tf_op jit(solution)/shard_map/ppermute | solution.py:85
  46.1 3.1 %collective-permute-start.2 = (bf16[768,384]{0,1:T(8,128)(2,1)S(1)}, bf16[768,384]{0,1:T(8,128)(2,1)S(1)}, u32[]{:S(2)}, u32[]{:S(2)}) collective-permute-start(bf16[768,384]{0,1:T(8,128)(2,1)S(1)} %get-tuple-element.46), channel_id=1, source_target_pairs={{0,3},{1,0},{2,1},{3,2},{4,7},{5,4},{6,5},{7,6},{8,11},{9,8},{10,9... | collective-permute-start | bytes 1769480 | tf_op jit(solution)/shard_map/ppermute | solution.py:85
  49.2 7.2 %collective-permute-done = bf16[768,384]{0,1:T(8,128)(2,1)S(1)} collective-permute-done((bf16[768,384]{0,1:T(8,128)(2,1)}, bf16[768,384]{0,1:T(8,128)(2,1)S(1)}, u32[]{:S(2)}, u32[]{:S(2)}) %collective-permute-start) | collective-permute-done | bytes 589856 | tf_op jit(solution)/shard_map/ppermute | solution.py:85
  56.4 13.6 %collective-permute-done.1 = bf16[768,384]{0,1:T(8,128)(2,1)S(1)} collective-permute-done((bf16[768,384]{0,1:T(8,128)(2,1)}, bf16[768,384]{0,1:T(8,128)(2,1)S(1)}, u32[]{:S(2)}, u32[]{:S(2)}) %collective-permute-start.1) | collective-permute-done | bytes 589856 | tf_op jit(solution)/shard_map/ppermute | solution.py:85
  70.0 1.3 collective-permute-done.2
  72.1 16.9 %all-to-all-done = bf16[64,24,128]{2,1,0:T(8,128)(2,1)} async-done(((bf16[64,24,128]{2,1,0:T(8,128)(2,1)}), bf16[64,24,128]{2,1,0:T(8,128)(2,1)}, u32[]{:S(2)}, u32[]{:S(2)}) %all-to-all-start) | async-done | bytes 393248 | tf_op jit(solution)/shard_map/all_to_all | solution.py:20
  89.0 1.4 convolution_bitcast_fusion.1
  90.9 23.4 %all_to_all.30 = bf16[4,384,512]{2,1,0:T(8,128)(2,1)S(1)} all-to-all(bf16[4,384,512]{2,1,0:T(8,128)(2,1)S(1)} %broadcast_in_dim.152), channel_id=1, replica_groups=mesh['dp'=64,'y'=4,'x'=4] {'x'}, dimensions={0} | all-to-all | bytes 3145728 | tf_op jit(solution)/shard_map/all_to_all | solution.py:20
  114.3 0.6 convolution_convert_fusion.4
  115.0 0.6 convolution_convert_fusion.3
  115.6 0.6 convolution_convert_fusion.2
  116.3 0.9 copy.61
  117.1 14.9 %all_to_all.31 = bf16[4,96,1152]{2,1,0:T(8,128)(2,1)S(1)} all-to-all(bf16[4,96,1152]{2,1,0:T(8,128)(2,1)S(1)} %bitcast.128), channel_id=1, replica_groups=mesh['dp'=64,'y'=4,'x'=4] {'y'}, dimensions={0} | all-to-all | bytes 1769472 | tf_op jit(solution)/shard_map/all_to_all | solution.py:20
  132.3 11.5 %all_gather.3 = bf16[384,1152]{1,0:T(8,128)(2,1)S(1)} all-gather(bf16[96,1152]{1,0:T(8,128)(2,1)S(1)} %pad_maximum_fusion.9), channel_id=1, replica_groups=mesh['dp'=64,'y'=4,'x'=4] {'y'}, dimensions={0}, use_global_device_ids=true | all-gather | bytes 1105920 | tf_op jit(solution)/shard_map/all_gather | solution.py:115
  146.5 17.4 %all_to_all.32 = bf16[4,384,512]{2,1,0:T(8,128)(2,1)S(1)} all-to-all(bf16[4,384,512]{2,1,0:T(8,128)(2,1)S(1)} %pad_maximum_fusion.3), channel_id=1, replica_groups=mesh['dp'=64,'y'=4,'x'=4] {'x'}, dimensions={0} | all-to-all | bytes 3145728 | tf_op jit(solution)/shard_map/all_to_all | solution.py:20
  164.5 1.2 convolution_bitcast_fusion
  165.6 13.4 %all-to-all-start.4 = ((bf16[64,24,128]{2,1,0:T(8,128)(2,1)}), bf16[64,24,128]{2,1,0:T(8,128)(2,1)S(1)}, u32[]{:S(2)}, u32[]{:S(2)}) async-start(bf16[64,24,128]{2,1,0:T(8,128)(2,1)} %bitcast.51), calls=%async_computation.4 | async-start | bytes 786432 | tf_op jit(solution)/shard_map/all_to_all | solution.py:20
  180.5 51.4 %all-to-all-done.4 = bf16[64,24,128]{2,1,0:T(8,128)(2,1)S(1)} async-done(((bf16[64,24,128]{2,1,0:T(8,128)(2,1)}), bf16[64,24,128]{2,1,0:T(8,128)(2,1)S(1)}, u32[]{:S(2)}, u32[]{:S(2)}) %all-to-all-start.4) | async-done | bytes 393248 | tf_op jit(solution)/shard_map/all_to_all | solution.py:20
  233.4 0.7 reshape.195
  234.1 3.5 %all-to-all-start.5 = ((f32[16,1,384]{2,1,0:T(1,128)}), f32[16,1,384]{2,1,0:T(1,128)S(1)}, u32[]{:S(2)}, u32[]{:S(2)}) async-start(f32[16,1,384]{2,1,0:T(1,128)} %reshape.195), calls=%async_computation.5 | async-start | bytes 49152 | tf_op jit(solution)/shard_map/all_to_all | solution.py:20
  237.6 0.6 pad_maximum_fusion.15
  238.2 0.6 pad_maximum_fusion.14
  238.8 5.2 %all-to-all-done.5 = f32[16,1,384]{2,1,0:T(1,128)S(1)} async-done(((f32[16,1,384]{2,1,0:T(1,128)}), f32[16,1,384]{2,1,0:T(1,128)S(1)}, u32[]{:S(2)}, u32[]{:S(2)}) %all-to-all-start.5) | async-done | bytes 24608 | tf_op jit(solution)/shard_map/all_to_all | solution.py:20
  244.5 0.7 reduce.13
  245.3 0.6 reduce_sum.72
  (91 shorter events, 10.6 us)
Async XLA Ops:
  0.6 35.1 %copy-start.5 = (bf16[1,256,1536]{2,1,0:T(8,128)(2,1)S(1)}, bf16[1,256,1536]{2,1,0:T(8,128)(2,1)}, u32[]{:S(2)}) copy-start(bf16[1,256,1536]{2,1,0:T(8,128)(2,1)} %param.10) | copy-start | bytes 2359300
  3.8 32.2 %copy-start.6 = (bf16[1,256,1536]{2,1,0:T(8,128)(2,1)S(1)}, bf16[1,256,1536]{2,1,0:T(8,128)(2,1)}, u32[]{:S(2)}) copy-start(bf16[1,256,1536]{2,1,0:T(8,128)(2,1)} %param.11) | copy-start | bytes 2359300
  5.1 83.9 %all-to-all-start = ((bf16[64,24,128]{2,1,0:T(8,128)(2,1)}), bf16[64,24,128]{2,1,0:T(8,128)(2,1)}, u32[]{:S(2)}, u32[]{:S(2)}) async-start(bf16[64,24,128]{2,1,0:T(8,128)(2,1)} %fusion.6), calls=%async_computation | async-start | bytes 786432 | tf_op jit(solution)/shard_map/all_to_all | solution.py:20
  35.7 1.1 copy-start.4
  38.6 17.8 %collective-permute-start = (bf16[768,384]{0,1:T(8,128)(2,1)}, bf16[768,384]{0,1:T(8,128)(2,1)S(1)}, u32[]{:S(2)}, u32[]{:S(2)}) collective-permute-start(bf16[768,384]{0,1:T(8,128)(2,1)} %get-tuple-element.48), channel_id=1, source_target_pairs={{0,1},{1,2},{2,3},{3,0},{4,5},{5,6},{6,7},{7,4},{8,9},{9,10},{10,1... | collective-permute-start | bytes 1769480 | tf_op jit(solution)/shard_map/ppermute | solution.py:85
  41.8 28.3 %collective-permute-start.1 = (bf16[768,384]{0,1:T(8,128)(2,1)}, bf16[768,384]{0,1:T(8,128)(2,1)S(1)}, u32[]{:S(2)}, u32[]{:S(2)}) collective-permute-start(bf16[768,384]{0,1:T(8,128)(2,1)} %get-tuple-element.47), channel_id=1, source_target_pairs={{0,2},{1,3},{2,0},{3,1},{4,6},{5,7},{6,4},{7,5},{8,10},{9,11},{10,... | collective-permute-start | bytes 1769480 | tf_op jit(solution)/shard_map/ppermute | solution.py:85
  46.1 25.2 %collective-permute-start.2 = (bf16[768,384]{0,1:T(8,128)(2,1)S(1)}, bf16[768,384]{0,1:T(8,128)(2,1)S(1)}, u32[]{:S(2)}, u32[]{:S(2)}) collective-permute-start(bf16[768,384]{0,1:T(8,128)(2,1)S(1)} %get-tuple-element.46), channel_id=1, source_target_pairs={{0,3},{1,0},{2,1},{3,2},{4,7},{5,4},{6,5},{7,6},{8,11},{9,8},{10,9... | collective-permute-start | bytes 1769480 | tf_op jit(solution)/shard_map/ppermute | solution.py:85
  72.1 42.3 %copy-start.2 = (bf16[1024,384]{0,1:T(8,128)(2,1)}, bf16[1024,384]{0,1:T(8,128)(2,1)S(1)}, u32[]{:S(2)}) copy-start(bf16[1024,384]{0,1:T(8,128)(2,1)S(1)} %get-tuple-element.16) | copy-start | bytes 2359300
  72.1 42.9 %copy-start = (bf16[1024,384]{0,1:T(8,128)(2,1)}, bf16[1024,384]{0,1:T(8,128)(2,1)S(1)}, u32[]{:S(2)}) copy-start(bf16[1024,384]{0,1:T(8,128)(2,1)S(1)} %get-tuple-element.17) | copy-start | bytes 2359300
  132.3 12.1 %copy-start.3 = (bf16[1024,384]{0,1:T(8,128)(2,1)S(1)}, bf16[1024,384]{0,1:T(8,128)(2,1)}, u32[]{:S(2)}) copy-start(bf16[1024,384]{0,1:T(8,128)(2,1)} %copy-done.2) | copy-start | bytes 2359300
  144.4 1.1 copy-start.1
  165.6 66.2 %all-to-all-start.4 = ((bf16[64,24,128]{2,1,0:T(8,128)(2,1)}), bf16[64,24,128]{2,1,0:T(8,128)(2,1)S(1)}, u32[]{:S(2)}, u32[]{:S(2)}) async-start(bf16[64,24,128]{2,1,0:T(8,128)(2,1)} %bitcast.51), calls=%async_computation.4 | async-start | bytes 786432 | tf_op jit(solution)/shard_map/all_to_all | solution.py:20
  179.7 52.8 %copy-start.7 = (s32[48,8]{0,1:T(8,128)S(1)}, s32[48,8]{0,1:T(8,128)}, u32[]{:S(2)}) copy-start(s32[48,8]{0,1:T(8,128)} %param.8) | copy-start | bytes 4612
  234.1 9.9 %all-to-all-start.5 = ((f32[16,1,384]{2,1,0:T(1,128)}), f32[16,1,384]{2,1,0:T(1,128)S(1)}, u32[]{:S(2)}, u32[]{:S(2)}) async-start(f32[16,1,384]{2,1,0:T(1,128)} %reshape.195), calls=%async_computation.5 | async-start | bytes 49152 | tf_op jit(solution)/shard_map/all_to_all | solution.py:20

commit v6 on v5

--- a/solution.py
+++ b/solution.py
@@ -90,7 +90,6 @@
     )
     weights = [take(weights, me + SIDE - i) for i in range(SIDE)]
     held = [jnp.concatenate([w[i * feats : (i + 1) * feats] for w in weights], axis=0) for i in range(3)]
-    recv, *held = lax.optimization_barrier((recv, *held))
 
     q = jnp.arange(quarter * pieces, dtype=jnp.int32)
     q_place = (q % pieces) // CAP * block + q // pieces * CAP + q % CAP
@@ -98,6 +97,7 @@
     recv = recv.reshape(SIDE, quarter * pieces, LANES)
     recv = lax.dot_general(order, recv, (((1,), (1,)), ((), ())), preferred_element_type=BF16)
     recv = recv.reshape(2 * halves, block, SIDE, LANES).transpose(2, 1, 0, 3).reshape(slots, 2 * feats)
+    recv, *held = lax.optimization_barrier((recv, *held))
     recv = exchange(jnp.broadcast_to(recv[None], (SIDE, slots, 2 * feats)), "x")
     tok = jnp.concatenate([recv[i, :, :feats] for i in range(SIDE)], axis=1)
     grad = jnp.concatenate([recv[i, :, feats:] for i in range(SIDE)], axis=1)
@@ -142,8 +142,10 @@
     dots = sum(dots[:, h * CAP : (h + 1) * CAP] for h in range(halves))
     dots = sum(jnp.where(rank == i, dots[:, i : i + 1], 0.0) for i in range(CAP))
     local = jnp.sum(jnp.where(names, dots[None], 0.0), axis=1)
+    local = jnp.pad(local, ((0, 0), (0, LANES - rows)))
     back, local = lax.optimization_barrier((back, local))
-    grad_gates = jnp.sum(exchange(jnp.broadcast_to(local, (SIDE * SIDE, *local.shape)), ("y", "x")), axis=0).T
+    local = jnp.broadcast_to(local[None], (SIDE * SIDE, *local.shape))
+    grad_gates = jnp.sum(exchange(local, ("y", "x")), axis=0)[:, :rows].T
 
     out = lax.dot_general(
         mix, back.reshape(experts * pieces, LANES), (((0,), (0,)), ((), ())), preferred_element_type=F32

time: 247 us -> 246 us (level)
  no operation moved by 1% of the time
where the time goes in v6:
time: 246 us; the launch traced here: 245 us
  waiting for transfers between devices  96 us (39%)
  blocking collectives  67.1 us (27%)
  starting transfers between devices  57.9 us (24%)
  matrix products  8.32 us (3%)
  local copies, waits for them, and re-layouts  8.02 us (3%)
  other arithmetic  6.28 us (3%)
    all_to_all x3, waiting for transfers between devices, exchange(): return lax.all_to_all(v, axes, split_axis=0, concat_axis=0, tiled=True)  74 us
    all_to_all x3, blocking collectives, exchange(): return lax.all_to_all(v, axes, split_axis=0, concat_axis=0, tiled=True)  55.7 us
    all_to_all x3, starting transfers between devices, exchange(): return lax.all_to_all(v, axes, split_axis=0, concat_axis=0, tiled=True)  47.3 us
    ppermute x3, waiting for transfers between devices, shards(): lax.ppermute(take(weights, me + i), 'x', [(d, (d + i) % SIDE) for d in ra...  22.1 us
    all_gather x1, blocking collectives, shards(): lax.all_gather(jnp.concatenate([act, grad_gate, grad_up], axis=1), 'y', a...  11.5 us
    ppermute x3, starting transfers between devices, shards(): lax.ppermute(take(weights, me + i), 'x', [(d, (d + i) % SIDE) for d in ra...  10.5 us
  transfers between devices with their start and end apart: 6, of which 6 were waited for; matrix products, arithmetic and copies ran while one was open for 2% of the time, Pallas kernels for 0%

profile of v6, /device:TPU:1, one launch (start us, length us, event | category | flops | bytes accessed | tf_op | source)
XLA Modules:
  0.0 245.0 jit_solution(12822712210494627437)
XLA Ops:
  0.7 0.9 fusion.32
  1.9 0.9 select_reduce_fusion.2
  3.1 0.8 fusion.70
  3.8 1.2 fusion.6
  5.1 30.6 %all-to-all-start = ((bf16[64,24,128]{2,1,0:T(8,128)(2,1)}), bf16[64,24,128]{2,1,0:T(8,128)(2,1)}, u32[]{:S(2)}, u32[]{:S(2)}) async-start(bf16[64,24,128]{2,1,0:T(8,128)(2,1)} %fusion.6), calls=%async_computation | async-start | bytes 786432 | tf_op jit(solution)/shard_map/all_to_all | solution.py:20
  37.5 1.2 constant_dynamic-slice_fusion
  38.6 3.1 %collective-permute-start = (bf16[768,384]{0,1:T(8,128)(2,1)}, bf16[768,384]{0,1:T(8,128)(2,1)S(1)}, u32[]{:S(2)}, u32[]{:S(2)}) collective-permute-start(bf16[768,384]{0,1:T(8,128)(2,1)} %get-tuple-element.48), channel_id=1, source_target_pairs={{0,1},{1,2},{2,3},{3,0},{4,5},{5,6},{6,7},{7,4},{8,9},{9,10},{10,1... | collective-permute-start | bytes 1769480 | tf_op jit(solution)/shard_map/ppermute | solution.py:85
  41.8 4.4 %collective-permute-start.1 = (bf16[768,384]{0,1:T(8,128)(2,1)}, bf16[768,384]{0,1:T(8,128)(2,1)S(1)}, u32[]{:S(2)}, u32[]{:S(2)}) collective-permute-start(bf16[768,384]{0,1:T(8,128)(2,1)} %get-tuple-element.47), channel_id=1, source_target_pairs={{0,2},{1,3},{2,0},{3,1},{4,6},{5,7},{6,4},{7,5},{8,10},{9,11},{10,... | collective-permute-start | bytes 1769480 | tf_op jit(solution)/shard_map/ppermute | solution.py:85
  46.1 3.1 %collective-permute-start.2 = (bf16[768,384]{0,1:T(8,128)(2,1)S(1)}, bf16[768,384]{0,1:T(8,128)(2,1)S(1)}, u32[]{:S(2)}, u32[]{:S(2)}) collective-permute-start(bf16[768,384]{0,1:T(8,128)(2,1)S(1)} %get-tuple-element.46), channel_id=1, source_target_pairs={{0,3},{1,0},{2,1},{3,2},{4,7},{5,4},{6,5},{7,6},{8,11},{9,8},{10,9... | collective-permute-start | bytes 1769480 | tf_op jit(solution)/shard_map/ppermute | solution.py:85
  49.2 7.2 %collective-permute-done = bf16[768,384]{0,1:T(8,128)(2,1)S(1)} collective-permute-done((bf16[768,384]{0,1:T(8,128)(2,1)}, bf16[768,384]{0,1:T(8,128)(2,1)S(1)}, u32[]{:S(2)}, u32[]{:S(2)}) %collective-permute-start) | collective-permute-done | bytes 589856 | tf_op jit(solution)/shard_map/ppermute | solution.py:85
  56.4 13.6 %collective-permute-done.1 = bf16[768,384]{0,1:T(8,128)(2,1)S(1)} collective-permute-done((bf16[768,384]{0,1:T(8,128)(2,1)}, bf16[768,384]{0,1:T(8,128)(2,1)S(1)}, u32[]{:S(2)}, u32[]{:S(2)}) %collective-permute-start.1) | collective-permute-done | bytes 589856 | tf_op jit(solution)/shard_map/ppermute | solution.py:85
  70.0 1.3 collective-permute-done.2
  72.1 16.9 %all-to-all-done = bf16[64,24,128]{2,1,0:T(8,128)(2,1)} async-done(((bf16[64,24,128]{2,1,0:T(8,128)(2,1)}), bf16[64,24,128]{2,1,0:T(8,128)(2,1)}, u32[]{:S(2)}, u32[]{:S(2)}) %all-to-all-start) | async-done | bytes 393248 | tf_op jit(solution)/shard_map/all_to_all | solution.py:20
  89.0 1.4 convolution_bitcast_fusion.1
  90.9 23.4 %all_to_all.30 = bf16[4,384,512]{2,1,0:T(8,128)(2,1)S(1)} all-to-all(bf16[4,384,512]{2,1,0:T(8,128)(2,1)S(1)} %broadcast_in_dim.153), channel_id=1, replica_groups=mesh['dp'=64,'y'=4,'x'=4] {'x'}, dimensions={0} | all-to-all | bytes 3145728 | tf_op jit(solution)/shard_map/all_to_all | solution.py:20
  114.4 0.6 convolution_convert_fusion.4
  115.0 0.6 convolution_convert_fusion.3
  115.6 0.6 convolution_convert_fusion.2
  116.3 0.9 copy.61
  117.2 14.9 %all_to_all.31 = bf16[4,96,1152]{2,1,0:T(8,128)(2,1)S(1)} all-to-all(bf16[4,96,1152]{2,1,0:T(8,128)(2,1)S(1)} %bitcast.129), channel_id=1, replica_groups=mesh['dp'=64,'y'=4,'x'=4] {'y'}, dimensions={0} | all-to-all | bytes 1769472 | tf_op jit(solution)/shard_map/all_to_all | solution.py:20
  132.3 11.5 %all_gather.3 = bf16[384,1152]{1,0:T(8,128)(2,1)S(1)} all-gather(bf16[96,1152]{1,0:T(8,128)(2,1)S(1)} %pad_maximum_fusion.9), channel_id=1, replica_groups=mesh['dp'=64,'y'=4,'x'=4] {'y'}, dimensions={0}, use_global_device_ids=true | all-gather | bytes 1105920 | tf_op jit(solution)/shard_map/all_gather | solution.py:115
  143.8 0.6 convolution_convert_fusion
  146.5 17.4 %all_to_all.32 = bf16[4,384,512]{2,1,0:T(8,128)(2,1)S(1)} all-to-all(bf16[4,384,512]{2,1,0:T(8,128)(2,1)S(1)} %pad_maximum_fusion.3), channel_id=1, replica_groups=mesh['dp'=64,'y'=4,'x'=4] {'x'}, dimensions={0} | all-to-all | bytes 3145728 | tf_op jit(solution)/shard_map/all_to_all | solution.py:20
  164.5 1.2 convolution_bitcast_fusion
  165.7 13.3 %all-to-all-start.4 = ((bf16[64,24,128]{2,1,0:T(8,128)(2,1)}), bf16[64,24,128]{2,1,0:T(8,128)(2,1)S(1)}, u32[]{:S(2)}, u32[]{:S(2)}) async-start(bf16[64,24,128]{2,1,0:T(8,128)(2,1)} %bitcast.51), calls=%async_computation.4 | async-start | bytes 786432 | tf_op jit(solution)/shard_map/all_to_all | solution.py:20
  180.5 51.9 %all-to-all-done.4 = bf16[64,24,128]{2,1,0:T(8,128)(2,1)S(1)} async-done(((bf16[64,24,128]{2,1,0:T(8,128)(2,1)}), bf16[64,24,128]{2,1,0:T(8,128)(2,1)S(1)}, u32[]{:S(2)}, u32[]{:S(2)}) %all-to-all-start.4) | async-done | bytes 393248 | tf_op jit(solution)/shard_map/all_to_all | solution.py:20
  233.8 0.6 broadcast_in_dim.170
  234.4 3.5 %all-to-all-start.5 = ((f32[16,8,128]{2,1,0:T(8,128)}), f32[16,8,128]{2,1,0:T(8,128)S(1)}, u32[]{:S(2)}, u32[]{:S(2)}) async-start(f32[16,8,128]{2,1,0:T(8,128)} %broadcast_in_dim.170), calls=%async_computation.5 | async-start | bytes 131072 | tf_op jit(solution)/shard_map/all_to_all | solution.py:20
  238.0 0.6 pad_maximum_fusion.15
  238.6 0.6 pad_maximum_fusion.14
  239.2 5.2 %all-to-all-done.5 = f32[16,8,128]{2,1,0:T(8,128)S(1)} async-done(((f32[16,8,128]{2,1,0:T(8,128)}), f32[16,8,128]{2,1,0:T(8,128)S(1)}, u32[]{:S(2)}, u32[]{:S(2)}) %all-to-all-start.5) | async-done | bytes 65568 | tf_op jit(solution)/shard_map/all_to_all | solution.py:20
  244.4 0.6 slice_bitcast_fusion.14
  (89 shorter events, 9.5 us)
Async XLA Ops:
  0.6 35.1 %copy-start.5 = (bf16[1,256,1536]{2,1,0:T(8,128)(2,1)S(1)}, bf16[1,256,1536]{2,1,0:T(8,128)(2,1)}, u32[]{:S(2)}) copy-start(bf16[1,256,1536]{2,1,0:T(8,128)(2,1)} %param.11) | copy-start | bytes 2359300
  3.8 32.2 %copy-start.6 = (bf16[1,256,1536]{2,1,0:T(8,128)(2,1)S(1)}, bf16[1,256,1536]{2,1,0:T(8,128)(2,1)}, u32[]{:S(2)}) copy-start(bf16[1,256,1536]{2,1,0:T(8,128)(2,1)} %param.10) | copy-start | bytes 2359300
  5.1 83.9 %all-to-all-start = ((bf16[64,24,128]{2,1,0:T(8,128)(2,1)}), bf16[64,24,128]{2,1,0:T(8,128)(2,1)}, u32[]{:S(2)}, u32[]{:S(2)}) async-start(bf16[64,24,128]{2,1,0:T(8,128)(2,1)} %fusion.6), calls=%async_computation | async-start | bytes 786432 | tf_op jit(solution)/shard_map/all_to_all | solution.py:20
  35.7 1.1 copy-start.4
  38.6 17.8 %collective-permute-start = (bf16[768,384]{0,1:T(8,128)(2,1)}, bf16[768,384]{0,1:T(8,128)(2,1)S(1)}, u32[]{:S(2)}, u32[]{:S(2)}) collective-permute-start(bf16[768,384]{0,1:T(8,128)(2,1)} %get-tuple-element.48), channel_id=1, source_target_pairs={{0,1},{1,2},{2,3},{3,0},{4,5},{5,6},{6,7},{7,4},{8,9},{9,10},{10,1... | collective-permute-start | bytes 1769480 | tf_op jit(solution)/shard_map/ppermute | solution.py:85
  41.8 28.3 %collective-permute-start.1 = (bf16[768,384]{0,1:T(8,128)(2,1)}, bf16[768,384]{0,1:T(8,128)(2,1)S(1)}, u32[]{:S(2)}, u32[]{:S(2)}) collective-permute-start(bf16[768,384]{0,1:T(8,128)(2,1)} %get-tuple-element.47), channel_id=1, source_target_pairs={{0,2},{1,3},{2,0},{3,1},{4,6},{5,7},{6,4},{7,5},{8,10},{9,11},{10,... | collective-permute-start | bytes 1769480 | tf_op jit(solution)/shard_map/ppermute | solution.py:85
  46.1 25.2 %collective-permute-start.2 = (bf16[768,384]{0,1:T(8,128)(2,1)S(1)}, bf16[768,384]{0,1:T(8,128)(2,1)S(1)}, u32[]{:S(2)}, u32[]{:S(2)}) collective-permute-start(bf16[768,384]{0,1:T(8,128)(2,1)S(1)} %get-tuple-element.46), channel_id=1, source_target_pairs={{0,3},{1,0},{2,1},{3,2},{4,7},{5,4},{6,5},{7,6},{8,11},{9,8},{10,9... | collective-permute-start | bytes 1769480 | tf_op jit(solution)/shard_map/ppermute | solution.py:85
  72.1 42.3 %copy-start.2 = (bf16[1024,384]{0,1:T(8,128)(2,1)}, bf16[1024,384]{0,1:T(8,128)(2,1)S(1)}, u32[]{:S(2)}) copy-start(bf16[1024,384]{0,1:T(8,128)(2,1)S(1)} %get-tuple-element.16) | copy-start | bytes 2359300
  72.1 42.9 %copy-start = (bf16[1024,384]{0,1:T(8,128)(2,1)}, bf16[1024,384]{0,1:T(8,128)(2,1)S(1)}, u32[]{:S(2)}) copy-start(bf16[1024,384]{0,1:T(8,128)(2,1)S(1)} %get-tuple-element.17) | copy-start | bytes 2359300
  132.3 12.1 %copy-start.3 = (bf16[1024,384]{0,1:T(8,128)(2,1)S(1)}, bf16[1024,384]{0,1:T(8,128)(2,1)}, u32[]{:S(2)}) copy-start(bf16[1024,384]{0,1:T(8,128)(2,1)} %copy-done.2) | copy-start | bytes 2359300
  144.4 1.1 copy-start.1
  165.7 66.7 %all-to-all-start.4 = ((bf16[64,24,128]{2,1,0:T(8,128)(2,1)}), bf16[64,24,128]{2,1,0:T(8,128)(2,1)S(1)}, u32[]{:S(2)}, u32[]{:S(2)}) async-start(bf16[64,24,128]{2,1,0:T(8,128)(2,1)} %bitcast.51), calls=%async_computation.4 | async-start | bytes 786432 | tf_op jit(solution)/shard_map/all_to_all | solution.py:20
  179.7 53.3 %copy-start.7 = (s32[48,8]{0,1:T(8,128)S(1)}, s32[48,8]{0,1:T(8,128)}, u32[]{:S(2)}) copy-start(s32[48,8]{0,1:T(8,128)} %param.8) | copy-start | bytes 4612
  234.4 10.0 %all-to-all-start.5 = ((f32[16,8,128]{2,1,0:T(8,128)}), f32[16,8,128]{2,1,0:T(8,128)S(1)}, u32[]{:S(2)}, u32[]{:S(2)}) async-start(f32[16,8,128]{2,1,0:T(8,128)} %broadcast_in_dim.170), calls=%async_computation.5 | async-start | bytes 131072 | tf_op jit(solution)/shard_map/all_to_all | solution.py:20

commit v7 on v5

--- a/solution.py
+++ b/solution.py
@@ -33,6 +33,11 @@
     before = jnp.arange(rows)[:, None] < jnp.arange(rows)[None, :]
     rank = jnp.dot(member.astype(BF16), before.astype(BF16), preferred_element_type=F32)
     return names, jnp.where(member, rank, -1000.0), gate
+
+
+def split2(v):
+    hi = v.astype(BF16)
+    return hi, (v - hi.astype(F32)).astype(BF16)
 
 
 def times(a, b):
@@ -90,14 +95,22 @@
     )
     weights = [take(weights, me + SIDE - i) for i in range(SIDE)]
     held = [jnp.concatenate([w[i * feats : (i + 1) * feats] for w in weights], axis=0) for i in range(3)]
-    recv, *held = lax.optimization_barrier((recv, *held))
 
     q = jnp.arange(quarter * pieces, dtype=jnp.int32)
     q_place = (q % pieces) // CAP * block + q // pieces * CAP + q % CAP
     order = (q_place[None, :] == q[:, None]).astype(BF16)
+    longer = pieces + 2
+    p = jnp.arange(quarter * longer, dtype=jnp.int32)
+    p_row = p % longer
+    p_place = jnp.where(
+        p_row < pieces, p_row // CAP * block + p // longer * CAP + p_row % CAP, p_row * quarter + p // longer
+    )
+    back_order = (p_place[:, None] == p[None, :]).astype(BF16)
+    first_lanes = [(jnp.arange(LANES)[None, :] == i).astype(BF16) for i in range(2)]
     recv = recv.reshape(SIDE, quarter * pieces, LANES)
     recv = lax.dot_general(order, recv, (((1,), (1,)), ((), ())), preferred_element_type=BF16)
     recv = recv.reshape(2 * halves, block, SIDE, LANES).transpose(2, 1, 0, 3).reshape(slots, 2 * feats)
+    recv, back_order, first_lanes, held = lax.optimization_barrier((recv, back_order, first_lanes, held))
     recv = exchange(jnp.broadcast_to(recv[None], (SIDE, slots, 2 * feats)), "x")
     tok = jnp.concatenate([recv[i, :, :feats] for i in range(SIDE)], axis=1)
     grad = jnp.concatenate([recv[i, :, feats:] for i in range(SIDE)], axis=1)
@@ -112,41 +125,53 @@
     act = (silu * up_pre).astype(BF16)
     grad_gate = (grad_hidden * up_pre * (logistic * (1.0 + gate_pre * (1.0 - logistic)))).astype(BF16)
     grad_up = (grad_hidden * silu).astype(BF16)
-    every = lax.all_gather(jnp.concatenate([act, grad_gate, grad_up], axis=1), "y", axis=0, tiled=True)
+    dots = jnp.sum(act.astype(F32) * grad_hidden, axis=1, keepdims=True)
+    dots = sum(v * lane for v, lane in zip(split2(dots), first_lanes))
+    every = lax.all_gather(jnp.concatenate([act, grad_gate, grad_up, dots], axis=1), "y", axis=0, tiled=True)
 
     act, grad_gate, grad_up = (every[:, i * share : (i + 1) * share] for i in range(3))
     expert_out = times_t(act, held[2]).astype(BF16)
     grad_pick = (times_t(grad_gate, held[0]) + times_t(grad_up, held[1])).astype(BF16)
+    dots = every[:, 3 * share].astype(F32) + every[:, 3 * share + 1].astype(F32)
+    dots = jnp.pad(jnp.stack(split2(dots)), ((0, 6), (0, 2 * feats - slots)))
     back = jnp.stack(
         [
-            jnp.concatenate([v[:, i * feats : (i + 1) * feats] for v in (expert_out, grad_pick)], axis=1)
+            jnp.concatenate(
+                [
+                    jnp.concatenate([v[:, i * feats : (i + 1) * feats] for v in (expert_out, grad_pick)], axis=1),
+                    dots,
+                ],
+                axis=0,
+            )
             for i in range(SIDE)
         ]
     )
-    back = jnp.sum(exchange(back, "x").astype(F32), axis=0).astype(BF16)
-    back = back.reshape(SIDE, block, 2 * halves, LANES).transpose(2, 1, 0, 3)
-    back = back.reshape(quarter * pieces, SIDE, LANES)
-    back = lax.dot_general(order, back, (((0,), (0,)), ((), ())), preferred_element_type=BF16)
-    back = back.transpose(1, 0, 2)
+    back = jnp.sum(exchange(back, "x").astype(F32), axis=0)
+    dots = (back[slots, :slots] + back[slots + 1, :slots]).reshape(experts, CAP)
+    dots = jnp.pad(dots, ((0, 0), (0, LANES - CAP))).reshape(SIDE, quarter, LANES)
+    back = back[:slots].astype(BF16).reshape(SIDE, block, 2 * halves, LANES).transpose(0, 2, 1, 3)
+    back = jnp.concatenate([back.reshape(SIDE, quarter * pieces, LANES), *split2(dots)], axis=1)
+
+    back = lax.dot_general(back_order, back, (((1,), (1,)), ((), ())), preferred_element_type=BF16)
+    back = back.transpose(1, 0, 2).reshape(experts, longer // 2, 2, LANES)
     back, rank, gate = lax.optimization_barrier((back, rank, gate))
-    back = exchange(back.reshape(experts, pieces, LANES), "dp")
-
-    cot_rows = select(rows_of(rank, range(halves)), source[halves * rows :]).astype(BF16)
+    back = exchange(back, "dp").reshape(experts * longer, LANES)
+
     kinds = [g for g in split3(gate)] + [jnp.ones_like(gate)]
     value = jnp.concatenate([g for g in kinds for _ in range(halves)], axis=1)[:, None, :]
     mix = rows_of(rank, [i // 3 * halves + h for i in range(4) for h in range(halves)])
-    mix = jnp.where(mix == j_row, value, 0.0).astype(BF16).reshape(experts * pieces, -1)
-    back, cot_rows, mix = lax.optimization_barrier((back, cot_rows, mix))
-
-    dots = jnp.sum(cot_rows.astype(F32) * back.astype(F32), axis=2)
-    dots = sum(dots[:, h * CAP : (h + 1) * CAP] for h in range(halves))
+    all_rows = jnp.arange(longer, dtype=jnp.int32).astype(F32)[None, :, None]
+    mix = jnp.where(mix == all_rows, value, 0.0).astype(BF16).reshape(experts * longer, -1)
+    place = jnp.arange(experts * longer, dtype=jnp.int32)[None, :]
+    last = (place // longer == jnp.arange(experts)[:, None]) & (place % longer >= pieces)
+    back, mix, last = lax.optimization_barrier((back, mix, last.astype(BF16)))
+
+    dots = times(last, back)
     dots = sum(jnp.where(rank == i, dots[:, i : i + 1], 0.0) for i in range(CAP))
-    local = jnp.sum(jnp.where(names, dots[None], 0.0), axis=1)
-    back, local = lax.optimization_barrier((back, local))
-    grad_gates = jnp.sum(exchange(jnp.broadcast_to(local, (SIDE * SIDE, *local.shape)), ("y", "x")), axis=0).T
+    grad_gates = (jnp.sum(jnp.where(names, dots[None], 0.0), axis=1) / gates.T).T
 
     out = lax.dot_general(
-        mix, back.reshape(experts * pieces, LANES), (((0,), (0,)), ((), ())), preferred_element_type=F32
+        mix, back, (((0,), (0,)), ((), ())), preferred_element_type=F32
     ).reshape(4, halves, rows, LANES)
     mixed = out[0] + out[1] + out[2]
     mixed = jnp.concatenate([mixed[h] for h in range(halves)], axis=1).astype(BF16)

time: 247 us -> 244 us (0.988)
  waiting for transfers between devices: 95.5 us -> 83.8 us
  local copies, waits for them, and re-layouts: 8.1 us -> 13.9 us
  starting transfers between devices: 57.9 us -> 53.2 us
  other arithmetic: 7.57 us -> 10.3 us
    all_to_all x3 -> x2, waiting for transfers between devices: 73.4 us -> 62.6 us  [exchange(): return lax.all_to_all(v, axes, split_axis=0, concat_axis=0, tiled=True)]
    broadcast_in_dim x1 -> x2, local copies, waits for them, and re-layouts: 0.01 us -> 4.74 us  [shards(): jnp.where(mix == all_rows, value, 0.0).astype(BF16)]
    all_to_all x3 -> x2, starting transfers between devices: 47.4 us -> 42.7 us  [exchange(): return lax.all_to_all(v, axes, split_axis=0, concat_axis=0, tiled=True)]
    convert_element_type x2 -> x9, other arithmetic: 0.38 us -> 3.91 us  [the longest x1 2.73 us: shards(): jnp.where(mix == all_rows, value, 0.0).astype(BF16)]
  transfers between devices with their start and end apart: 6 -> 5, of which waited for: 6 -> 5; matrix products, arithmetic and copies ran while one was open for 2% -> 6% of each run, Pallas kernels for 0% -> 0%
where the time goes in v7:
time: 244 us; the launch traced here: 243 us
  waiting for transfers between devices  83.8 us (34%)
  blocking collectives  69.5 us (28%)
  starting transfers between devices  53.2 us (22%)
  local copies, waits for them, and re-layouts  13.9 us (6%)
  matrix products  10.6 us (4%)
  other arithmetic  10.3 us (4%)
    all_to_all x2, waiting for transfers between devices, exchange(): return lax.all_to_all(v, axes, split_axis=0, concat_axis=0, tiled=True)  62.6 us
    all_to_all x3, blocking collectives, exchange(): return lax.all_to_all(v, axes, split_axis=0, concat_axis=0, tiled=True)  57.1 us
    all_to_all x2, starting transfers between devices, exchange(): return lax.all_to_all(v, axes, split_axis=0, concat_axis=0, tiled=True)  42.7 us
    ppermute x3, waiting for transfers between devices, shards(): lax.ppermute(take(weights, me + i), 'x', [(d, (d + i) % SIDE) for d in ra...  21.1 us
    all_gather x1, blocking collectives, shards(): lax.all_gather(jnp.concatenate([act, grad_gate, grad_up, dots], axis=1),...  12.4 us
    ppermute x3, starting transfers between devices, shards(): lax.ppermute(take(weights, me + i), 'x', [(d, (d + i) % SIDE) for d in ra...  10.5 us
  transfers between devices with their start and end apart: 5, of which 5 were waited for; matrix products, arithmetic and copies ran while one was open for 6% of the time, Pallas kernels for 0%

profile of v7, /device:TPU:1, one launch (start us, length us, event | category | flops | bytes accessed | tf_op | source)
XLA Modules:
  0.0 242.7 jit_solution(869782435238808377)
XLA Ops:
  0.7 0.9 fusion.39
  1.9 0.9 select_reduce_fusion.2
  3.1 0.8 fusion.100
  3.8 1.2 fusion.5
  5.1 30.6 %all-to-all-start = ((bf16[64,24,128]{2,1,0:T(8,128)(2,1)}), bf16[64,24,128]{2,1,0:T(8,128)(2,1)}, u32[]{:S(2)}, u32[]{:S(2)}) async-start(bf16[64,24,128]{2,1,0:T(8,128)(2,1)} %fusion.5), calls=%async_computation | async-start | bytes 786432 | tf_op jit(solution)/shard_map/all_to_all | solution.py:20
  37.5 1.2 constant_dynamic-slice_fusion
  38.6 3.1 %collective-permute-start = (bf16[768,384]{0,1:T(8,128)(2,1)}, bf16[768,384]{0,1:T(8,128)(2,1)S(1)}, u32[]{:S(2)}, u32[]{:S(2)}) collective-permute-start(bf16[768,384]{0,1:T(8,128)(2,1)} %get-tuple-element.54), channel_id=1, source_target_pairs={{0,1},{1,2},{2,3},{3,0},{4,5},{5,6},{6,7},{7,4},{8,9},{9,10},{10,1... | collective-permute-start | bytes 1769480 | tf_op jit(solution)/shard_map/ppermute | solution.py:90
  41.7 4.4 %collective-permute-start.1 = (bf16[768,384]{0,1:T(8,128)(2,1)}, bf16[768,384]{0,1:T(8,128)(2,1)S(1)}, u32[]{:S(2)}, u32[]{:S(2)}) collective-permute-start(bf16[768,384]{0,1:T(8,128)(2,1)} %get-tuple-element.53), channel_id=1, source_target_pairs={{0,2},{1,3},{2,0},{3,1},{4,6},{5,7},{6,4},{7,5},{8,10},{9,11},{10,... | collective-permute-start | bytes 1769480 | tf_op jit(solution)/shard_map/ppermute | solution.py:90
  46.1 3.1 %collective-permute-start.2 = (bf16[768,384]{0,1:T(8,128)(2,1)S(1)}, bf16[768,384]{0,1:T(8,128)(2,1)S(1)}, u32[]{:S(2)}, u32[]{:S(2)}) collective-permute-start(bf16[768,384]{0,1:T(8,128)(2,1)S(1)} %get-tuple-element.52), channel_id=1, source_target_pairs={{0,3},{1,0},{2,1},{3,2},{4,7},{5,4},{6,5},{7,6},{8,11},{9,8},{10,9... | collective-permute-start | bytes 1769480 | tf_op jit(solution)/shard_map/ppermute | solution.py:90
  49.3 0.9 fusion.8
  50.2 6.2 %collective-permute-done = bf16[768,384]{0,1:T(8,128)(2,1)S(1)} collective-permute-done((bf16[768,384]{0,1:T(8,128)(2,1)}, bf16[768,384]{0,1:T(8,128)(2,1)S(1)}, u32[]{:S(2)}, u32[]{:S(2)}) %collective-permute-start) | collective-permute-done | bytes 589856 | tf_op jit(solution)/shard_map/ppermute | solution.py:90
  56.4 13.6 %collective-permute-done.1 = bf16[768,384]{0,1:T(8,128)(2,1)S(1)} collective-permute-done((bf16[768,384]{0,1:T(8,128)(2,1)}, bf16[768,384]{0,1:T(8,128)(2,1)S(1)}, u32[]{:S(2)}, u32[]{:S(2)}) %collective-permute-start.1) | collective-permute-done | bytes 589856 | tf_op jit(solution)/shard_map/ppermute | solution.py:90
  70.0 1.3 collective-permute-done.2
  72.2 16.8 %all-to-all-done = bf16[64,24,128]{2,1,0:T(8,128)(2,1)} async-done(((bf16[64,24,128]{2,1,0:T(8,128)(2,1)}), bf16[64,24,128]{2,1,0:T(8,128)(2,1)}, u32[]{:S(2)}, u32[]{:S(2)}) %all-to-all-start) | async-done | bytes 393248 | tf_op jit(solution)/shard_map/all_to_all | solution.py:20
  88.9 1.4 convolution_bitcast_fusion
  90.9 23.4 %all_to_all.25 = bf16[4,384,512]{2,1,0:T(8,128)(2,1)S(1)} all-to-all(bf16[4,384,512]{2,1,0:T(8,128)(2,1)S(1)} %broadcast_in_dim.154), channel_id=1, replica_groups=mesh['dp'=64,'y'=4,'x'=4] {'x'}, dimensions={0} | all-to-all | bytes 3145728 | tf_op jit(solution)/shard_map/all_to_all | solution.py:20
  116.2 0.9 copy.39
  117.1 14.9 %all_to_all.26 = bf16[4,96,1152]{2,1,0:T(8,128)(2,1)S(1)} all-to-all(bf16[4,96,1152]{2,1,0:T(8,128)(2,1)S(1)} %bitcast.122), channel_id=1, replica_groups=mesh['dp'=64,'y'=4,'x'=4] {'y'}, dimensions={0} | all-to-all | bytes 1769472 | tf_op jit(solution)/shard_map/all_to_all | solution.py:20
  132.5 12.4 %all_gather.3 = bf16[384,1280]{1,0:T(8,128)(2,1)S(1)} all-gather(bf16[96,1280]{1,0:T(8,128)(2,1)S(1)} %pad_maximum_fusion.13), channel_id=1, replica_groups=mesh['dp'=64,'y'=4,'x'=4] {'y'}, dimensions={0}, use_global_device_ids=true | all-gather | bytes 1228800 | tf_op jit(solution)/shard_map/all_gather | solution.py:130
  147.7 18.8 %all_to_all.27 = bf16[4,392,512]{2,1,0:T(8,128)(2,1)S(1)} all-to-all(bf16[4,392,512]{2,1,0:T(8,128)(2,1)S(1)} %pad_maximum_fusion.3), channel_id=1, replica_groups=mesh['dp'=64,'y'=4,'x'=4] {'x'}, dimensions={0} | all-to-all | bytes 3211264 | tf_op jit(solution)/shard_map/all_to_all | solution.py:20
  167.7 1.2 fusion.20
  168.8 12.1 %all-to-all-start.4 = ((bf16[64,13,2,128]{3,2,1,0:T(2,128)(2,1)}), bf16[64,13,2,128]{3,2,1,0:T(2,128)(2,1)}, u32[]{:S(2)}, u32[]{:S(2)}) async-start(bf16[64,13,2,128]{3,2,1,0:T(2,128)(2,1)} %bitcast.54), calls=%async_computation.4 | async-start | bytes 851968 | tf_op jit(solution)/shard_map/all_to_all | solution.py:20
  181.7 1.6 eq.217
  183.8 1.3 broadcast_in_dim.155
  185.1 3.5 %broadcast_in_dim.156 = bf16[1664,384]{1,0:T(8,128)(2,1)} reshape(bf16[64,26,384]{2,1,0:T(8,128)(2,1)} %broadcast_in_dim.155) | data formatting | bytes 2555904 | tf_op jit(solution)/shard_map/jit(_where)/broadcast_in_dim | solution.py:164
  188.5 2.7 %select_convert_fusion = bf16[1664,384]{1,0:T(8,128)(2,1)} fusion(bf16[1664,384]{1,0:T(8,128)(2,1)} %broadcast_in_dim.156, f32[1664,384]{1,0:T(8,128)S(1)} %copy-done, f32[1664]{0:T(1024)S(1)} %eq.219), kind=kLoop, calls=%fused_computation.1 | loop fusion | flops 1277952 | bytes 5118464 | tf_op jit(solution)/shard_map/convert_element_type | solution.py:164
  191.3 45.9 %all-to-all-done.4 = bf16[64,13,2,128]{3,2,1,0:T(2,128)(2,1)} async-done(((bf16[64,13,2,128]{3,2,1,0:T(2,128)(2,1)}), bf16[64,13,2,128]{3,2,1,0:T(2,128)(2,1)}, u32[]{:S(2)}, u32[]{:S(2)}) %all-to-all-start.4) | async-done | bytes 426016 | tf_op jit(solution)/shard_map/all_to_all | solution.py:20
  237.1 1.2 fusion.104
  238.9 0.6 bitcast_divide_fusion
  239.5 1.9 fusion.103
  241.5 0.6 pad_maximum_fusion.18
  242.1 0.6 pad_maximum_fusion.17
  (109 shorter events, 11.5 us)
Async XLA Ops:
  0.6 35.1 %copy-start.8 = (bf16[1,256,1536]{2,1,0:T(8,128)(2,1)S(1)}, bf16[1,256,1536]{2,1,0:T(8,128)(2,1)}, u32[]{:S(2)}) copy-start(bf16[1,256,1536]{2,1,0:T(8,128)(2,1)} %param.10) | copy-start | bytes 2359300
  3.8 32.1 %copy-start.9 = (bf16[1,256,1536]{2,1,0:T(8,128)(2,1)S(1)}, bf16[1,256,1536]{2,1,0:T(8,128)(2,1)}, u32[]{:S(2)}) copy-start(bf16[1,256,1536]{2,1,0:T(8,128)(2,1)} %param.11) | copy-start | bytes 2359300
  5.1 83.9 %all-to-all-start = ((bf16[64,24,128]{2,1,0:T(8,128)(2,1)}), bf16[64,24,128]{2,1,0:T(8,128)(2,1)}, u32[]{:S(2)}, u32[]{:S(2)}) async-start(bf16[64,24,128]{2,1,0:T(8,128)(2,1)} %fusion.5), calls=%async_computation | async-start | bytes 786432 | tf_op jit(solution)/shard_map/all_to_all | solution.py:20
  35.7 1.1 copy-start.7
  38.6 17.8 %collective-permute-start = (bf16[768,384]{0,1:T(8,128)(2,1)}, bf16[768,384]{0,1:T(8,128)(2,1)S(1)}, u32[]{:S(2)}, u32[]{:S(2)}) collective-permute-start(bf16[768,384]{0,1:T(8,128)(2,1)} %get-tuple-element.54), channel_id=1, source_target_pairs={{0,1},{1,2},{2,3},{3,0},{4,5},{5,6},{6,7},{7,4},{8,9},{9,10},{10,1... | collective-permute-start | bytes 1769480 | tf_op jit(solution)/shard_map/ppermute | solution.py:90
  41.7 28.3 %collective-permute-start.1 = (bf16[768,384]{0,1:T(8,128)(2,1)}, bf16[768,384]{0,1:T(8,128)(2,1)S(1)}, u32[]{:S(2)}, u32[]{:S(2)}) collective-permute-start(bf16[768,384]{0,1:T(8,128)(2,1)} %get-tuple-element.53), channel_id=1, source_target_pairs={{0,2},{1,3},{2,0},{3,1},{4,6},{5,7},{6,4},{7,5},{8,10},{9,11},{10,... | collective-permute-start | bytes 1769480 | tf_op jit(solution)/shard_map/ppermute | solution.py:90
  46.1 25.2 %collective-permute-start.2 = (bf16[768,384]{0,1:T(8,128)(2,1)S(1)}, bf16[768,384]{0,1:T(8,128)(2,1)S(1)}, u32[]{:S(2)}, u32[]{:S(2)}) collective-permute-start(bf16[768,384]{0,1:T(8,128)(2,1)S(1)} %get-tuple-element.52), channel_id=1, source_target_pairs={{0,3},{1,0},{2,1},{3,2},{4,7},{5,4},{6,5},{7,6},{8,11},{9,8},{10,9... | collective-permute-start | bytes 1769480 | tf_op jit(solution)/shard_map/ppermute | solution.py:90
  71.9 43.6 %copy-start.1 = (bf16[1024,384]{0,1:T(8,128)(2,1)}, bf16[1024,384]{0,1:T(8,128)(2,1)S(1)}, u32[]{:S(2)}) copy-start(bf16[1024,384]{0,1:T(8,128)(2,1)S(1)} %pad_maximum_fusion.11) | copy-start | bytes 2359300
  72.1 42.2 %copy-start.5 = (bf16[1024,384]{0,1:T(8,128)(2,1)}, bf16[1024,384]{0,1:T(8,128)(2,1)S(1)}, u32[]{:S(2)}) copy-start(bf16[1024,384]{0,1:T(8,128)(2,1)S(1)} %get-tuple-element.18) | copy-start | bytes 2359300
  72.2 42.8 %copy-start.3 = (bf16[1024,384]{0,1:T(8,128)(2,1)}, bf16[1024,384]{0,1:T(8,128)(2,1)S(1)}, u32[]{:S(2)}) copy-start(bf16[1024,384]{0,1:T(8,128)(2,1)S(1)} %get-tuple-element.19) | copy-start | bytes 2359300
  132.1 12.9 %copy-start.2 = (bf16[1024,384]{0,1:T(8,128)(2,1)S(1)}, bf16[1024,384]{0,1:T(8,128)(2,1)}, u32[]{:S(2)}) copy-start(bf16[1024,384]{0,1:T(8,128)(2,1)} %copy-done.1) | copy-start | bytes 2359300
  132.5 13.0 %copy-start.6 = (bf16[1024,384]{0,1:T(8,128)(2,1)S(1)}, bf16[1024,384]{0,1:T(8,128)(2,1)}, u32[]{:S(2)}) copy-start(bf16[1024,384]{0,1:T(8,128)(2,1)} %copy-done.5) | copy-start | bytes 2359300
  145.5 1.1 copy-start.4
  166.7 1.0 copy-start.10
  168.8 68.3 %all-to-all-start.4 = ((bf16[64,13,2,128]{3,2,1,0:T(2,128)(2,1)}), bf16[64,13,2,128]{3,2,1,0:T(2,128)(2,1)}, u32[]{:S(2)}, u32[]{:S(2)}) async-start(bf16[64,13,2,128]{3,2,1,0:T(2,128)(2,1)} %bitcast.54), calls=%async_computation.4 | async-start | bytes 851968 | tf_op jit(solution)/shard_map/all_to_all | solution.py:20
  185.1 3.5 %copy-start = (f32[1664,384]{1,0:T(8,128)S(1)}, f32[1664,384]{1,0:T(8,128)}, u32[]{:S(2)}) copy-start(f32[1664,384]{1,0:T(8,128)} %eq.217) | copy-start | bytes 7667716
  188.5 50.1 %copy-start.11 = (s32[48,8]{0,1:T(8,128)S(1)}, s32[48,8]{0,1:T(8,128)}, u32[]{:S(2)}) copy-start(s32[48,8]{0,1:T(8,128)} %param.8) | copy-start | bytes 4612
  188.5 50.4 %copy-start.12 = (f32[48,8]{0,1:T(8,128)S(1)}, f32[48,8]{0,1:T(8,128)}, u32[]{:S(2)}) copy-start(f32[48,8]{0,1:T(8,128)} %param.9) | copy-start | bytes 4612

commit v8 on v7

--- a/solution.py
+++ b/solution.py
@@ -106,11 +106,12 @@
         p_row < pieces, p_row // CAP * block + p // longer * CAP + p_row % CAP, p_row * quarter + p // longer
     )
     back_order = (p_place[:, None] == p[None, :]).astype(BF16)
+    place = jnp.arange(experts * longer, dtype=jnp.int32)[:, None]
     first_lanes = [(jnp.arange(LANES)[None, :] == i).astype(BF16) for i in range(2)]
     recv = recv.reshape(SIDE, quarter * pieces, LANES)
     recv = lax.dot_general(order, recv, (((1,), (1,)), ((), ())), preferred_element_type=BF16)
     recv = recv.reshape(2 * halves, block, SIDE, LANES).transpose(2, 1, 0, 3).reshape(slots, 2 * feats)
-    recv, back_order, first_lanes, held = lax.optimization_barrier((recv, back_order, first_lanes, held))
+    recv, back_order, place, first_lanes, held = lax.optimization_barrier((recv, back_order, place, first_lanes, held))
     recv = exchange(jnp.broadcast_to(recv[None], (SIDE, slots, 2 * feats)), "x")
     tok = jnp.concatenate([recv[i, :, :feats] for i in range(SIDE)], axis=1)
     grad = jnp.concatenate([recv[i, :, feats:] for i in range(SIDE)], axis=1)
@@ -154,25 +155,26 @@
 
     back = lax.dot_general(back_order, back, (((1,), (1,)), ((), ())), preferred_element_type=BF16)
     back = back.transpose(1, 0, 2).reshape(experts, longer // 2, 2, LANES)
-    back, rank, gate = lax.optimization_barrier((back, rank, gate))
+    back, rank, gate, place = lax.optimization_barrier((back, rank, gate, place))
     back = exchange(back, "dp").reshape(experts * longer, LANES)
 
     kinds = [g for g in split3(gate)] + [jnp.ones_like(gate)]
-    value = jnp.concatenate([g for g in kinds for _ in range(halves)], axis=1)[:, None, :]
-    mix = rows_of(rank, [i // 3 * halves + h for i in range(4) for h in range(halves)])
-    all_rows = jnp.arange(longer, dtype=jnp.int32).astype(F32)[None, :, None]
-    mix = jnp.where(mix == all_rows, value, 0.0).astype(BF16).reshape(experts * longer, -1)
-    place = jnp.arange(experts * longer, dtype=jnp.int32)[None, :]
-    last = (place // longer == jnp.arange(experts)[:, None]) & (place % longer >= pieces)
-    back, mix, last = lax.optimization_barrier((back, mix, last.astype(BF16)))
-
-    dots = times(last, back)
+    value = jnp.concatenate([g for g in kinds for _ in range(halves)], axis=1).astype(BF16)
+    target = jnp.concatenate([rank + CAP * (i // 3 * halves + h) for i in range(4) for h in range(halves)], axis=1)
+    source_of = place // longer == jnp.arange(experts, dtype=jnp.int32)[None, :]
+    spread = source_of.astype(BF16)
+    mix = times(spread, target.astype(BF16)) == (place % longer).astype(F32)
+    mix = jnp.where(mix, times(spread, value), 0.0).astype(BF16)
+    last = (source_of & (place % longer >= pieces)).astype(BF16)
+    mix = jnp.concatenate([mix, last], axis=1)
+    back, mix = lax.optimization_barrier((back, mix))
+    out = lax.dot_general(mix, back, (((0,), (0,)), ((), ())), preferred_element_type=F32)
+
+    dots = out[4 * halves * rows :]
     dots = sum(jnp.where(rank == i, dots[:, i : i + 1], 0.0) for i in range(CAP))
     grad_gates = (jnp.sum(jnp.where(names, dots[None], 0.0), axis=1) / gates.T).T
 
-    out = lax.dot_general(
-        mix, back, (((0,), (0,)), ((), ())), preferred_element_type=F32
-    ).reshape(4, halves, rows, LANES)
+    out = out[: 4 * halves * rows].reshape(4, halves, rows, LANES)
     mixed = out[0] + out[1] + out[2]
     mixed = jnp.concatenate([mixed[h] for h in range(halves)], axis=1).astype(BF16)
     grad_tokens = jnp.concatenate([out[3, h] for h in range(halves)], axis=1).astype(BF16)

time: 244 us -> 240 us (0.984)
  waiting for transfers between devices: 83.8 us -> 92.8 us
  local copies, waits for them, and re-layouts: 13.9 us -> 6.53 us
  other arithmetic: 10.3 us -> 7.12 us
    all_to_all x2, waiting for transfers between devices: 62.6 us -> 71 us  [exchange(): return lax.all_to_all(v, axes, split_axis=0, concat_axis=0, tiled=True)]
    broadcast_in_dim x2 -> x0, local copies, waits for them, and re-layouts: 4.74 us -> none  [shards(): jnp.where(mix == all_rows, value, 0.0).astype(BF16)]
    convert_element_type x4 -> x2, other arithmetic: 2.81 us -> 0.12 us  [the longest x1 0.07 us: shards(): last = (source_of & (place % longer >= pieces)).astype(BF16)]
  transfers between devices with their start and end apart: 5 -> 5, of which waited for: 5 -> 5; matrix products, arithmetic and copies ran while one was open for 6% -> 2% of each run, Pallas kernels for 0% -> 0%
where the time goes in v8:
time: 240 us
  waiting for transfers between devices  92.8 us (39%)
  blocking collectives  69.5 us (29%)
  starting transfers between devices  53 us (22%)
  matrix products  9.06 us (4%)
  other arithmetic  7.12 us (3%)
  local copies, waits for them, and re-layouts  6.53 us (3%)
    all_to_all x2, waiting for transfers between devices, exchange(): return lax.all_to_all(v, axes, split_axis=0, concat_axis=0, tiled=True)  71 us
    all_to_all x3, blocking collectives, exchange(): return lax.all_to_all(v, axes, split_axis=0, concat_axis=0, tiled=True)  57.1 us
    all_to_all x2, starting transfers between devices, exchange(): return lax.all_to_all(v, axes, split_axis=0, concat_axis=0, tiled=True)  42.5 us
    ppermute x3, waiting for transfers between devices, shards(): lax.ppermute(take(weights, me + i), 'x', [(d, (d + i) % SIDE) for d in ra...  21.9 us
    all_gather x1, blocking collectives, shards(): lax.all_gather(jnp.concatenate([act, grad_gate, grad_up, dots], axis=1),...  12.4 us
    ppermute x3, starting transfers between devices, shards(): lax.ppermute(take(weights, me + i), 'x', [(d, (d + i) % SIDE) for d in ra...  10.5 us
  transfers between devices with their start and end apart: 5, of which 5 were waited for; matrix products, arithmetic and copies ran while one was open for 2% of the time, Pallas kernels for 0%

profile of v8, /device:TPU:1, one launch (start us, length us, event | category | flops | bytes accessed | tf_op | source)
XLA Modules:
  0.0 239.5 jit_solution(16476843746818979119)
XLA Ops:
  0.7 0.9 fusion.42
  1.9 0.9 select_reduce_fusion.2
  3.1 0.8 fusion.95
  3.8 1.2 fusion.6
  5.1 30.6 %all-to-all-start = ((bf16[64,24,128]{2,1,0:T(8,128)(2,1)}), bf16[64,24,128]{2,1,0:T(8,128)(2,1)}, u32[]{:S(2)}, u32[]{:S(2)}) async-start(bf16[64,24,128]{2,1,0:T(8,128)(2,1)} %fusion.6), calls=%async_computation | async-start | bytes 786432 | tf_op jit(solution)/shard_map/all_to_all | solution.py:20
  37.5 1.2 constant_dynamic-slice_fusion
  38.6 3.1 %collective-permute-start = (bf16[768,384]{0,1:T(8,128)(2,1)}, bf16[768,384]{0,1:T(8,128)(2,1)S(1)}, u32[]{:S(2)}, u32[]{:S(2)}) collective-permute-start(bf16[768,384]{0,1:T(8,128)(2,1)} %get-tuple-element.58), channel_id=1, source_target_pairs={{0,1},{1,2},{2,3},{3,0},{4,5},{5,6},{6,7},{7,4},{8,9},{9,10},{10,1... | collective-permute-start | bytes 1769480 | tf_op jit(solution)/shard_map/ppermute | solution.py:90
  41.8 4.4 %collective-permute-start.1 = (bf16[768,384]{0,1:T(8,128)(2,1)}, bf16[768,384]{0,1:T(8,128)(2,1)S(1)}, u32[]{:S(2)}, u32[]{:S(2)}) collective-permute-start(bf16[768,384]{0,1:T(8,128)(2,1)} %get-tuple-element.57), channel_id=1, source_target_pairs={{0,2},{1,3},{2,0},{3,1},{4,6},{5,7},{6,4},{7,5},{8,10},{9,11},{10,... | collective-permute-start | bytes 1769480 | tf_op jit(solution)/shard_map/ppermute | solution.py:90
  46.1 3.1 %collective-permute-start.2 = (bf16[768,384]{0,1:T(8,128)(2,1)S(1)}, bf16[768,384]{0,1:T(8,128)(2,1)S(1)}, u32[]{:S(2)}, u32[]{:S(2)}) collective-permute-start(bf16[768,384]{0,1:T(8,128)(2,1)S(1)} %get-tuple-element.56), channel_id=1, source_target_pairs={{0,3},{1,0},{2,1},{3,2},{4,7},{5,4},{6,5},{7,6},{8,11},{9,8},{10,9... | collective-permute-start | bytes 1769480 | tf_op jit(solution)/shard_map/ppermute | solution.py:90
  49.4 7.0 %collective-permute-done = bf16[768,384]{0,1:T(8,128)(2,1)S(1)} collective-permute-done((bf16[768,384]{0,1:T(8,128)(2,1)}, bf16[768,384]{0,1:T(8,128)(2,1)S(1)}, u32[]{:S(2)}, u32[]{:S(2)}) %collective-permute-start) | collective-permute-done | bytes 589856 | tf_op jit(solution)/shard_map/ppermute | solution.py:90
  56.4 13.6 %collective-permute-done.1 = bf16[768,384]{0,1:T(8,128)(2,1)S(1)} collective-permute-done((bf16[768,384]{0,1:T(8,128)(2,1)}, bf16[768,384]{0,1:T(8,128)(2,1)S(1)}, u32[]{:S(2)}, u32[]{:S(2)}) %collective-permute-start.1) | collective-permute-done | bytes 589856 | tf_op jit(solution)/shard_map/ppermute | solution.py:90
  70.1 1.3 collective-permute-done.2
  72.2 16.7 %all-to-all-done = bf16[64,24,128]{2,1,0:T(8,128)(2,1)} async-done(((bf16[64,24,128]{2,1,0:T(8,128)(2,1)}), bf16[64,24,128]{2,1,0:T(8,128)(2,1)}, u32[]{:S(2)}, u32[]{:S(2)}) %all-to-all-start) | async-done | bytes 393248 | tf_op jit(solution)/shard_map/all_to_all | solution.py:20
  89.0 1.4 convolution_bitcast_fusion
  90.9 23.4 %all_to_all.25 = bf16[4,384,512]{2,1,0:T(8,128)(2,1)S(1)} all-to-all(bf16[4,384,512]{2,1,0:T(8,128)(2,1)S(1)} %broadcast_in_dim.141), channel_id=1, replica_groups=mesh['dp'=64,'y'=4,'x'=4] {'x'}, dimensions={0} | all-to-all | bytes 3145728 | tf_op jit(solution)/shard_map/all_to_all | solution.py:20
  114.4 0.6 convolution_convert_fusion.3
  115.0 0.6 convolution_convert_fusion.2
  115.6 0.6 convolution_convert_fusion.1
  116.3 0.9 copy.36
  117.1 15.0 %all_to_all.26 = bf16[4,96,1152]{2,1,0:T(8,128)(2,1)S(1)} all-to-all(bf16[4,96,1152]{2,1,0:T(8,128)(2,1)S(1)} %bitcast.122), channel_id=1, replica_groups=mesh['dp'=64,'y'=4,'x'=4] {'y'}, dimensions={0} | all-to-all | bytes 1769472 | tf_op jit(solution)/shard_map/all_to_all | solution.py:20
  132.6 12.4 %all_gather.3 = bf16[384,1280]{1,0:T(8,128)(2,1)S(1)} all-gather(bf16[96,1280]{1,0:T(8,128)(2,1)S(1)} %pad_maximum_fusion.14), channel_id=1, replica_groups=mesh['dp'=64,'y'=4,'x'=4] {'y'}, dimensions={0}, use_global_device_ids=true | all-gather | bytes 1228800 | tf_op jit(solution)/shard_map/all_gather | solution.py:131
  145.0 0.6 convolution_convert_fusion
  145.6 0.6 fusion.35
  146.7 0.6 add_convert_fusion
  147.7 18.8 %all_to_all.27 = bf16[4,392,512]{2,1,0:T(8,128)(2,1)S(1)} all-to-all(bf16[4,392,512]{2,1,0:T(8,128)(2,1)S(1)} %pad_maximum_fusion.3), channel_id=1, replica_groups=mesh['dp'=64,'y'=4,'x'=4] {'x'}, dimensions={0} | all-to-all | bytes 3211264 | tf_op jit(solution)/shard_map/all_to_all | solution.py:20
  167.2 1.1 fusion.21
  168.4 11.9 %all-to-all-start.4 = ((bf16[64,13,2,128]{3,2,1,0:T(2,128)(2,1)}), bf16[64,13,2,128]{3,2,1,0:T(2,128)(2,1)S(1)}, u32[]{:S(2)}, u32[]{:S(2)}) async-start(bf16[64,13,2,128]{3,2,1,0:T(2,128)(2,1)} %bitcast.54), calls=%async_computation.4 | async-start | bytes 851968 | tf_op jit(solution)/shard_map/all_to_all | solution.py:20
  181.5 0.6 fusion
  182.3 54.2 %all-to-all-done.4 = bf16[64,13,2,128]{3,2,1,0:T(2,128)(2,1)S(1)} async-done(((bf16[64,13,2,128]{3,2,1,0:T(2,128)(2,1)}), bf16[64,13,2,128]{3,2,1,0:T(2,128)(2,1)S(1)}, u32[]{:S(2)}, u32[]{:S(2)}) %all-to-all-start.4) | async-done | bytes 426016 | tf_op jit(solution)/shard_map/all_to_all | solution.py:20
  237.7 0.6 bitcast_divide_fusion
  238.3 0.6 pad_maximum_fusion.19
  238.9 0.6 pad_maximum_fusion.18
  (96 shorter events, 8.5 us)
Async XLA Ops:
  0.6 35.1 %copy-start.5 = (bf16[1,256,1536]{2,1,0:T(8,128)(2,1)S(1)}, bf16[1,256,1536]{2,1,0:T(8,128)(2,1)}, u32[]{:S(2)}) copy-start(bf16[1,256,1536]{2,1,0:T(8,128)(2,1)} %param.10) | copy-start | bytes 2359300
  3.8 32.2 %copy-start.6 = (bf16[1,256,1536]{2,1,0:T(8,128)(2,1)S(1)}, bf16[1,256,1536]{2,1,0:T(8,128)(2,1)}, u32[]{:S(2)}) copy-start(bf16[1,256,1536]{2,1,0:T(8,128)(2,1)} %param.11) | copy-start | bytes 2359300
  5.1 83.9 %all-to-all-start = ((bf16[64,24,128]{2,1,0:T(8,128)(2,1)}), bf16[64,24,128]{2,1,0:T(8,128)(2,1)}, u32[]{:S(2)}, u32[]{:S(2)}) async-start(bf16[64,24,128]{2,1,0:T(8,128)(2,1)} %fusion.6), calls=%async_computation | async-start | bytes 786432 | tf_op jit(solution)/shard_map/all_to_all | solution.py:20
  35.7 1.1 copy-start.4
  38.6 17.8 %collective-permute-start = (bf16[768,384]{0,1:T(8,128)(2,1)}, bf16[768,384]{0,1:T(8,128)(2,1)S(1)}, u32[]{:S(2)}, u32[]{:S(2)}) collective-permute-start(bf16[768,384]{0,1:T(8,128)(2,1)} %get-tuple-element.58), channel_id=1, source_target_pairs={{0,1},{1,2},{2,3},{3,0},{4,5},{5,6},{6,7},{7,4},{8,9},{9,10},{10,1... | collective-permute-start | bytes 1769480 | tf_op jit(solution)/shard_map/ppermute | solution.py:90
  41.8 28.3 %collective-permute-start.1 = (bf16[768,384]{0,1:T(8,128)(2,1)}, bf16[768,384]{0,1:T(8,128)(2,1)S(1)}, u32[]{:S(2)}, u32[]{:S(2)}) collective-permute-start(bf16[768,384]{0,1:T(8,128)(2,1)} %get-tuple-element.57), channel_id=1, source_target_pairs={{0,2},{1,3},{2,0},{3,1},{4,6},{5,7},{6,4},{7,5},{8,10},{9,11},{10,... | collective-permute-start | bytes 1769480 | tf_op jit(solution)/shard_map/ppermute | solution.py:90
  46.1 25.2 %collective-permute-start.2 = (bf16[768,384]{0,1:T(8,128)(2,1)S(1)}, bf16[768,384]{0,1:T(8,128)(2,1)S(1)}, u32[]{:S(2)}, u32[]{:S(2)}) collective-permute-start(bf16[768,384]{0,1:T(8,128)(2,1)S(1)} %get-tuple-element.56), channel_id=1, source_target_pairs={{0,3},{1,0},{2,1},{3,2},{4,7},{5,4},{6,5},{7,6},{8,11},{9,8},{10,9... | collective-permute-start | bytes 1769480 | tf_op jit(solution)/shard_map/ppermute | solution.py:90
  72.2 42.1 %copy-start.2 = (bf16[1024,384]{0,1:T(8,128)(2,1)}, bf16[1024,384]{0,1:T(8,128)(2,1)S(1)}, u32[]{:S(2)}) copy-start(bf16[1024,384]{0,1:T(8,128)(2,1)S(1)} %get-tuple-element.19) | copy-start | bytes 2359300
  72.2 42.7 %copy-start = (bf16[1024,384]{0,1:T(8,128)(2,1)}, bf16[1024,384]{0,1:T(8,128)(2,1)S(1)}, u32[]{:S(2)}) copy-start(bf16[1024,384]{0,1:T(8,128)(2,1)S(1)} %get-tuple-element.20) | copy-start | bytes 2359300
  132.6 13.0 %copy-start.3 = (bf16[1024,384]{0,1:T(8,128)(2,1)S(1)}, bf16[1024,384]{0,1:T(8,128)(2,1)}, u32[]{:S(2)}) copy-start(bf16[1024,384]{0,1:T(8,128)(2,1)} %copy-done.2) | copy-start | bytes 2359300
  145.6 1.1 copy-start.1
  168.4 68.2 %all-to-all-start.4 = ((bf16[64,13,2,128]{3,2,1,0:T(2,128)(2,1)}), bf16[64,13,2,128]{3,2,1,0:T(2,128)(2,1)S(1)}, u32[]{:S(2)}, u32[]{:S(2)}) async-start(bf16[64,13,2,128]{3,2,1,0:T(2,128)(2,1)} %bitcast.54), calls=%async_computation.4 | async-start | bytes 851968 | tf_op jit(solution)/shard_map/all_to_all | solution.py:20
  182.3 55.2 %copy-start.7 = (s32[48,8]{0,1:T(8,128)S(1)}, s32[48,8]{0,1:T(8,128)}, u32[]{:S(2)}) copy-start(s32[48,8]{0,1:T(8,128)} %param.8) | copy-start | bytes 4612
  182.3 55.4 %copy-start.8 = (f32[48,8]{0,1:T(8,128)S(1)}, f32[48,8]{0,1:T(8,128)}, u32[]{:S(2)}) copy-start(f32[48,8]{0,1:T(8,128)} %param.9) | copy-start | bytes 4612

commit v9 on v8

--- a/solution.py
+++ b/solution.py
@@ -85,16 +85,12 @@
     weights = jnp.concatenate([w_gate[0], w_up[0], w_down[0].T], axis=0)
     weights = jnp.stack([weights[:, i * share : (i + 1) * share] for i in range(SIDE)])
     me = lax.axis_index("x")
-    weights = jnp.stack(
-        [
-            lax.ppermute(take(weights, me + i), "x", [(d, (d + i) % SIDE) for d in range(SIDE)])
-            if i
-            else take(weights, me)
-            for i in range(SIDE)
-        ]
-    )
-    weights = [take(weights, me + SIDE - i) for i in range(SIDE)]
-    held = [jnp.concatenate([w[i * feats : (i + 1) * feats] for w in weights], axis=0) for i in range(3)]
+    came = [
+        lax.ppermute(take(weights, me + i), "x", [(d, (d + i) % SIDE) for d in range(SIDE)])
+        if i
+        else take(weights, me)
+        for i in range(SIDE)
+    ]
 
     q = jnp.arange(quarter * pieces, dtype=jnp.int32)
     q_place = (q % pieces) // CAP * block + q // pieces * CAP + q % CAP
@@ -111,6 +107,10 @@
     recv = recv.reshape(SIDE, quarter * pieces, LANES)
     recv = lax.dot_general(order, recv, (((1,), (1,)), ((), ())), preferred_element_type=BF16)
     recv = recv.reshape(2 * halves, block, SIDE, LANES).transpose(2, 1, 0, 3).reshape(slots, 2 * feats)
+    recv, *came = lax.optimization_barrier((recv, *came))
+    weights = jnp.stack(came)
+    weights = [take(weights, me + SIDE - i) for i in range(SIDE)]
+    held = [jnp.concatenate([w[i * feats : (i + 1) * feats] for w in weights], axis=0) for i in range(3)]
     recv, back_order, place, first_lanes, held = lax.optimization_barrier((recv, back_order, place, first_lanes, held))
     recv = exchange(jnp.broadcast_to(recv[None], (SIDE, slots, 2 * feats)), "x")
     tok = jnp.concatenate([recv[i, :, :feats] for i in range(SIDE)], axis=1)

time: 240 us -> 240 us (level)
    all_to_all x2, waiting for transfers between devices: 71 us -> 93.7 us  [exchange(): return lax.all_to_all(v, axes, split_axis=0, concat_axis=0, tiled=True)]
    ppermute x3, waiting for transfers between devices: 21.9 us -> 0.01 us  [shards(): lax.ppermute(take(weights, me + i), 'x', [(d, (d + i) % SIDE) for d in ra...]
  transfers between devices with their start and end apart: 5 -> 5, of which waited for: 5 -> 2; matrix products, arithmetic and copies ran while one was open for 2% -> 3% of each run, Pallas kernels for 0% -> 0%
where the time goes in v9:
time: 240 us; the launch traced here: 239 us
  waiting for transfers between devices  93.8 us (39%)
  blocking collectives  69.4 us (29%)
  starting transfers between devices  52.2 us (22%)
  matrix products  9.02 us (4%)
  other arithmetic  7.1 us (3%)
  local copies, waits for them, and re-layouts  6.53 us (3%)
    all_to_all x2, waiting for transfers between devices, exchange(): return lax.all_to_all(v, axes, split_axis=0, concat_axis=0, tiled=True)  93.7 us
    all_to_all x3, blocking collectives, exchange(): return lax.all_to_all(v, axes, split_axis=0, concat_axis=0, tiled=True)  57 us
    all_to_all x2, starting transfers between devices, exchange(): return lax.all_to_all(v, axes, split_axis=0, concat_axis=0, tiled=True)  41.6 us
    all_gather x1, blocking collectives, shards(): lax.all_gather(jnp.concatenate([act, grad_gate, grad_up, dots], axis=1),...  12.4 us
    ppermute x3, starting transfers between devices, shards(): lax.ppermute(take(weights, me + i), 'x', [(d, (d + i) % SIDE) for d in ra...  10.5 us
  transfers between devices with their start and end apart: 5, of which 2 were waited for; matrix products, arithmetic and copies ran while one was open for 3% of the time, Pallas kernels for 0%

profile of v9, /device:TPU:1, one launch (start us, length us, event | category | flops | bytes accessed | tf_op | source)
XLA Modules:
  0.0 239.5 jit_solution(11338134691391289646)
XLA Ops:
  0.7 0.9 fusion.42
  1.9 0.9 select_reduce_fusion.2
  3.1 0.8 fusion.95
  3.8 1.2 fusion.6
  5.0 30.6 %all-to-all-start = ((bf16[64,24,128]{2,1,0:T(8,128)(2,1)}), bf16[64,24,128]{2,1,0:T(8,128)(2,1)}, u32[]{:S(2)}, u32[]{:S(2)}) async-start(bf16[64,24,128]{2,1,0:T(8,128)(2,1)} %fusion.6), calls=%async_computation | async-start | bytes 786432 | tf_op jit(solution)/shard_map/all_to_all | solution.py:20
  36.3 0.5 copy-done.4
  37.4 1.2 dynamic-slice_bitcast_fusion
  38.6 3.1 %collective-permute-start = (bf16[768,384]{0,1:T(8,128)(2,1)}, bf16[768,384]{0,1:T(8,128)(2,1)S(1)}, u32[]{:S(2)}, u32[]{:S(2)}) collective-permute-start(bf16[768,384]{0,1:T(8,128)(2,1)} %get-tuple-element.67), channel_id=1, source_target_pairs={{0,1},{1,2},{2,3},{3,0},{4,5},{5,6},{6,7},{7,4},{8,9},{9,10},{10,1... | collective-permute-start | bytes 1769480 | tf_op jit(solution)/shard_map/ppermute | solution.py:89
  41.7 4.4 %collective-permute-start.1 = (bf16[768,384]{0,1:T(8,128)(2,1)}, bf16[768,384]{0,1:T(8,128)(2,1)S(1)}, u32[]{:S(2)}, u32[]{:S(2)}) collective-permute-start(bf16[768,384]{0,1:T(8,128)(2,1)} %get-tuple-element.66), channel_id=1, source_target_pairs={{0,2},{1,3},{2,0},{3,1},{4,6},{5,7},{6,4},{7,5},{8,10},{9,11},{10,... | collective-permute-start | bytes 1769480 | tf_op jit(solution)/shard_map/ppermute | solution.py:89
  46.1 3.1 %collective-permute-start.2 = (bf16[768,384]{0,1:T(8,128)(2,1)S(1)}, bf16[768,384]{0,1:T(8,128)(2,1)S(1)}, u32[]{:S(2)}, u32[]{:S(2)}) collective-permute-start(bf16[768,384]{0,1:T(8,128)(2,1)S(1)} %get-tuple-element.65), channel_id=1, source_target_pairs={{0,3},{1,0},{2,1},{3,2},{4,7},{5,4},{6,5},{7,6},{8,11},{9,8},{10,9... | collective-permute-start | bytes 1769480 | tf_op jit(solution)/shard_map/ppermute | solution.py:89
  49.4 39.5 %all-to-all-done = bf16[64,24,128]{2,1,0:T(8,128)(2,1)} async-done(((bf16[64,24,128]{2,1,0:T(8,128)(2,1)}), bf16[64,24,128]{2,1,0:T(8,128)(2,1)}, u32[]{:S(2)}, u32[]{:S(2)}) %all-to-all-start) | async-done | bytes 393248 | tf_op jit(solution)/shard_map/all_to_all | solution.py:20
  88.9 1.4 convolution_bitcast_fusion
  91.8 23.4 %all_to_all.25 = bf16[4,384,512]{2,1,0:T(8,128)(2,1)S(1)} all-to-all(bf16[4,384,512]{2,1,0:T(8,128)(2,1)S(1)} %broadcast_in_dim.141), channel_id=1, replica_groups=mesh['dp'=64,'y'=4,'x'=4] {'x'}, dimensions={0} | all-to-all | bytes 3145728 | tf_op jit(solution)/shard_map/all_to_all | solution.py:20
  115.3 0.6 convolution_convert_fusion.3
  115.9 0.6 convolution_convert_fusion.2
  116.5 0.6 convolution_convert_fusion.1
  117.2 0.9 copy.36
  118.0 15.0 %all_to_all.26 = bf16[4,96,1152]{2,1,0:T(8,128)(2,1)S(1)} all-to-all(bf16[4,96,1152]{2,1,0:T(8,128)(2,1)S(1)} %bitcast.125), channel_id=1, replica_groups=mesh['dp'=64,'y'=4,'x'=4] {'y'}, dimensions={0} | all-to-all | bytes 1769472 | tf_op jit(solution)/shard_map/all_to_all | solution.py:20
  133.5 12.4 %all_gather.3 = bf16[384,1280]{1,0:T(8,128)(2,1)S(1)} all-gather(bf16[96,1280]{1,0:T(8,128)(2,1)S(1)} %pad_maximum_fusion.14), channel_id=1, replica_groups=mesh['dp'=64,'y'=4,'x'=4] {'y'}, dimensions={0}, use_global_device_ids=true | all-gather | bytes 1228800 | tf_op jit(solution)/shard_map/all_gather | solution.py:131
  145.9 0.6 convolution_convert_fusion
  146.5 0.6 fusion.35
  147.6 0.6 add_convert_fusion
  148.6 18.7 %all_to_all.27 = bf16[4,392,512]{2,1,0:T(8,128)(2,1)S(1)} all-to-all(bf16[4,392,512]{2,1,0:T(8,128)(2,1)S(1)} %pad_maximum_fusion.3), channel_id=1, replica_groups=mesh['dp'=64,'y'=4,'x'=4] {'x'}, dimensions={0} | all-to-all | bytes 3211264 | tf_op jit(solution)/shard_map/all_to_all | solution.py:20
  168.0 1.1 fusion.21
  169.2 11.1 %all-to-all-start.4 = ((bf16[64,13,2,128]{3,2,1,0:T(2,128)(2,1)}), bf16[64,13,2,128]{3,2,1,0:T(2,128)(2,1)S(1)}, u32[]{:S(2)}, u32[]{:S(2)}) async-start(bf16[64,13,2,128]{3,2,1,0:T(2,128)(2,1)} %bitcast.56), calls=%async_computation.4 | async-start | bytes 851968 | tf_op jit(solution)/shard_map/all_to_all | solution.py:20
  181.0 0.5 convolution_compare_fusion
  181.5 0.6 fusion
  182.3 54.2 %all-to-all-done.4 = bf16[64,13,2,128]{3,2,1,0:T(2,128)(2,1)S(1)} async-done(((bf16[64,13,2,128]{3,2,1,0:T(2,128)(2,1)}), bf16[64,13,2,128]{3,2,1,0:T(2,128)(2,1)S(1)}, u32[]{:S(2)}, u32[]{:S(2)}) %all-to-all-start.4) | async-done | bytes 426016 | tf_op jit(solution)/shard_map/all_to_all | solution.py:20
  236.5 0.6 fusion.98
  237.6 0.6 bitcast_divide_fusion
  238.2 0.6 pad_maximum_fusion.19
  238.9 0.6 pad_maximum_fusion.18
  (97 shorter events, 6.9 us)
Async XLA Ops:
  0.6 35.0 %copy-start.5 = (bf16[1,256,1536]{2,1,0:T(8,128)(2,1)S(1)}, bf16[1,256,1536]{2,1,0:T(8,128)(2,1)}, u32[]{:S(2)}) copy-start(bf16[1,256,1536]{2,1,0:T(8,128)(2,1)} %param.10) | copy-start | bytes 2359300
  3.8 32.1 %copy-start.6 = (bf16[1,256,1536]{2,1,0:T(8,128)(2,1)S(1)}, bf16[1,256,1536]{2,1,0:T(8,128)(2,1)}, u32[]{:S(2)}) copy-start(bf16[1,256,1536]{2,1,0:T(8,128)(2,1)} %param.11) | copy-start | bytes 2359300
  5.0 83.9 %all-to-all-start = ((bf16[64,24,128]{2,1,0:T(8,128)(2,1)}), bf16[64,24,128]{2,1,0:T(8,128)(2,1)}, u32[]{:S(2)}, u32[]{:S(2)}) async-start(bf16[64,24,128]{2,1,0:T(8,128)(2,1)} %fusion.6), calls=%async_computation | async-start | bytes 786432 | tf_op jit(solution)/shard_map/all_to_all | solution.py:20
  35.7 1.1 copy-start.4
  38.6 52.1 %collective-permute-start = (bf16[768,384]{0,1:T(8,128)(2,1)}, bf16[768,384]{0,1:T(8,128)(2,1)S(1)}, u32[]{:S(2)}, u32[]{:S(2)}) collective-permute-start(bf16[768,384]{0,1:T(8,128)(2,1)} %get-tuple-element.67), channel_id=1, source_target_pairs={{0,1},{1,2},{2,3},{3,0},{4,5},{5,6},{6,7},{7,4},{8,9},{9,10},{10,1... | collective-permute-start | bytes 1769480 | tf_op jit(solution)/shard_map/ppermute | solution.py:89
  41.7 49.0 %collective-permute-start.1 = (bf16[768,384]{0,1:T(8,128)(2,1)}, bf16[768,384]{0,1:T(8,128)(2,1)S(1)}, u32[]{:S(2)}, u32[]{:S(2)}) collective-permute-start(bf16[768,384]{0,1:T(8,128)(2,1)} %get-tuple-element.66), channel_id=1, source_target_pairs={{0,2},{1,3},{2,0},{3,1},{4,6},{5,7},{6,4},{7,5},{8,10},{9,11},{10,... | collective-permute-start | bytes 1769480 | tf_op jit(solution)/shard_map/ppermute | solution.py:89
  46.1 44.6 %collective-permute-start.2 = (bf16[768,384]{0,1:T(8,128)(2,1)S(1)}, bf16[768,384]{0,1:T(8,128)(2,1)S(1)}, u32[]{:S(2)}, u32[]{:S(2)}) collective-permute-start(bf16[768,384]{0,1:T(8,128)(2,1)S(1)} %get-tuple-element.65), channel_id=1, source_target_pairs={{0,3},{1,0},{2,1},{3,2},{4,7},{5,4},{6,5},{7,6},{8,11},{9,8},{10,9... | collective-permute-start | bytes 1769480 | tf_op jit(solution)/shard_map/ppermute | solution.py:89
  91.5 24.3 %copy-start = (bf16[1024,384]{0,1:T(8,128)(2,1)}, bf16[1024,384]{0,1:T(8,128)(2,1)S(1)}, u32[]{:S(2)}) copy-start(bf16[1024,384]{0,1:T(8,128)(2,1)S(1)} %pad_maximum_fusion.11) | copy-start | bytes 2359300
  91.6 23.6 %copy-start.2 = (bf16[1024,384]{0,1:T(8,128)(2,1)}, bf16[1024,384]{0,1:T(8,128)(2,1)S(1)}, u32[]{:S(2)}) copy-start(bf16[1024,384]{0,1:T(8,128)(2,1)S(1)} %pad_maximum_fusion.10) | copy-start | bytes 2359300
  133.4 13.0 %copy-start.3 = (bf16[1024,384]{0,1:T(8,128)(2,1)S(1)}, bf16[1024,384]{0,1:T(8,128)(2,1)}, u32[]{:S(2)}) copy-start(bf16[1024,384]{0,1:T(8,128)(2,1)} %copy-done.2) | copy-start | bytes 2359300
  146.4 1.1 copy-start.1
  169.2 67.3 %all-to-all-start.4 = ((bf16[64,13,2,128]{3,2,1,0:T(2,128)(2,1)}), bf16[64,13,2,128]{3,2,1,0:T(2,128)(2,1)S(1)}, u32[]{:S(2)}, u32[]{:S(2)}) async-start(bf16[64,13,2,128]{3,2,1,0:T(2,128)(2,1)} %bitcast.56), calls=%async_computation.4 | async-start | bytes 851968 | tf_op jit(solution)/shard_map/all_to_all | solution.py:20
  182.2 55.2 %copy-start.7 = (s32[48,8]{0,1:T(8,128)S(1)}, s32[48,8]{0,1:T(8,128)}, u32[]{:S(2)}) copy-start(s32[48,8]{0,1:T(8,128)} %param.8) | copy-start | bytes 4612
  182.2 55.4 %copy-start.8 = (f32[48,8]{0,1:T(8,128)S(1)}, f32[48,8]{0,1:T(8,128)}, u32[]{:S(2)}) copy-start(f32[48,8]{0,1:T(8,128)} %param.9) | copy-start | bytes 4612

commit v10 on v9

--- a/solution.py
+++ b/solution.py
@@ -111,11 +111,12 @@
     weights = jnp.stack(came)
     weights = [take(weights, me + SIDE - i) for i in range(SIDE)]
     held = [jnp.concatenate([w[i * feats : (i + 1) * feats] for w in weights], axis=0) for i in range(3)]
+    held = [jnp.concatenate(held[:2], axis=1), held[2]]
     recv, back_order, place, first_lanes, held = lax.optimization_barrier((recv, back_order, place, first_lanes, held))
     recv = exchange(jnp.broadcast_to(recv[None], (SIDE, slots, 2 * feats)), "x")
     tok = jnp.concatenate([recv[i, :, :feats] for i in range(SIDE)], axis=1)
     grad = jnp.concatenate([recv[i, :, feats:] for i in range(SIDE)], axis=1)
-    pre = [times(v, w).astype(BF16) for v, w in zip((tok, tok, grad), held)]
+    pre = [times(v, w).astype(BF16) for v, w in zip((tok, grad), held)]
     pre = jnp.concatenate(pre, axis=1)
 
     pre = exchange(pre.reshape(SIDE, slots // SIDE, 3 * share), "y")
@@ -130,9 +131,8 @@
     dots = sum(v * lane for v, lane in zip(split2(dots), first_lanes))
     every = lax.all_gather(jnp.concatenate([act, grad_gate, grad_up, dots], axis=1), "y", axis=0, tiled=True)
 
-    act, grad_gate, grad_up = (every[:, i * share : (i + 1) * share] for i in range(3))
-    expert_out = times_t(act, held[2]).astype(BF16)
-    grad_pick = (times_t(grad_gate, held[0]) + times_t(grad_up, held[1])).astype(BF16)
+    expert_out = times_t(every[:, :share], held[1]).astype(BF16)
+    grad_pick = times_t(every[:, share : 3 * share], held[0]).astype(BF16)
     dots = every[:, 3 * share].astype(F32) + every[:, 3 * share + 1].astype(F32)
     dots = jnp.pad(jnp.stack(split2(dots)), ((0, 6), (0, 2 * feats - slots)))
     back = jnp.stack(

time: 240 us -> 247 us (1.029)
  other arithmetic: 7.1 us -> 16.5 us
    concatenate x0 -> x1, other arithmetic: none -> 9.6 us  [shards(): held = [jnp.concatenate(held[:2], axis=1), held[2]]]
  transfers between devices with their start and end apart: 5 -> 5, of which waited for: 2 -> 2; matrix products, arithmetic and copies ran while one was open for 3% -> 2% of each run, Pallas kernels for 0% -> 0%
where the time goes in v10:
time: 247 us
  waiting for transfers between devices  93.8 us (38%)
  blocking collectives  69.3 us (28%)
  starting transfers between devices  52.2 us (21%)
  other arithmetic  16.5 us (7%)
  matrix products  8.31 us (3%)
  local copies, waits for them, and re-layouts  5.36 us (2%)
    all_to_all x2, waiting for transfers between devices, exchange(): return lax.all_to_all(v, axes, split_axis=0, concat_axis=0, tiled=True)  93.8 us
    all_to_all x3, blocking collectives, exchange(): return lax.all_to_all(v, axes, split_axis=0, concat_axis=0, tiled=True)  57 us
    all_to_all x2, starting transfers between devices, exchange(): return lax.all_to_all(v, axes, split_axis=0, concat_axis=0, tiled=True)  41.6 us
    all_gather x1, blocking collectives, shards(): lax.all_gather(jnp.concatenate([act, grad_gate, grad_up, dots], axis=1),...  12.3 us
    ppermute x3, starting transfers between devices, shards(): lax.ppermute(take(weights, me + i), 'x', [(d, (d + i) % SIDE) for d in ra...  10.5 us
    concatenate x1, other arithmetic, shards(): held = [jnp.concatenate(held[:2], axis=1), held[2]]  9.6 us
  transfers between devices with their start and end apart: 5, of which 2 were waited for; matrix products, arithmetic and copies ran while one was open for 2% of the time, Pallas kernels for 0%

profile of v10, /device:TPU:1, one launch (start us, length us, event | category | flops | bytes accessed | tf_op | source)
XLA Modules:
  0.0 246.8 jit_solution(18383834492227226368)
XLA Ops:
  0.7 0.9 fusion.47
  1.9 0.9 select_reduce_fusion.2
  3.1 0.8 fusion.99
  3.8 1.2 fusion.6
  5.0 30.6 %all-to-all-start = ((bf16[64,24,128]{2,1,0:T(8,128)(2,1)}), bf16[64,24,128]{2,1,0:T(8,128)(2,1)}, u32[]{:S(2)}, u32[]{:S(2)}) async-start(bf16[64,24,128]{2,1,0:T(8,128)(2,1)} %fusion.6), calls=%async_computation | async-start | bytes 786432 | tf_op jit(solution)/shard_map/all_to_all | solution.py:20
  36.3 0.5 copy-done
  37.1 0.3 pad_maximum_fusion.1
  37.4 1.2 dynamic-slice_bitcast_fusion
  38.6 3.1 %collective-permute-start = (bf16[768,384]{0,1:T(8,128)(2,1)}, bf16[768,384]{0,1:T(8,128)(2,1)S(1)}, u32[]{:S(2)}, u32[]{:S(2)}) collective-permute-start(bf16[768,384]{0,1:T(8,128)(2,1)} %get-tuple-element.65), channel_id=1, source_target_pairs={{0,1},{1,2},{2,3},{3,0},{4,5},{5,6},{6,7},{7,4},{8,9},{9,10},{10,1... | collective-permute-start | bytes 1769480 | tf_op jit(solution)/shard_map/ppermute | solution.py:89
  41.7 4.4 %collective-permute-start.1 = (bf16[768,384]{0,1:T(8,128)(2,1)}, bf16[768,384]{0,1:T(8,128)(2,1)S(1)}, u32[]{:S(2)}, u32[]{:S(2)}) collective-permute-start(bf16[768,384]{0,1:T(8,128)(2,1)} %get-tuple-element.64), channel_id=1, source_target_pairs={{0,2},{1,3},{2,0},{3,1},{4,6},{5,7},{6,4},{7,5},{8,10},{9,11},{10,... | collective-permute-start | bytes 1769480 | tf_op jit(solution)/shard_map/ppermute | solution.py:89
  46.1 3.1 %collective-permute-start.2 = (bf16[768,384]{0,1:T(8,128)(2,1)S(1)}, bf16[768,384]{0,1:T(8,128)(2,1)S(1)}, u32[]{:S(2)}, u32[]{:S(2)}) collective-permute-start(bf16[768,384]{0,1:T(8,128)(2,1)S(1)} %get-tuple-element.63), channel_id=1, source_target_pairs={{0,3},{1,0},{2,1},{3,2},{4,7},{5,4},{6,5},{7,6},{8,11},{9,8},{10,9... | collective-permute-start | bytes 1769480 | tf_op jit(solution)/shard_map/ppermute | solution.py:89
  49.4 39.6 %all-to-all-done = bf16[64,24,128]{2,1,0:T(8,128)(2,1)} async-done(((bf16[64,24,128]{2,1,0:T(8,128)(2,1)}), bf16[64,24,128]{2,1,0:T(8,128)(2,1)}, u32[]{:S(2)}, u32[]{:S(2)}) %all-to-all-start) | async-done | bytes 393248 | tf_op jit(solution)/shard_map/all_to_all | solution.py:20
  88.9 1.4 convolution_bitcast_fusion
  90.3 0.3 copy.34
  91.4 9.6 %maximum_maximum_fusion = bf16[1024,768]{0,1:T(8,128)(2,1)S(1)} fusion(bf16[256,384]{0,1:T(8,128)(2,1)S(1)} %get-tuple-element.52, bf16[256,384]{0,1:T(8,128)(2,1)S(1)} %get-tuple-element.53, bf16[256,384]{0,1:T(8,128)(2,1)S(1)} %get-tuple-element.54, bf16[256,384]{0,1:T(8,128)(2,1)S(1)} %get-tuple-element.55, bf16[256,384]{0,1:T(8,128)(2,1)S(1)} %get-tuple-element.56, ...), kind=kLoop, calls=%fused_computation.9 | loop fusion | flops 12582912 | bytes 3145728 | tf_op jit(solution)/shard_map/concatenate | solution.py:114
  101.2 23.3 %all_to_all.25 = bf16[4,384,512]{2,1,0:T(8,128)(2,1)S(1)} all-to-all(bf16[4,384,512]{2,1,0:T(8,128)(2,1)S(1)} %broadcast_in_dim.141), channel_id=1, replica_groups=mesh['dp'=64,'y'=4,'x'=4] {'x'}, dimensions={0} | all-to-all | bytes 3145728 | tf_op jit(solution)/shard_map/all_to_all | solution.py:20
  124.6 0.8 convolution_convert_fusion.2
  125.5 0.6 convolution_convert_fusion.3
  126.1 14.9 %all_to_all.26 = bf16[4,96,1152]{2,1,0:T(8,128)(2,1)S(1)} all-to-all(bf16[4,96,1152]{2,1,0:T(8,128)(2,1)S(1)} %bitcast.123), channel_id=1, replica_groups=mesh['dp'=64,'y'=4,'x'=4] {'y'}, dimensions={0} | all-to-all | bytes 1769472 | tf_op jit(solution)/shard_map/all_to_all | solution.py:20
  141.5 12.3 %all_gather.3 = bf16[384,1280]{1,0:T(8,128)(2,1)S(1)} all-gather(bf16[96,1280]{1,0:T(8,128)(2,1)S(1)} %pad_maximum_fusion.11), channel_id=1, replica_groups=mesh['dp'=64,'y'=4,'x'=4] {'y'}, dimensions={0}, use_global_device_ids=true | all-gather | bytes 1228800 | tf_op jit(solution)/shard_map/all_gather | solution.py:132
  153.8 0.6 convolution_convert_fusion.1
  154.4 0.8 convolution_convert_fusion
  155.9 18.7 %all_to_all.27 = bf16[4,392,512]{2,1,0:T(8,128)(2,1)S(1)} all-to-all(bf16[4,392,512]{2,1,0:T(8,128)(2,1)S(1)} %pad_maximum_fusion.3), channel_id=1, replica_groups=mesh['dp'=64,'y'=4,'x'=4] {'x'}, dimensions={0} | all-to-all | bytes 3211264 | tf_op jit(solution)/shard_map/all_to_all | solution.py:20
  175.3 1.1 fusion.29
  176.4 11.1 %all-to-all-start.4 = ((bf16[64,13,2,128]{3,2,1,0:T(2,128)(2,1)}), bf16[64,13,2,128]{3,2,1,0:T(2,128)(2,1)S(1)}, u32[]{:S(2)}, u32[]{:S(2)}) async-start(bf16[64,13,2,128]{3,2,1,0:T(2,128)(2,1)} %bitcast.56), calls=%async_computation.4 | async-start | bytes 851968 | tf_op jit(solution)/shard_map/all_to_all | solution.py:20
  188.2 0.5 convolution_compare_fusion
  188.8 0.6 fusion
  189.5 54.2 %all-to-all-done.4 = bf16[64,13,2,128]{3,2,1,0:T(2,128)(2,1)S(1)} async-done(((bf16[64,13,2,128]{3,2,1,0:T(2,128)(2,1)}), bf16[64,13,2,128]{3,2,1,0:T(2,128)(2,1)S(1)}, u32[]{:S(2)}, u32[]{:S(2)}) %all-to-all-start.4) | async-done | bytes 426016 | tf_op jit(solution)/shard_map/all_to_all | solution.py:20
  243.8 0.6 fusion.102
  244.9 0.6 bitcast_divide_fusion
  245.5 0.6 pad_maximum_fusion.14
  246.1 0.6 pad_maximum_fusion.13
  (85 shorter events, 5.8 us)
Async XLA Ops:
  0.6 35.1 %copy-start.1 = (bf16[1,256,1536]{2,1,0:T(8,128)(2,1)S(1)}, bf16[1,256,1536]{2,1,0:T(8,128)(2,1)}, u32[]{:S(2)}) copy-start(bf16[1,256,1536]{2,1,0:T(8,128)(2,1)} %param.10) | copy-start | bytes 2359300
  3.8 32.1 %copy-start.2 = (bf16[1,256,1536]{2,1,0:T(8,128)(2,1)S(1)}, bf16[1,256,1536]{2,1,0:T(8,128)(2,1)}, u32[]{:S(2)}) copy-start(bf16[1,256,1536]{2,1,0:T(8,128)(2,1)} %param.11) | copy-start | bytes 2359300
  5.0 83.9 %all-to-all-start = ((bf16[64,24,128]{2,1,0:T(8,128)(2,1)}), bf16[64,24,128]{2,1,0:T(8,128)(2,1)}, u32[]{:S(2)}, u32[]{:S(2)}) async-start(bf16[64,24,128]{2,1,0:T(8,128)(2,1)} %fusion.6), calls=%async_computation | async-start | bytes 786432 | tf_op jit(solution)/shard_map/all_to_all | solution.py:20
  35.6 1.1 copy-start
  38.6 52.1 %collective-permute-start = (bf16[768,384]{0,1:T(8,128)(2,1)}, bf16[768,384]{0,1:T(8,128)(2,1)S(1)}, u32[]{:S(2)}, u32[]{:S(2)}) collective-permute-start(bf16[768,384]{0,1:T(8,128)(2,1)} %get-tuple-element.65), channel_id=1, source_target_pairs={{0,1},{1,2},{2,3},{3,0},{4,5},{5,6},{6,7},{7,4},{8,9},{9,10},{10,1... | collective-permute-start | bytes 1769480 | tf_op jit(solution)/shard_map/ppermute | solution.py:89
  41.7 49.0 %collective-permute-start.1 = (bf16[768,384]{0,1:T(8,128)(2,1)}, bf16[768,384]{0,1:T(8,128)(2,1)S(1)}, u32[]{:S(2)}, u32[]{:S(2)}) collective-permute-start(bf16[768,384]{0,1:T(8,128)(2,1)} %get-tuple-element.64), channel_id=1, source_target_pairs={{0,2},{1,3},{2,0},{3,1},{4,6},{5,7},{6,4},{7,5},{8,10},{9,11},{10,... | collective-permute-start | bytes 1769480 | tf_op jit(solution)/shard_map/ppermute | solution.py:89
  46.1 44.7 %collective-permute-start.2 = (bf16[768,384]{0,1:T(8,128)(2,1)S(1)}, bf16[768,384]{0,1:T(8,128)(2,1)S(1)}, u32[]{:S(2)}, u32[]{:S(2)}) collective-permute-start(bf16[768,384]{0,1:T(8,128)(2,1)S(1)} %get-tuple-element.63), channel_id=1, source_target_pairs={{0,3},{1,0},{2,1},{3,2},{4,7},{5,4},{6,5},{7,6},{8,11},{9,8},{10,9... | collective-permute-start | bytes 1769480 | tf_op jit(solution)/shard_map/ppermute | solution.py:89
  176.4 67.3 %all-to-all-start.4 = ((bf16[64,13,2,128]{3,2,1,0:T(2,128)(2,1)}), bf16[64,13,2,128]{3,2,1,0:T(2,128)(2,1)S(1)}, u32[]{:S(2)}, u32[]{:S(2)}) async-start(bf16[64,13,2,128]{3,2,1,0:T(2,128)(2,1)} %bitcast.56), calls=%async_computation.4 | async-start | bytes 851968 | tf_op jit(solution)/shard_map/all_to_all | solution.py:20
  189.5 55.2 %copy-start.3 = (s32[48,8]{0,1:T(8,128)S(1)}, s32[48,8]{0,1:T(8,128)}, u32[]{:S(2)}) copy-start(s32[48,8]{0,1:T(8,128)} %param.8) | copy-start | bytes 4612
  189.5 55.4 %copy-start.4 = (f32[48,8]{0,1:T(8,128)S(1)}, f32[48,8]{0,1:T(8,128)}, u32[]{:S(2)}) copy-start(f32[48,8]{0,1:T(8,128)} %param.9) | copy-start | bytes 4612
